TPU v7x, 256 devices: a whole 4x4x8 slice. The times are simulated.
256 devices in a mesh: dp: 16 (over x, z_lo, core), row: 4 (over y), col: 4 (over z_hi).
Axes of the slice: x: 4, y: 4, z: 8 (z_hi: 4, z_lo: 2; z = z_hi * 2 + z_lo), core: 2. Of those that a mesh axis runs over, the one named last changes fastest.
Arguments:
- tokens: bfloat16 [256, 12288], P(('dp', 'col'), 'row'), may hold values from -6 to 6
- cotangent: bfloat16 [256, 12288], P(('dp', 'col'), 'row'), may hold values from -1.796875 to 1.796875
- w_in: bfloat16 [12288, 24576], P('row', ('dp', 'col')), may hold values from -0.0546875 to 0.0546875
- w_out: bfloat16 [24576, 12288], P(('dp', 'col'), 'row'), may hold values from -0.0390625 to 0.0390625
Outputs:
- layer_output: bfloat16 [256, 12288], P(('dp', 'col'), 'row')
- input_grad: bfloat16 [256, 12288], P(('dp', 'col'), 'row')
- w_in_grad: bfloat16 [12288, 24576], P('row', ('dp', 'col'))
- w_out_grad: bfloat16 [24576, 12288], P(('dp', 'col'), 'row')
All inputs are finite; a program needn't handle non-finite values.
Results may differ from a plain program's by a relative error of at most 0.017.
Values may be sent and summed in bfloat16 or wider, within the bound.
No kernel may reach another device: no remote copies, remote signals or barrier semaphores. Data moves between devices by JAX's collectives and lax.ppermute only.
A program may use at most 64 MiB of HBM per device.

v0:
```python
import jax
import jax.numpy as jnp
from jax import lax
from jax.sharding import PartitionSpec as P

SQRT_TWO_PI = 0.7978845608028654
CUBIC = 0.044715


def gelu_value(preact):
    inner = SQRT_TWO_PI * (preact + CUBIC * preact * preact * preact)
    return 0.5 * preact * (1.0 + jnp.tanh(inner))


def gelu_slope(preact):
    tangent = jnp.tanh(SQRT_TWO_PI * (preact + CUBIC * preact * preact * preact))
    return 0.5 * (1.0 + tangent) + 0.5 * preact * (1.0 - tangent * tangent) * SQRT_TWO_PI * (
        1.0 + 3.0 * CUBIC * preact * preact
    )


def on_device(tokens, cotangent, w_in, w_out):
    x_whole, grad_whole = (
        lax.all_gather(tokens, ("dp", "col"), axis=0, tiled=True),
        lax.all_gather(cotangent, ("dp", "col"), axis=0, tiled=True),
    )
    inner_part = jnp.dot(x_whole, w_in, preferred_element_type=jnp.float32)
    back_part = lax.dot_general(
        grad_whole, w_out, (((1,), (1,)), ((), ())), preferred_element_type=jnp.float32
    )
    preact, grad_act = (
        lax.psum_scatter(inner_part, "row", scatter_dimension=0, tiled=True),
        lax.psum_scatter(back_part, "row", scatter_dimension=0, tiled=True),
    )
    act_share = gelu_value(preact).astype(jnp.bfloat16)
    grad_share = (grad_act * gelu_slope(preact)).astype(jnp.bfloat16)
    activated, grad_pre = (
        lax.all_gather(act_share, "row", axis=0, tiled=True),
        lax.all_gather(grad_share, "row", axis=0, tiled=True),
    )
    w_in_grad = lax.dot_general(
        x_whole, grad_pre, (((0,), (0,)), ((), ())), preferred_element_type=jnp.float32
    ).astype(jnp.bfloat16)
    w_out_grad = lax.dot_general(
        activated, grad_whole, (((0,), (0,)), ((), ())), preferred_element_type=jnp.float32
    ).astype(jnp.bfloat16)
    width = w_out.shape[1]
    forward = jnp.dot(activated, w_out, preferred_element_type=jnp.float32)
    backward = lax.dot_general(
        grad_pre, w_in, (((1,), (1,)), ((), ())), preferred_element_type=jnp.float32
    )
    summed = lax.psum_scatter(
        jnp.concatenate([forward, backward], axis=1), ("dp", "col"), scatter_dimension=0, tiled=True
    )
    layer_output = summed[:, :width].astype(jnp.bfloat16)
    input_grad = summed[:, width:].astype(jnp.bfloat16)
    return (layer_output, input_grad, w_in_grad, w_out_grad)


def solution(mesh):
    in_specs = (
        P(("dp", "col"), "row"),
        P(("dp", "col"), "row"),
        P("row", ("dp", "col")),
        P(("dp", "col"), "row"),
    )
    out_specs = (
        P(("dp", "col"), "row"),
        P(("dp", "col"), "row"),
        P("row", ("dp", "col")),
        P(("dp", "col"), "row"),
    )
    return jax.shard_map(
        on_device, mesh=mesh, in_specs=in_specs, out_specs=out_specs, check_vma=False
    )
```

profile of v0, /device:TPU:1, one launch (start us, length us, event | category | flops | bytes accessed | tf_op | source)
XLA Modules:
  0.0 858.1 jit_solution(2788734068515596788)
XLA Ops:
  7.2 0.0 copy-start
  7.2 0.0 all-gather.5.cloned.1.call-start
  7.2 0.7 all-gather.5.cloned.1.call-update
  7.9 0.0 all-gather.7.cloned.1.call-start
  8.0 0.7 all-gather.7.cloned.1.call-update
  8.7 0.0 reduce-scatter.3.cloned.1.call-start
  8.7 186.4 %all-gather.5.cloned.1.call-done = bf16[64,4,3072]{2,1,0:T(4,128)(2,1)} async-done(((bf16[1,4,3072]{2,1,0:T(4,128)(2,1)}), bf16[64,4,3072]{2,1,0:T(4,128)(2,1)}) %all-gather.5.cloned.1.call-update) | async-done | bytes 1572880 | tf_op jit(solution)/shard_map/all_gather | solution.py:24
  195.1 3.7 reshape.9
  198.8 3.1 fusion.9
  201.9 0.0 reduce-scatter.3.cloned.1.call-update
  201.9 0.0 reduce-scatter.5.cloned.1.call-start
  202.0 180.5 %all-gather.7.cloned.1.call-done = bf16[64,4,3072]{2,1,0:T(4,128)(2,1)} async-done(((bf16[1,4,3072]{2,1,0:T(4,128)(2,1)}), bf16[64,4,3072]{2,1,0:T(4,128)(2,1)}) %all-gather.7.cloned.1.call-update) | async-done | bytes 1572880 | tf_op jit(solution)/shard_map/all_gather | solution.py:25
  382.5 3.7 reshape.11
  386.2 3.9 fusion.11
  390.1 0.0 reduce-scatter.5.cloned.1.call-update
  390.2 0.6 dynamic-slice
  391.4 19.2 %reduce-scatter.3.cloned.1.call-done = f32[64,384]{1,0:T(8,128)} async-done(((f32[256,384]{1,0:T(8,128)}), f32[64,384]{1,0:T(8,128)}) %reduce-scatter.3.cloned.1.call-update) | async-done | bytes 98320 | tf_op jit(solution)/shard_map/reduce_scatter | solution.py:32
  410.6 25.7 %reduce-scatter.5.cloned.1.call-done = f32[64,384]{1,0:T(8,128)} async-done(((f32[256,384]{1,0:T(8,128)}), f32[64,384]{1,0:T(8,128)}) %reduce-scatter.5.cloned.1.call-update) | async-done | bytes 98320 | tf_op jit(solution)/shard_map/reduce_scatter | solution.py:33
  436.4 1.0 multiply_convert_fusion
  437.4 9.8 %all_gather.15 = bf16[256,384]{1,0:T(8,128)(2,1)S(1)} all-gather(bf16[64,384]{1,0:T(8,128)(2,1)S(1)} %get-tuple-element.13), channel_id=1, replica_groups=mesh['dp'=16,'row'=4,'col'=4] {'row'}, dimensions={0}, use_global_device_ids=true | all-gather | bytes 245760 | tf_op jit(solution)/shard_map/all_gather | solution.py:39
  447.2 1.0 fusion.12
  448.2 0.4 copy-done.1
  448.6 2.2 fusion
  450.8 9.2 %all_gather.13 = bf16[256,384]{1,0:T(8,128)(2,1)S(1)} all-gather(bf16[64,384]{1,0:T(8,128)(2,1)S(1)} %get-tuple-element.12), channel_id=1, replica_groups=mesh['dp'=16,'row'=4,'col'=4] {'row'}, dimensions={0}, use_global_device_ids=true | all-gather | bytes 245760 | tf_op jit(solution)/shard_map/all_gather | solution.py:38
  460.0 1.0 fusion.10
  461.0 0.4 copy-done.2
  461.4 2.2 convolution_convert_fusion
  463.6 3.1 pad_maximum_fusion
  466.7 379.0 %all-reduce.2 = bf16[256,6144]{1,0:T(8,128)(2,1)} all-reduce(f32[256,6144]{1,0:T(8,128)} %pad_maximum_fusion), channel_id=4, replica_groups=mesh['dp'=16,'row'=4,'col'=4] {'dp','col'}, use_global_device_ids=true, to_apply=%region_2.0.clone | all-reduce | flops 1572864 | bytes 9437184
  845.8 0.9 dynamic-slice_convert_fusion
  846.7 0.6 fusion.8
  847.3 4.3 copy.9
  (7 shorter events, 0.0 us)
Async XLA Ops:
  7.2 191.6 %copy-start = (bf16[3072,384]{1,0:T(8,128)(2,1)S(1)}, bf16[3072,384]{1,0:T(8,128)(2,1)}, u32[]{:S(2)}) copy-start(bf16[3072,384]{1,0:T(8,128)(2,1)} %param.6) | copy-start | bytes 7077892
  7.2 187.9 %all-gather.5.cloned.1.call-start = ((), (), s32[]{:S(2)}) async-start(), calls=%async_computation.4 | async-start | bytes 1597440 | tf_op jit(solution)/shard_map/all_gather | solution.py:24
  7.9 374.6 %all-gather.7.cloned.1.call-start = ((), (), s32[]{:S(2)}) async-start(), calls=%async_computation.5 | async-start | bytes 1597440 | tf_op jit(solution)/shard_map/all_gather | solution.py:25
  8.7 402.0 %reduce-scatter.3.cloned.1.call-start = ((), (), s32[]{:S(2)}) async-start(), calls=%async_computation.2 | async-start | bytes 491520 | tf_op jit(solution)/shard_map/reduce_scatter | solution.py:32
  201.9 234.4 %reduce-scatter.5.cloned.1.call-start = ((), (), s32[]{:S(2)}) async-start(), calls=%async_computation.3 | async-start | bytes 491520 | tf_op jit(solution)/shard_map/reduce_scatter | solution.py:33
  386.2 3.9 copy-start.4
  447.2 1.4 copy-start.1
  448.6 11.4 %copy-start.3 = (bf16[384,3072]{1,0:T(8,128)(2,1)S(1)}, bf16[384,3072]{1,0:T(8,128)(2,1)}, u32[]{:S(2)}) copy-start(bf16[384,3072]{1,0:T(8,128)(2,1)} %param.7) | copy-start | bytes 7077892
  460.0 1.4 copy-start.2
Sparse Core Ops, SparseCore 0:
  9.8 185.2 all-gather.4
  196.9 185.5 all-gather.6
  385.1 25.5 reduce-scatter.2
  413.2 23.1 reduce-scatter.4
where the time goes:
time: 859 us; the launch traced here: 858 us
  waiting for transfers between devices  413 us (48%)
  blocking collectives  398 us (46%)
  local copies, waits for them, and re-layouts  14.6 us (2%)
  between operations  14.5 us (2%)
  matrix products  13.5 us (2%)
    unnamed x1, blocking collectives  379 us
    all_gather x1, waiting for transfers between devices, on_device(): lax.all_gather(tokens, ('dp', 'col'), axis=0, tiled=True)  186 us
    all_gather x1, waiting for transfers between devices, on_device(): lax.all_gather(cotangent, ('dp', 'col'), axis=0, tiled=True)  181 us
    reduce_scatter x1, waiting for transfers between devices, on_device(): lax.psum_scatter(back_part, 'row', scatter_dimension=0, tiled=True)  25.7 us
    reduce_scatter x1, waiting for transfers between devices, on_device(): lax.psum_scatter(inner_part, 'row', scatter_dimension=0, tiled=True)  19.2 us
  transfers between devices with their start and end apart: 4, of which 4 were waited for; matrix products, arithmetic and copies ran while one was open for 2% of the time, Pallas kernels for 0%

commit v1 on v0

v1 whole, which is shorter than its diff:
```python
import jax
import jax.numpy as jnp
from jax import lax
from jax.sharding import PartitionSpec as P

SQRT_TWO_PI = 0.7978845608028654
CUBIC = 0.044715
PLANE = ("dp", "col")
NX, NZ, NC = 4, 8, 2
BF16, F32 = jnp.bfloat16, jnp.float32


def place(flat):
    dp, z_hi = divmod(flat, 4)
    return dp // 4, z_hi * 2 + (dp // 2) % 2, dp % 2


def index(x, z, core):
    x, z, core = x % NX, z % NZ, core % NC
    return ((x * 2 + z % 2) * 2 + core) * 4 + z // 2


def pairs(source_of):
    return [(index(*source_of(*place(f))), f) for f in range(NX * NZ * NC)]


def inverse(perm):
    return [(b, a) for a, b in perm]


OTHER_CORE = pairs(lambda x, z, c: (x, z, c + 1))
Z_SLOTS = [pairs(lambda x, z, c: (x, z + 4 * c, c))] + [
    pairs(lambda x, z, c, d=d: (x, z + (d if c == 0 else -d), c)) for d in (1, 2, 3)
]
X_SLOTS = [pairs(lambda x, z, c, d=d: (x + d, z, c)) for d in (1, 2, 3)]
ROW_SHIFTS = [[(i, (i + d) % 4) for i in range(4)] for d in (1, 2, 3)]


def send(value, perm):
    return lax.ppermute(value, PLANE, perm)


def gelu_both(preact):
    tangent = jnp.tanh(SQRT_TWO_PI * (preact + CUBIC * preact * preact * preact))
    value = 0.5 * preact * (1.0 + tangent)
    slope = 0.5 * (1.0 + tangent) + 0.5 * preact * (1.0 - tangent * tangent) * SQRT_TWO_PI * (
        1.0 + 3.0 * CUBIC * preact * preact
    )
    return value, slope


def collect_x(share):
    own = jnp.concatenate([share] + [send(share, p) for p in X_SLOTS], axis=0)
    return own, send(own, OTHER_CORE)


def sum_rows(part):
    rounded = part.astype(BF16)
    for shift in ROW_SHIFTS:
        part = part + lax.ppermute(rounded, "row", shift).astype(F32)
    return part


def reduce_x(part):
    half = part.shape[0] // 2
    total = part[:half] + send(part[half:].astype(BF16), OTHER_CORE).astype(F32)
    rows = half // NX
    rounded = total[rows:].astype(BF16)
    total = total[:rows]
    for i, perm in enumerate(X_SLOTS):
        total = total + send(rounded[i * rows : (i + 1) * rows], inverse(perm)).astype(F32)
    return total


def on_device(tokens, cotangent, w_in, w_out):
    width = tokens.shape[1]
    mine = jnp.stack([tokens, cotangent])
    block = jnp.concatenate([mine, send(mine, OTHER_CORE)], axis=1)
    share = jnp.concatenate([send(block, p) for p in Z_SLOTS], axis=1)

    x_own, x_other = collect_x(share[0])
    g_own, g_other = collect_x(share[1])
    x_whole = jnp.concatenate([x_own, x_other], axis=0)
    g_whole = jnp.concatenate([g_own, g_other], axis=0)

    preact = sum_rows(jnp.dot(x_whole, w_in, preferred_element_type=F32))
    value, slope = gelu_both(preact)
    activated = value.astype(BF16)
    forward = reduce_x(jnp.dot(activated, w_out, preferred_element_type=F32))

    grad_act = sum_rows(
        lax.dot_general(g_whole, w_out, (((1,), (1,)), ((), ())), preferred_element_type=F32)
    )
    grad_pre = (grad_act * slope).astype(BF16)
    backward = reduce_x(
        lax.dot_general(grad_pre, w_in, (((1,), (1,)), ((), ())), preferred_element_type=F32)
    )

    w_in_grad = lax.dot_general(
        x_whole, grad_pre, (((0,), (0,)), ((), ())), preferred_element_type=F32
    ).astype(BF16)
    w_out_grad = lax.dot_general(
        activated, g_whole, (((0,), (0,)), ((), ())), preferred_element_type=F32
    ).astype(BF16)

    both = jnp.stack([forward, backward]).astype(BF16)
    summed = jnp.zeros((2, 8, width), F32)
    for i, perm in enumerate(Z_SLOTS):
        summed = summed + send(both[:, 8 * i : 8 * i + 8], inverse(perm)).astype(F32)
    summed = summed[:, :4] + send(summed[:, 4:], OTHER_CORE)
    layer_output, input_grad = summed[0].astype(BF16), summed[1].astype(BF16)
    return (layer_output, input_grad, w_in_grad, w_out_grad)


def solution(mesh):
    in_specs = (
        P(PLANE, "row"),
        P(PLANE, "row"),
        P("row", PLANE),
        P(PLANE, "row"),
    )
    out_specs = (
        P(PLANE, "row"),
        P(PLANE, "row"),
        P("row", PLANE),
        P(PLANE, "row"),
    )
    return jax.shard_map(
        on_device, mesh=mesh, in_specs=in_specs, out_specs=out_specs, check_vma=False
    )
```

time: 859 us -> 119 us (0.14)
  blocking collectives: 398 us -> 0 us
  waiting for transfers between devices: 413 us -> 56.7 us
  starting transfers between devices: 0.16 us -> 46.3 us
  between operations: 14.5 us -> 0.95 us
  local copies, waits for them, and re-layouts: 14.6 us -> 2.72 us
    unnamed x1 -> x0, blocking collectives: 379 us -> none
    all_gather x2 -> x0, waiting for transfers between devices: 367 us -> none  [the longest x1 186 us: on_device(): lax.all_gather(tokens, ('dp', 'col'), axis=0, tiled=True)]
    ppermute x0 -> x32, waiting for transfers between devices: none -> 56.7 us  [the longest x26 41.5 us: send(): return lax.ppermute(value, PLANE, perm)]
    ppermute x0 -> x32, starting transfers between devices: none -> 46.3 us  [the longest x26 39 us: send(): return lax.ppermute(value, PLANE, perm)]
    reduce_scatter x2 -> x0, waiting for transfers between devices: 45 us -> none  [the longest x1 25.7 us: on_device(): lax.psum_scatter(back_part, 'row', scatter_dimension=0, tiled=True)]
    all_gather x2 -> x0, blocking collectives: 19 us -> none  [the longest x1 9.78 us: on_device(): lax.all_gather(grad_share, 'row', axis=0, tiled=True)]
    unnamed x14, local copies, waits for them, and re-layouts: 13 us -> 1.65 us
  transfers between devices with their start and end apart: 4 -> 32, of which waited for: 4 -> 23; matrix products, arithmetic and copies ran while one was open for 2% -> 7% of each run, Pallas kernels for 0% -> 0%
where the time goes in v1:
time: 119 us; the launch traced here: 118 us
  waiting for transfers between devices  56.7 us (48%)
  starting transfers between devices  46.3 us (39%)
  matrix products  8.62 us (7%)
  other arithmetic  3.03 us (3%)
  local copies, waits for them, and re-layouts  2.72 us (2%)
    ppermute x26, waiting for transfers between devices, send(): return lax.ppermute(value, PLANE, perm)  41.5 us
    ppermute x26, starting transfers between devices, send(): return lax.ppermute(value, PLANE, perm)  39 us
    ppermute x6, waiting for transfers between devices, sum_rows(): part = part + lax.ppermute(rounded, 'row', shift).astype(F32)  15.3 us
    ppermute x6, starting transfers between devices, sum_rows(): part = part + lax.ppermute(rounded, 'row', shift).astype(F32)  7.33 us
    dot_general x1, matrix products, on_device(): lax.dot_general(x_whole, grad_pre, (((0,), (0,)), ((), ())), preferred_el...  2.43 us
  transfers between devices with their start and end apart: 32, of which 23 were waited for; matrix products, arithmetic and copies ran while one was open for 7% of the time, Pallas kernels for 0%

profile of v1, /device:TPU:1, one launch (start us, length us, event | category | flops | bytes accessed | tf_op | source)
XLA Modules:
  0.0 118.3 jit_solution(16856453342987670404)
XLA Ops:
  1.6 3.3 %collective-permute-start = (bf16[2,4,3072]{2,1,0:T(4,128)(2,1)S(1)}, bf16[2,4,3072]{2,1,0:T(4,128)(2,1)S(1)}, u32[]{:S(2)}, u32[]{:S(2)}) collective-permute-start(bf16[2,4,3072]{2,1,0:T(4,128)(2,1)S(1)} %pad_maximum_fusion.4), channel_id=1, source_target_pairs={{16,0},{17,1},{18,2},{19,3},{0,16},{1,17},{2,18},{3,19},{48,32},{4... | collective-permute-start | bytes 147464 | tf_op jit(solution)/shard_map/ppermute | solution.py:40
  6.6 7.1 %collective-permute-start.1 = (bf16[2,8,3072]{2,1,0:T(8,128)(2,1)S(1)}, bf16[2,8,3072]{2,1,0:T(8,128)(2,1)S(1)}, u32[]{:S(2)}, u32[]{:S(2)}) collective-permute-start(bf16[2,8,3072]{2,1,0:T(8,128)(2,1)S(1)} %pad_maximum_fusion.3), channel_id=1, source_target_pairs={{0,0},{1,1},{2,2},{3,3},{18,16},{19,17},{16,18},{17,19},{32,32},{3... | collective-permute-start | bytes 294920 | tf_op jit(solution)/shard_map/ppermute | solution.py:40
  16.0 2.8 %collective-permute-done.2 = bf16[2,8,3072]{2,1,0:T(8,128)(2,1)S(1)} collective-permute-done((bf16[2,8,3072]{2,1,0:T(8,128)(2,1)S(1)}, bf16[2,8,3072]{2,1,0:T(8,128)(2,1)S(1)}, u32[]{:S(2)}, u32[]{:S(2)}) %collective-permute-start.2) | collective-permute-done | bytes 98336 | tf_op jit(solution)/shard_map/ppermute | solution.py:40
  18.8 4.5 %collective-permute-done.3 = bf16[2,8,3072]{2,1,0:T(8,128)(2,1)S(1)} collective-permute-done((bf16[2,8,3072]{2,1,0:T(8,128)(2,1)S(1)}, bf16[2,8,3072]{2,1,0:T(8,128)(2,1)S(1)}, u32[]{:S(2)}, u32[]{:S(2)}) %collective-permute-start.3) | collective-permute-done | bytes 98336 | tf_op jit(solution)/shard_map/ppermute | solution.py:40
  23.3 2.6 %collective-permute-start.5 = (bf16[32,3072]{1,0:T(8,128)(2,1)S(1)}, bf16[32,3072]{1,0:T(8,128)(2,1)S(1)}, u32[]{:S(2)}, u32[]{:S(2)}) collective-permute-start(bf16[32,3072]{1,0:T(8,128)(2,1)S(1)} %get-tuple-element.20), channel_id=1, source_target_pairs={{64,0},{65,1},{66,2},{67,3},{80,16},{81,17},{82,18},{83,19},{96,32... | collective-permute-start | bytes 589832 | tf_op jit(solution)/shard_map/ppermute | solution.py:40
  27.0 2.1 %collective-permute-start.16 = (bf16[32,3072]{1,0:T(8,128)(2,1)S(1)}, bf16[32,3072]{1,0:T(8,128)(2,1)S(1)}, u32[]{:S(2)}, u32[]{:S(2)}) collective-permute-start(bf16[32,3072]{1,0:T(8,128)(2,1)S(1)} %get-tuple-element.21), channel_id=1, source_target_pairs={{64,0},{65,1},{66,2},{67,3},{80,16},{81,17},{82,18},{83,19},{96,32... | collective-permute-start | bytes 589832 | tf_op jit(solution)/shard_map/ppermute | solution.py:40
  30.4 3.7 %collective-permute-done.5 = bf16[32,3072]{1,0:T(8,128)(2,1)S(1)} collective-permute-done((bf16[32,3072]{1,0:T(8,128)(2,1)S(1)}, bf16[32,3072]{1,0:T(8,128)(2,1)S(1)}, u32[]{:S(2)}, u32[]{:S(2)}) %collective-permute-start.5) | collective-permute-done | bytes 196640 | tf_op jit(solution)/shard_map/ppermute | solution.py:40
  34.4 4.5 %collective-permute-done.7 = bf16[32,3072]{1,0:T(8,128)(2,1)S(1)} collective-permute-done((bf16[32,3072]{1,0:T(8,128)(2,1)S(1)}, bf16[32,3072]{1,0:T(8,128)(2,1)S(1)}, u32[]{:S(2)}, u32[]{:S(2)}) %collective-permute-start.7) | collective-permute-done | bytes 196640 | tf_op jit(solution)/shard_map/ppermute | solution.py:40
  39.0 1.5 %collective-permute-done.16 = bf16[32,3072]{1,0:T(8,128)(2,1)S(1)} collective-permute-done((bf16[32,3072]{1,0:T(8,128)(2,1)S(1)}, bf16[32,3072]{1,0:T(8,128)(2,1)S(1)}, u32[]{:S(2)}, u32[]{:S(2)}) %collective-permute-start.16) | collective-permute-done | bytes 196640 | tf_op jit(solution)/shard_map/ppermute | solution.py:40
  40.6 1.6 %collective-permute-done.17 = bf16[32,3072]{1,0:T(8,128)(2,1)S(1)} collective-permute-done((bf16[32,3072]{1,0:T(8,128)(2,1)S(1)}, bf16[32,3072]{1,0:T(8,128)(2,1)S(1)}, u32[]{:S(2)}, u32[]{:S(2)}) %collective-permute-start.17) | collective-permute-done | bytes 196640 | tf_op jit(solution)/shard_map/ppermute | solution.py:40
  42.2 2.1 %collective-permute-done.18 = bf16[32,3072]{1,0:T(8,128)(2,1)S(1)} collective-permute-done((bf16[32,3072]{1,0:T(8,128)(2,1)S(1)}, bf16[32,3072]{1,0:T(8,128)(2,1)S(1)}, u32[]{:S(2)}, u32[]{:S(2)}) %collective-permute-start.18) | collective-permute-done | bytes 196640 | tf_op jit(solution)/shard_map/ppermute | solution.py:40
  44.6 1.5 %copy-done.1 = bf16[3072,384]{1,0:T(8,128)(2,1)S(1)} copy-done((bf16[3072,384]{1,0:T(8,128)(2,1)S(1)}, bf16[3072,384]{1,0:T(8,128)(2,1)}, u32[]{:S(2)}) %copy-start.1) | copy-done | bytes 2359320
  47.1 2.8 %collective-permute-start.11 = (bf16[256,384]{1,0:T(8,128)(2,1)S(1)}, bf16[256,384]{1,0:T(8,128)(2,1)S(1)}, u32[]{:S(2)}, u32[]{:S(2)}) collective-permute-start(bf16[256,384]{1,0:T(8,128)(2,1)S(1)} %get-tuple-element.26), channel_id=1, source_target_pairs={{0,12},{4,0},{8,4},{12,8},{1,13},{5,1},{9,5},{13,9},{2,14},{6,2},{... | collective-permute-start | bytes 589832 | tf_op jit(solution)/shard_map/ppermute | solution.py:60
  52.0 2.1 %collective-permute-start.22 = (bf16[256,384]{1,0:T(8,128)(2,1)S(1)}, bf16[256,384]{1,0:T(8,128)(2,1)S(1)}, u32[]{:S(2)}, u32[]{:S(2)}) collective-permute-start(bf16[256,384]{1,0:T(8,128)(2,1)S(1)} %get-tuple-element.28), channel_id=1, source_target_pairs={{0,12},{4,0},{8,4},{12,8},{1,13},{5,1},{9,5},{13,9},{2,14},{6,2},{... | collective-permute-start | bytes 589832 | tf_op jit(solution)/shard_map/ppermute | solution.py:60
  54.1 1.4 %collective-permute-start.21 = (bf16[256,384]{1,0:T(8,128)(2,1)S(1)}, bf16[256,384]{1,0:T(8,128)(2,1)S(1)}, u32[]{:S(2)}, u32[]{:S(2)}) collective-permute-start(bf16[256,384]{1,0:T(8,128)(2,1)S(1)} %get-tuple-element.28), channel_id=1, source_target_pairs={{0,8},{4,12},{8,0},{12,4},{1,9},{5,13},{9,1},{13,5},{2,10},{6,14},... | collective-permute-start | bytes 589832 | tf_op jit(solution)/shard_map/ppermute | solution.py:60
  55.5 1.5 %collective-permute-done.11 = bf16[256,384]{1,0:T(8,128)(2,1)S(1)} collective-permute-done((bf16[256,384]{1,0:T(8,128)(2,1)S(1)}, bf16[256,384]{1,0:T(8,128)(2,1)S(1)}, u32[]{:S(2)}, u32[]{:S(2)}) %collective-permute-start.11) | collective-permute-done | bytes 196640 | tf_op jit(solution)/shard_map/ppermute | solution.py:60
  57.1 6.4 %collective-permute-done.9 = bf16[256,384]{1,0:T(8,128)(2,1)S(1)} collective-permute-done((bf16[256,384]{1,0:T(8,128)(2,1)S(1)}, bf16[256,384]{1,0:T(8,128)(2,1)S(1)}, u32[]{:S(2)}, u32[]{:S(2)}) %collective-permute-start.9) | collective-permute-done | bytes 196640 | tf_op jit(solution)/shard_map/ppermute | solution.py:60
  63.6 2.6 %collective-permute-done.22 = bf16[256,384]{1,0:T(8,128)(2,1)S(1)} collective-permute-done((bf16[256,384]{1,0:T(8,128)(2,1)S(1)}, bf16[256,384]{1,0:T(8,128)(2,1)S(1)}, u32[]{:S(2)}, u32[]{:S(2)}) %collective-permute-start.22) | collective-permute-done | bytes 196640 | tf_op jit(solution)/shard_map/ppermute | solution.py:60
  66.2 4.6 %collective-permute-done.20 = bf16[256,384]{1,0:T(8,128)(2,1)S(1)} collective-permute-done((bf16[256,384]{1,0:T(8,128)(2,1)S(1)}, bf16[256,384]{1,0:T(8,128)(2,1)S(1)}, u32[]{:S(2)}, u32[]{:S(2)}) %collective-permute-start.20) | collective-permute-done | bytes 196640 | tf_op jit(solution)/shard_map/ppermute | solution.py:60
  77.0 2.5 %collective-permute-start.26 = (bf16[32,3072]{1,0:T(8,128)(2,1)S(1)}, bf16[32,3072]{1,0:T(8,128)(2,1)S(1)}, u32[]{:S(2)}, u32[]{:S(2)}) collective-permute-start(bf16[32,3072]{1,0:T(8,128)(2,1)S(1)} %get-tuple-element.14), channel_id=1, source_target_pairs={{0,192},{1,193},{2,194},{3,195},{16,208},{17,209},{18,210},{19,211... | collective-permute-start | bytes 589832 | tf_op jit(solution)/shard_map/ppermute | solution.py:40
  79.5 1.3 %collective-permute-start.25 = (bf16[32,3072]{1,0:T(8,128)(2,1)S(1)}, bf16[32,3072]{1,0:T(8,128)(2,1)S(1)}, u32[]{:S(2)}, u32[]{:S(2)}) collective-permute-start(bf16[32,3072]{1,0:T(8,128)(2,1)S(1)} %get-tuple-element.15), channel_id=1, source_target_pairs={{0,128},{1,129},{2,130},{3,131},{16,144},{17,145},{18,146},{19,147... | collective-permute-start | bytes 589832 | tf_op jit(solution)/shard_map/ppermute | solution.py:40
  81.6 1.4 %collective-permute-done.14 = bf16[32,3072]{1,0:T(8,128)(2,1)S(1)} collective-permute-done((bf16[32,3072]{1,0:T(8,128)(2,1)S(1)}, bf16[32,3072]{1,0:T(8,128)(2,1)S(1)}, u32[]{:S(2)}, u32[]{:S(2)}) %collective-permute-start.14) | collective-permute-done | bytes 196640 | tf_op jit(solution)/shard_map/ppermute | solution.py:40
  82.9 6.2 %collective-permute-done.13 = bf16[32,3072]{1,0:T(8,128)(2,1)S(1)} collective-permute-done((bf16[32,3072]{1,0:T(8,128)(2,1)S(1)}, bf16[32,3072]{1,0:T(8,128)(2,1)S(1)}, u32[]{:S(2)}, u32[]{:S(2)}) %collective-permute-start.13) | collective-permute-done | bytes 196640 | tf_op jit(solution)/shard_map/ppermute | solution.py:40
  89.9 1.5 %collective-permute-done.25 = bf16[32,3072]{1,0:T(8,128)(2,1)S(1)} collective-permute-done((bf16[32,3072]{1,0:T(8,128)(2,1)S(1)}, bf16[32,3072]{1,0:T(8,128)(2,1)S(1)}, u32[]{:S(2)}, u32[]{:S(2)}) %collective-permute-start.25) | collective-permute-done | bytes 196640 | tf_op jit(solution)/shard_map/ppermute | solution.py:40
  91.4 5.2 %collective-permute-done.24 = bf16[32,3072]{1,0:T(8,128)(2,1)S(1)} collective-permute-done((bf16[32,3072]{1,0:T(8,128)(2,1)S(1)}, bf16[32,3072]{1,0:T(8,128)(2,1)S(1)}, u32[]{:S(2)}, u32[]{:S(2)}) %collective-permute-start.24) | collective-permute-done | bytes 196640 | tf_op jit(solution)/shard_map/ppermute | solution.py:40
  96.7 3.8 %collective-permute-start.30 = (bf16[2,8,3072]{2,1,0:T(8,128)(2,1)S(1)}, bf16[2,8,3072]{2,1,0:T(8,128)(2,1)S(1)}, u32[]{:S(2)}, u32[]{:S(2)}) collective-permute-start(bf16[2,8,3072]{2,1,0:T(8,128)(2,1)S(1)} %get-tuple-element.18), channel_id=1, source_target_pairs={{0,33},{1,34},{2,35},{3,32},{16,50},{17,51},{18,48},{19,49},{32,2}... | collective-permute-start | bytes 294920 | tf_op jit(solution)/shard_map/ppermute | solution.py:40
  100.5 2.3 %collective-permute-start.29 = (bf16[2,8,3072]{2,1,0:T(8,128)(2,1)S(1)}, bf16[2,8,3072]{2,1,0:T(8,128)(2,1)S(1)}, u32[]{:S(2)}, u32[]{:S(2)}) collective-permute-start(bf16[2,8,3072]{2,1,0:T(8,128)(2,1)S(1)} %get-tuple-element.19), channel_id=1, source_target_pairs={{0,1},{1,2},{2,3},{3,0},{16,19},{17,16},{18,17},{19,18},{32,33},{3... | collective-permute-start | bytes 294920 | tf_op jit(solution)/shard_map/ppermute | solution.py:40
  102.8 2.1 %collective-permute-start.28 = (bf16[2,8,3072]{2,1,0:T(8,128)(2,1)S(1)}, bf16[2,8,3072]{2,1,0:T(8,128)(2,1)S(1)}, u32[]{:S(2)}, u32[]{:S(2)}) collective-permute-start(bf16[2,8,3072]{2,1,0:T(8,128)(2,1)S(1)} %get-tuple-element.17), channel_id=1, source_target_pairs={{0,32},{1,33},{2,34},{3,35},{16,51},{17,48},{18,49},{19,50},{32,1}... | collective-permute-start | bytes 294920 | tf_op jit(solution)/shard_map/ppermute | solution.py:40
  105.0 4.7 %collective-permute-start.27 = (bf16[2,8,3072]{2,1,0:T(8,128)(2,1)S(1)}, bf16[2,8,3072]{2,1,0:T(8,128)(2,1)S(1)}, u32[]{:S(2)}, u32[]{:S(2)}) collective-permute-start(bf16[2,8,3072]{2,1,0:T(8,128)(2,1)S(1)} %get-tuple-element.16), channel_id=1, source_target_pairs={{0,0},{1,1},{2,2},{3,3},{16,18},{17,19},{18,16},{19,17},{32,32},{3... | collective-permute-start | bytes 294920 | tf_op jit(solution)/shard_map/ppermute | solution.py:40
  109.6 2.4 %convolution_convert_fusion.1 = bf16[3072,384]{1,0:T(8,128)(2,1)} fusion(bf16[256,3072]{1,0:T(8,128)(2,1)S(1)} %constant_dynamic-update-slice_fusion.4, bf16[256,384]{1,0:T(8,128)(2,1)S(1)} %get-tuple-element.9), kind=kOutput, calls=%fused_computation.1 | convolution fusion | flops 605159424 | bytes 4128768 | tf_op jit(solution)/shard_map/dot_general | solution.py:99
  112.1 3.2 %collective-permute-done.27 = bf16[2,8,3072]{2,1,0:T(8,128)(2,1)S(1)} collective-permute-done((bf16[2,8,3072]{2,1,0:T(8,128)(2,1)S(1)}, bf16[2,8,3072]{2,1,0:T(8,128)(2,1)S(1)}, u32[]{:S(2)}, u32[]{:S(2)}) %collective-permute-start.27) | collective-permute-done | bytes 98336 | tf_op jit(solution)/shard_map/ppermute | solution.py:40
  115.4 2.2 %convolution_convert_fusion = bf16[384,3072]{1,0:T(8,128)(2,1)} fusion(bf16[256,384]{1,0:T(8,128)(2,1)S(1)} %get-tuple-element.8, bf16[256,3072]{1,0:T(8,128)(2,1)S(1)} %constant_dynamic-update-slice_fusion.9), kind=kOutput, calls=%fused_computation | convolution fusion | flops 605159424 | bytes 4128768 | tf_op jit(solution)/shard_map/dot_general | solution.py:102
  (74 shorter events, 19.9 us)
Async XLA Ops:
  1.6 4.2 %collective-permute-start = (bf16[2,4,3072]{2,1,0:T(4,128)(2,1)S(1)}, bf16[2,4,3072]{2,1,0:T(4,128)(2,1)S(1)}, u32[]{:S(2)}, u32[]{:S(2)}) collective-permute-start(bf16[2,4,3072]{2,1,0:T(4,128)(2,1)S(1)} %pad_maximum_fusion.4), channel_id=1, source_target_pairs={{16,0},{17,1},{18,2},{19,3},{0,16},{1,17},{2,18},{3,19},{48,32},{4... | collective-permute-start | bytes 147464 | tf_op jit(solution)/shard_map/ppermute | solution.py:40
  6.6 9.4 %collective-permute-start.1 = (bf16[2,8,3072]{2,1,0:T(8,128)(2,1)S(1)}, bf16[2,8,3072]{2,1,0:T(8,128)(2,1)S(1)}, u32[]{:S(2)}, u32[]{:S(2)}) collective-permute-start(bf16[2,8,3072]{2,1,0:T(8,128)(2,1)S(1)} %pad_maximum_fusion.3), channel_id=1, source_target_pairs={{0,0},{1,1},{2,2},{3,3},{18,16},{19,17},{16,18},{17,19},{32,32},{3... | collective-permute-start | bytes 294920 | tf_op jit(solution)/shard_map/ppermute | solution.py:40
  13.7 5.1 %collective-permute-start.2 = (bf16[2,8,3072]{2,1,0:T(8,128)(2,1)S(1)}, bf16[2,8,3072]{2,1,0:T(8,128)(2,1)S(1)}, u32[]{:S(2)}, u32[]{:S(2)}) collective-permute-start(bf16[2,8,3072]{2,1,0:T(8,128)(2,1)S(1)} %pad_maximum_fusion.3), channel_id=1, source_target_pairs={{32,0},{33,1},{34,2},{35,3},{51,16},{48,17},{49,18},{50,19},{1,32}... | collective-permute-start | bytes 294920 | tf_op jit(solution)/shard_map/ppermute | solution.py:40
  14.5 8.7 %collective-permute-start.3 = (bf16[2,8,3072]{2,1,0:T(8,128)(2,1)S(1)}, bf16[2,8,3072]{2,1,0:T(8,128)(2,1)S(1)}, u32[]{:S(2)}, u32[]{:S(2)}) collective-permute-start(bf16[2,8,3072]{2,1,0:T(8,128)(2,1)S(1)} %pad_maximum_fusion.3), channel_id=1, source_target_pairs={{1,0},{2,1},{3,2},{0,3},{19,16},{16,17},{17,18},{18,19},{33,32},{3... | collective-permute-start | bytes 294920 | tf_op jit(solution)/shard_map/ppermute | solution.py:40
  15.7 7.6 %collective-permute-start.4 = (bf16[2,8,3072]{2,1,0:T(8,128)(2,1)S(1)}, bf16[2,8,3072]{2,1,0:T(8,128)(2,1)S(1)}, u32[]{:S(2)}, u32[]{:S(2)}) collective-permute-start(bf16[2,8,3072]{2,1,0:T(8,128)(2,1)S(1)} %pad_maximum_fusion.3), channel_id=1, source_target_pairs={{33,0},{34,1},{35,2},{32,3},{50,16},{51,17},{48,18},{49,19},{2,32}... | collective-permute-start | bytes 294920 | tf_op jit(solution)/shard_map/ppermute | solution.py:40
  23.3 10.8 %collective-permute-start.5 = (bf16[32,3072]{1,0:T(8,128)(2,1)S(1)}, bf16[32,3072]{1,0:T(8,128)(2,1)S(1)}, u32[]{:S(2)}, u32[]{:S(2)}) collective-permute-start(bf16[32,3072]{1,0:T(8,128)(2,1)S(1)} %get-tuple-element.20), channel_id=1, source_target_pairs={{64,0},{65,1},{66,2},{67,3},{80,16},{81,17},{82,18},{83,19},{96,32... | collective-permute-start | bytes 589832 | tf_op jit(solution)/shard_map/ppermute | solution.py:40
  25.9 8.5 %collective-permute-start.6 = (bf16[32,3072]{1,0:T(8,128)(2,1)S(1)}, bf16[32,3072]{1,0:T(8,128)(2,1)S(1)}, u32[]{:S(2)}, u32[]{:S(2)}) collective-permute-start(bf16[32,3072]{1,0:T(8,128)(2,1)S(1)} %get-tuple-element.20), channel_id=1, source_target_pairs={{128,0},{129,1},{130,2},{131,3},{144,16},{145,17},{146,18},{147,19... | collective-permute-start | bytes 589832 | tf_op jit(solution)/shard_map/ppermute | solution.py:40
  26.4 12.5 %collective-permute-start.7 = (bf16[32,3072]{1,0:T(8,128)(2,1)S(1)}, bf16[32,3072]{1,0:T(8,128)(2,1)S(1)}, u32[]{:S(2)}, u32[]{:S(2)}) collective-permute-start(bf16[32,3072]{1,0:T(8,128)(2,1)S(1)} %get-tuple-element.20), channel_id=1, source_target_pairs={{192,0},{193,1},{194,2},{195,3},{208,16},{209,17},{210,18},{211,19... | collective-permute-start | bytes 589832 | tf_op jit(solution)/shard_map/ppermute | solution.py:40
  27.0 13.5 %collective-permute-start.16 = (bf16[32,3072]{1,0:T(8,128)(2,1)S(1)}, bf16[32,3072]{1,0:T(8,128)(2,1)S(1)}, u32[]{:S(2)}, u32[]{:S(2)}) collective-permute-start(bf16[32,3072]{1,0:T(8,128)(2,1)S(1)} %get-tuple-element.21), channel_id=1, source_target_pairs={{64,0},{65,1},{66,2},{67,3},{80,16},{81,17},{82,18},{83,19},{96,32... | collective-permute-start | bytes 589832 | tf_op jit(solution)/shard_map/ppermute | solution.py:40
  29.2 13.0 %collective-permute-start.17 = (bf16[32,3072]{1,0:T(8,128)(2,1)S(1)}, bf16[32,3072]{1,0:T(8,128)(2,1)S(1)}, u32[]{:S(2)}, u32[]{:S(2)}) collective-permute-start(bf16[32,3072]{1,0:T(8,128)(2,1)S(1)} %get-tuple-element.21), channel_id=1, source_target_pairs={{128,0},{129,1},{130,2},{131,3},{144,16},{145,17},{146,18},{147,19... | collective-permute-start | bytes 589832 | tf_op jit(solution)/shard_map/ppermute | solution.py:40
  34.1 10.2 %collective-permute-start.18 = (bf16[32,3072]{1,0:T(8,128)(2,1)S(1)}, bf16[32,3072]{1,0:T(8,128)(2,1)S(1)}, u32[]{:S(2)}, u32[]{:S(2)}) collective-permute-start(bf16[32,3072]{1,0:T(8,128)(2,1)S(1)} %get-tuple-element.21), channel_id=1, source_target_pairs={{192,0},{193,1},{194,2},{195,3},{208,16},{209,17},{210,18},{211,19... | collective-permute-start | bytes 589832 | tf_op jit(solution)/shard_map/ppermute | solution.py:40
  38.9 5.6 %collective-permute-start.8 = (bf16[128,3072]{1,0:T(8,128)(2,1)S(1)}, bf16[128,3072]{1,0:T(8,128)(2,1)S(1)}, u32[]{:S(2)}, u32[]{:S(2)}) collective-permute-start(bf16[128,3072]{1,0:T(8,128)(2,1)S(1)} %pad_maximum_fusion), channel_id=1, source_target_pairs={{16,0},{17,1},{18,2},{19,3},{0,16},{1,17},{2,18},{3,19},{48,32},{4... | collective-permute-start | bytes 2359304 | tf_op jit(solution)/shard_map/ppermute | solution.py:40
  44.3 6.7 %collective-permute-start.19 = (bf16[128,3072]{1,0:T(8,128)(2,1)S(1)}, bf16[128,3072]{1,0:T(8,128)(2,1)S(1)}, u32[]{:S(2)}, u32[]{:S(2)}) collective-permute-start(bf16[128,3072]{1,0:T(8,128)(2,1)S(1)} %pad_maximum_fusion.1), channel_id=1, source_target_pairs={{16,0},{17,1},{18,2},{19,3},{0,16},{1,17},{2,18},{3,19},{48,32},{4... | collective-permute-start | bytes 2359304 | tf_op jit(solution)/shard_map/ppermute | solution.py:40
  47.1 9.9 %collective-permute-start.11 = (bf16[256,384]{1,0:T(8,128)(2,1)S(1)}, bf16[256,384]{1,0:T(8,128)(2,1)S(1)}, u32[]{:S(2)}, u32[]{:S(2)}) collective-permute-start(bf16[256,384]{1,0:T(8,128)(2,1)S(1)} %get-tuple-element.26), channel_id=1, source_target_pairs={{0,12},{4,0},{8,4},{12,8},{1,13},{5,1},{9,5},{13,9},{2,14},{6,2},{... | collective-permute-start | bytes 589832 | tf_op jit(solution)/shard_map/ppermute | solution.py:60
  49.9 7.2 %collective-permute-start.10 = (bf16[256,384]{1,0:T(8,128)(2,1)S(1)}, bf16[256,384]{1,0:T(8,128)(2,1)S(1)}, u32[]{:S(2)}, u32[]{:S(2)}) collective-permute-start(bf16[256,384]{1,0:T(8,128)(2,1)S(1)} %get-tuple-element.26), channel_id=1, source_target_pairs={{0,8},{4,12},{8,0},{12,4},{1,9},{5,13},{9,1},{13,5},{2,10},{6,14},... | collective-permute-start | bytes 589832 | tf_op jit(solution)/shard_map/ppermute | solution.py:60
  50.3 13.3 %collective-permute-start.9 = (bf16[256,384]{1,0:T(8,128)(2,1)S(1)}, bf16[256,384]{1,0:T(8,128)(2,1)S(1)}, u32[]{:S(2)}, u32[]{:S(2)}) collective-permute-start(bf16[256,384]{1,0:T(8,128)(2,1)S(1)} %get-tuple-element.26), channel_id=1, source_target_pairs={{0,4},{4,8},{8,12},{12,0},{1,5},{5,9},{9,13},{13,1},{2,6},{6,10},{... | collective-permute-start | bytes 589832 | tf_op jit(solution)/shard_map/ppermute | solution.py:60
  52.0 14.2 %collective-permute-start.22 = (bf16[256,384]{1,0:T(8,128)(2,1)S(1)}, bf16[256,384]{1,0:T(8,128)(2,1)S(1)}, u32[]{:S(2)}, u32[]{:S(2)}) collective-permute-start(bf16[256,384]{1,0:T(8,128)(2,1)S(1)} %get-tuple-element.28), channel_id=1, source_target_pairs={{0,12},{4,0},{8,4},{12,8},{1,13},{5,1},{9,5},{13,9},{2,14},{6,2},{... | collective-permute-start | bytes 589832 | tf_op jit(solution)/shard_map/ppermute | solution.py:60
  54.1 12.1 %collective-permute-start.21 = (bf16[256,384]{1,0:T(8,128)(2,1)S(1)}, bf16[256,384]{1,0:T(8,128)(2,1)S(1)}, u32[]{:S(2)}, u32[]{:S(2)}) collective-permute-start(bf16[256,384]{1,0:T(8,128)(2,1)S(1)} %get-tuple-element.28), channel_id=1, source_target_pairs={{0,8},{4,12},{8,0},{12,4},{1,9},{5,13},{9,1},{13,5},{2,10},{6,14},... | collective-permute-start | bytes 589832 | tf_op jit(solution)/shard_map/ppermute | solution.py:60
  57.0 13.7 %collective-permute-start.20 = (bf16[256,384]{1,0:T(8,128)(2,1)S(1)}, bf16[256,384]{1,0:T(8,128)(2,1)S(1)}, u32[]{:S(2)}, u32[]{:S(2)}) collective-permute-start(bf16[256,384]{1,0:T(8,128)(2,1)S(1)} %get-tuple-element.28), channel_id=1, source_target_pairs={{0,4},{4,8},{8,12},{12,0},{1,5},{5,9},{9,13},{13,1},{2,6},{6,10},{... | collective-permute-start | bytes 589832 | tf_op jit(solution)/shard_map/ppermute | solution.py:60
  72.3 2.6 %collective-permute-start.12 = (bf16[128,3072]{1,0:T(8,128)(2,1)S(1)}, bf16[128,3072]{1,0:T(8,128)(2,1)S(1)}, u32[]{:S(2)}, u32[]{:S(2)}) collective-permute-start(bf16[128,3072]{1,0:T(8,128)(2,1)S(1)} %slice.178), channel_id=1, source_target_pairs={{16,0},{17,1},{18,2},{19,3},{0,16},{1,17},{2,18},{3,19},{48,32},{4... | collective-permute-start | bytes 2359304 | tf_op jit(solution)/shard_map/ppermute | solution.py:40
  74.1 2.6 %collective-permute-start.23 = (bf16[128,3072]{1,0:T(8,128)(2,1)S(1)}, bf16[128,3072]{1,0:T(8,128)(2,1)S(1)}, u32[]{:S(2)}, u32[]{:S(2)}) collective-permute-start(bf16[128,3072]{1,0:T(8,128)(2,1)S(1)} %slice.177), channel_id=1, source_target_pairs={{16,0},{17,1},{18,2},{19,3},{0,16},{1,17},{2,18},{3,19},{48,32},{4... | collective-permute-start | bytes 2359304 | tf_op jit(solution)/shard_map/ppermute | solution.py:40
  75.2 6.2 %collective-permute-start.15 = (bf16[32,3072]{1,0:T(8,128)(2,1)S(1)}, bf16[32,3072]{1,0:T(8,128)(2,1)S(1)}, u32[]{:S(2)}, u32[]{:S(2)}) collective-permute-start(bf16[32,3072]{1,0:T(8,128)(2,1)S(1)} %get-tuple-element.11), channel_id=1, source_target_pairs={{0,192},{1,193},{2,194},{3,195},{16,208},{17,209},{18,210},{19,211... | collective-permute-start | bytes 589832 | tf_op jit(solution)/shard_map/ppermute | solution.py:40
  75.6 7.3 %collective-permute-start.14 = (bf16[32,3072]{1,0:T(8,128)(2,1)S(1)}, bf16[32,3072]{1,0:T(8,128)(2,1)S(1)}, u32[]{:S(2)}, u32[]{:S(2)}) collective-permute-start(bf16[32,3072]{1,0:T(8,128)(2,1)S(1)} %get-tuple-element.12), channel_id=1, source_target_pairs={{0,128},{1,129},{2,130},{3,131},{16,144},{17,145},{18,146},{19,147... | collective-permute-start | bytes 589832 | tf_op jit(solution)/shard_map/ppermute | solution.py:40
  76.1 13.0 %collective-permute-start.13 = (bf16[32,3072]{1,0:T(8,128)(2,1)S(1)}, bf16[32,3072]{1,0:T(8,128)(2,1)S(1)}, u32[]{:S(2)}, u32[]{:S(2)}) collective-permute-start(bf16[32,3072]{1,0:T(8,128)(2,1)S(1)} %get-tuple-element.10), channel_id=1, source_target_pairs={{0,64},{1,65},{2,66},{3,67},{16,80},{17,81},{18,82},{19,83},{32,96... | collective-permute-start | bytes 589832 | tf_op jit(solution)/shard_map/ppermute | solution.py:40
  77.0 12.8 %collective-permute-start.26 = (bf16[32,3072]{1,0:T(8,128)(2,1)S(1)}, bf16[32,3072]{1,0:T(8,128)(2,1)S(1)}, u32[]{:S(2)}, u32[]{:S(2)}) collective-permute-start(bf16[32,3072]{1,0:T(8,128)(2,1)S(1)} %get-tuple-element.14), channel_id=1, source_target_pairs={{0,192},{1,193},{2,194},{3,195},{16,208},{17,209},{18,210},{19,211... | collective-permute-start | bytes 589832 | tf_op jit(solution)/shard_map/ppermute | solution.py:40
  79.5 11.9 %collective-permute-start.25 = (bf16[32,3072]{1,0:T(8,128)(2,1)S(1)}, bf16[32,3072]{1,0:T(8,128)(2,1)S(1)}, u32[]{:S(2)}, u32[]{:S(2)}) collective-permute-start(bf16[32,3072]{1,0:T(8,128)(2,1)S(1)} %get-tuple-element.15), channel_id=1, source_target_pairs={{0,128},{1,129},{2,130},{3,131},{16,144},{17,145},{18,146},{19,147... | collective-permute-start | bytes 589832 | tf_op jit(solution)/shard_map/ppermute | solution.py:40
  81.4 15.1 %collective-permute-start.24 = (bf16[32,3072]{1,0:T(8,128)(2,1)S(1)}, bf16[32,3072]{1,0:T(8,128)(2,1)S(1)}, u32[]{:S(2)}, u32[]{:S(2)}) collective-permute-start(bf16[32,3072]{1,0:T(8,128)(2,1)S(1)} %get-tuple-element.13), channel_id=1, source_target_pairs={{0,64},{1,65},{2,66},{3,67},{16,80},{17,81},{18,82},{19,83},{32,96... | collective-permute-start | bytes 589832 | tf_op jit(solution)/shard_map/ppermute | solution.py:40
  96.7 15.4 %collective-permute-start.30 = (bf16[2,8,3072]{2,1,0:T(8,128)(2,1)S(1)}, bf16[2,8,3072]{2,1,0:T(8,128)(2,1)S(1)}, u32[]{:S(2)}, u32[]{:S(2)}) collective-permute-start(bf16[2,8,3072]{2,1,0:T(8,128)(2,1)S(1)} %get-tuple-element.18), channel_id=1, source_target_pairs={{0,33},{1,34},{2,35},{3,32},{16,50},{17,51},{18,48},{19,49},{32,2}... | collective-permute-start | bytes 294920 | tf_op jit(solution)/shard_map/ppermute | solution.py:40
  100.5 11.6 %collective-permute-start.29 = (bf16[2,8,3072]{2,1,0:T(8,128)(2,1)S(1)}, bf16[2,8,3072]{2,1,0:T(8,128)(2,1)S(1)}, u32[]{:S(2)}, u32[]{:S(2)}) collective-permute-start(bf16[2,8,3072]{2,1,0:T(8,128)(2,1)S(1)} %get-tuple-element.19), channel_id=1, source_target_pairs={{0,1},{1,2},{2,3},{3,0},{16,19},{17,16},{18,17},{19,18},{32,33},{3... | collective-permute-start | bytes 294920 | tf_op jit(solution)/shard_map/ppermute | solution.py:40
  102.8 9.2 %collective-permute-start.28 = (bf16[2,8,3072]{2,1,0:T(8,128)(2,1)S(1)}, bf16[2,8,3072]{2,1,0:T(8,128)(2,1)S(1)}, u32[]{:S(2)}, u32[]{:S(2)}) collective-permute-start(bf16[2,8,3072]{2,1,0:T(8,128)(2,1)S(1)} %get-tuple-element.17), channel_id=1, source_target_pairs={{0,32},{1,33},{2,34},{3,35},{16,51},{17,48},{18,49},{19,50},{32,1}... | collective-permute-start | bytes 294920 | tf_op jit(solution)/shard_map/ppermute | solution.py:40
  105.0 10.3 %collective-permute-start.27 = (bf16[2,8,3072]{2,1,0:T(8,128)(2,1)S(1)}, bf16[2,8,3072]{2,1,0:T(8,128)(2,1)S(1)}, u32[]{:S(2)}, u32[]{:S(2)}) collective-permute-start(bf16[2,8,3072]{2,1,0:T(8,128)(2,1)S(1)} %get-tuple-element.16), channel_id=1, source_target_pairs={{0,0},{1,1},{2,2},{3,3},{16,18},{17,19},{18,16},{19,17},{32,32},{3... | collective-permute-start | bytes 294920 | tf_op jit(solution)/shard_map/ppermute | solution.py:40
  115.3 2.3 %collective-permute-start.31 = (f32[2,4,3072]{2,1,0:T(4,128)S(1)}, f32[2,4,3072]{2,1,0:T(4,128)S(1)}, u32[]{:S(2)}, u32[]{:S(2)}) collective-permute-start(f32[2,4,3072]{2,1,0:T(4,128)S(1)} %slice.123), channel_id=1, source_target_pairs={{16,0},{17,1},{18,2},{19,3},{0,16},{1,17},{2,18},{3,19},{48,32},{4... | collective-permute-start | bytes 294920 | tf_op jit(solution)/shard_map/ppermute | solution.py:40
  (2 other events, 52.1 us)

commit v2 on v1

v2 whole, which is shorter than its diff:
```python
import functools

import jax
import jax.numpy as jnp
from jax import lax
from jax.experimental import pallas as pl
from jax.experimental.pallas import tpu as pltpu
from jax.sharding import PartitionSpec as P

SQRT_TWO_PI = 0.7978845608028654
CUBIC = 0.044715
PLANE = ("dp", "col")
NX, NZ, NC = 4, 8, 2
BF16, F32 = jnp.bfloat16, jnp.float32
FLOPS = 4 * 10**9


def place(flat):
    dp, z_hi = divmod(flat, 4)
    return dp // 4, z_hi * 2 + (dp // 2) % 2, dp % 2


def index(x, z, core):
    x, z, core = x % NX, z % NZ, core % NC
    return ((x * 2 + z % 2) * 2 + core) * 4 + z // 2


def pairs(source_of):
    return [(index(*source_of(*place(f))), f) for f in range(NX * NZ * NC)]


def inverse(perm):
    return [(b, a) for a, b in perm]


OTHER_CORE = pairs(lambda x, z, c: (x, z, c + 1))
Z_SLOTS = [pairs(lambda x, z, c: (x, z + 4 * c, c))] + [
    pairs(lambda x, z, c, d=d: (x, z + (d if c == 0 else -d), c)) for d in (1, 2, 3)
]
X_NEXT = pairs(lambda x, z, c: (x + 1 - 2 * c, z, c))
X_FAR = pairs(lambda x, z, c: (x + 2, z, c))
ROW_SHIFTS = [[(i, (i + d) % 4) for i in range(4)] for d in (1, 2, 3)]


def send(value, perm):
    return lax.ppermute(value, PLANE, perm)


def gelu_both(preact):
    tangent = jnp.tanh(SQRT_TWO_PI * (preact + CUBIC * preact * preact * preact))
    value = 0.5 * preact * (1.0 + tangent)
    slope = 0.5 * (1.0 + tangent) + 0.5 * preact * (1.0 - tangent * tangent) * SQRT_TWO_PI * (
        1.0 + 3.0 * CUBIC * preact * preact
    )
    return value, slope


def after(value, *others):
    return lax.optimization_barrier((value,) + others)[0]


def exchange_rows(rounded):
    return [lax.ppermute(rounded, "row", shift) for shift in ROW_SHIFTS]


def total(part, received):
    for piece in received:
        part = part + piece.astype(F32)
    return part


def gather_x(share, both):
    return [share, send(both, X_NEXT), send(share, X_FAR)]


def finish_x(own, back):
    near, far = back
    rows = own.shape[0]
    across = send(near[rows:], OTHER_CORE)
    return total(own, [near[:rows], far, across]).astype(BF16)


def dot(a, b):
    return jnp.dot(a, b, preferred_element_type=F32)


def dot_t(a, b):
    return lax.dot_general(a, b, (((1,), (1,)), ((), ())), preferred_element_type=F32)


def t_dot(a, b):
    return lax.dot_general(a, b, (((0,), (0,)), ((), ())), preferred_element_type=F32)


def rows_of(pieces):
    return jnp.concatenate(pieces, axis=0)


CHUNK = 768


def cuts(size):
    return [slice(k, k + CHUNK) for k in range(0, size, CHUNK)]


def inward(transposed, own, near, far, w_a, w_b, part, rounded):
    units = part.shape[1] // 2
    for i, w in enumerate((w_a, w_b)):
        total = 0.0
        for cut in cuts(own.shape[1]):
            rows = rows_of([own[:, cut], near[:, cut], far[:, cut]])
            total = total + (dot_t(rows, w[:, cut]) if transposed else dot(rows, w[cut, :]))
        columns = slice(i * units, (i + 1) * units)
        part[:, columns] = total
        rounded[:, columns] = total.astype(BF16)


def outward(transposed, hidden, w_a, w_b, own, near, far):
    units = hidden.shape[1] // 2
    a, b = hidden[:, :units], hidden[:, units:]
    n_own, n_near = own.shape[0], near.shape[0]
    for cut in cuts(own.shape[1]):
        if transposed:
            out = dot_t(a, w_a[cut, :]) + dot_t(b, w_b[cut, :])
        else:
            out = dot(a, w_a[:, cut]) + dot(b, w_b[:, cut])
        own[:, cut] = out[:n_own]
        near[:, cut] = out[n_own : n_own + n_near].astype(BF16)
        far[:, cut] = out[n_own + n_near :].astype(BF16)


def forward_body(part, r0, r1, r2, w_a, w_b, activated, slope, own, near, far):
    preact = part[...]
    for r in (r0, r1, r2):
        preact = preact + r[...].astype(F32)
    value, slope[...] = gelu_both(preact)
    hidden = value.astype(BF16)
    activated[...] = hidden
    outward(False, hidden, w_a, w_b, own, near, far)


def backward_body(part, r0, r1, r2, slope, w_a, w_b, grad_pre, own, near, far):
    grad = part[...]
    for r in (r0, r1, r2):
        grad = grad + r[...].astype(F32)
    hidden = (grad * slope[...]).astype(BF16)
    grad_pre[...] = hidden
    outward(True, hidden, w_a, w_b, own, near, far)


def call(body, values, outs, flops=0):
    vmem = pl.BlockSpec(memory_space=pltpu.VMEM)
    return pl.pallas_call(
        body,
        out_shape=[jax.ShapeDtypeStruct(shape, dtype) for shape, dtype in outs],
        in_specs=[vmem] * len(values),
        out_specs=[vmem] * len(outs),
        compiler_params=pltpu.CompilerParams(vmem_limit_bytes=32 * 2**20),
        cost_estimate=pl.CostEstimate(flops=flops, bytes_accessed=0, transcendentals=0),
    )(*values)


def on_device(tokens, cotangent, w_in, w_out):
    width, units = w_in.shape
    mine = jnp.stack([tokens, cotangent])
    block = jnp.concatenate([mine, send(mine, OTHER_CORE)], axis=1)
    share = jnp.concatenate([send(block, p) for p in Z_SLOTS], axis=1)
    across = send(share, OTHER_CORE)
    both = jnp.concatenate([share, across], axis=1)

    x_pieces = gather_x(share[0], both[0])
    w_in_other = send(after(w_in, across), OTHER_CORE)
    w_out_other = send(after(w_out, across), OTHER_CORE)
    rows, hidden_shape = 4 * share.shape[1], (4 * share.shape[1], 2 * units)
    outgoing = [((rows // 4, width), F32), ((rows // 2, width), BF16), ((rows // 4, width), BF16)]
    g_pieces = gather_x(share[1], both[1])
    hidden_out = [(hidden_shape, F32), (hidden_shape, BF16)]

    inner_part, rounded = call(
        functools.partial(inward, False), x_pieces + [w_in, w_in_other], hidden_out, FLOPS
    )
    inner_rest = exchange_rows(rounded)
    g_pieces = [after(piece, inner_part) for piece in g_pieces]
    back_part, rounded = call(
        functools.partial(inward, True), g_pieces + [w_out, w_out_other], hidden_out
    )
    back_rest = exchange_rows(rounded)

    inner_rest = [after(piece, back_part) for piece in inner_rest]
    activated, slope, forward, near, far = call(
        forward_body, [inner_part] + inner_rest + [w_out, w_out_other],
        [(hidden_shape, BF16), (hidden_shape, F32)] + outgoing,
    )
    forward_rest = send(near, inverse(X_NEXT)), send(far, inverse(X_FAR))
    grad_pre, backward, near, far = call(
        backward_body, [back_part] + back_rest + [slope, w_in, w_in_other],
        [(hidden_shape, BF16)] + outgoing,
    )
    backward_rest = send(near, inverse(X_NEXT)), send(far, inverse(X_FAR))
    forward = finish_x(forward, [after(piece, backward) for piece in forward_rest])

    x_own, g_own = rows_of(x_pieces), rows_of(g_pieces)
    rest = after(jnp.stack([x_own[32:], g_own[32:]]), backward)
    rest = send(rest, OTHER_CORE)
    hidden = jnp.stack([activated[:, :units], grad_pre[:, :units]])
    hidden_rest = send(jnp.stack([activated[:, units:], grad_pre[:, units:]]), OTHER_CORE)
    x_whole = rows_of([x_own, across[0], rest[0]])
    g_whole = rows_of([g_own, across[1], rest[1]])
    w_out_grad = t_dot(rows_of([hidden[0], hidden_rest[0]]), g_whole).astype(BF16)
    w_in_grad = t_dot(x_whole, rows_of([hidden[1], hidden_rest[1]])).astype(BF16)

    backward_rest = [after(piece, w_in_grad, w_out_grad, forward) for piece in backward_rest]
    backward = finish_x(backward, backward_rest)
    result = jnp.stack([forward, backward])
    summed = jnp.zeros((2, 8, width), F32)
    for i, perm in enumerate(Z_SLOTS):
        summed = summed + send(result[:, 8 * i : 8 * i + 8], inverse(perm)).astype(F32)
    summed = summed[:, :4] + send(summed[:, 4:].astype(BF16), OTHER_CORE).astype(F32)
    layer_output, input_grad = summed[0].astype(BF16), summed[1].astype(BF16)
    return (layer_output, input_grad, w_in_grad, w_out_grad)


def solution(mesh):
    in_specs = (
        P(PLANE, "row"),
        P(PLANE, "row"),
        P("row", PLANE),
        P(PLANE, "row"),
    )
    out_specs = (
        P(PLANE, "row"),
        P(PLANE, "row"),
        P("row", PLANE),
        P(PLANE, "row"),
    )
    return jax.shard_map(
        on_device, mesh=mesh, in_specs=in_specs, out_specs=out_specs, check_vma=False
    )
```

time: 119 us -> 103 us (0.87)
  waiting for transfers between devices: 56.7 us -> 34.4 us
  starting transfers between devices: 46.3 us -> 53.9 us
  Pallas kernels: 0 us -> 5.24 us
  matrix products: 8.62 us -> 4.64 us
  local copies, waits for them, and re-layouts: 2.72 us -> 1.14 us
    ppermute x26 -> x25, waiting for transfers between devices: 41.5 us -> 29.8 us  [send(): return lax.ppermute(value, PLANE, perm)]
    ppermute x6, waiting for transfers between devices: 15.3 us -> 4.55 us  [exchange_rows(): return [lax.ppermute(rounded, 'row', shift) for shift in ROW_SHIFTS]]
    pallas_call x0 -> x4, Pallas kernels: none -> 5.24 us  [call(): pl.pallas_call(body, out_shape=[jax.ShapeDtypeStruct(shape, dtype) for sh...]
    ppermute x26 -> x25, starting transfers between devices: 39 us -> 44.1 us  [send(): return lax.ppermute(value, PLANE, perm)]
    dot_general x6 -> x2, matrix products: 8.62 us -> 4.64 us  [t_dot(): lax.dot_general(a, b, (((0,), (0,)), ((), ())), preferred_element_type=F32)]
    ppermute x6, starting transfers between devices: 7.33 us -> 9.74 us  [exchange_rows(): return [lax.ppermute(rounded, 'row', shift) for shift in ROW_SHIFTS]]
    unnamed x14 -> x15, local copies, waits for them, and re-layouts: 1.65 us -> 0.21 us
  transfers between devices with their start and end apart: 32 -> 31, of which waited for: 23 -> 15; matrix products, arithmetic and copies ran while one was open for 7% -> 5% of each run, Pallas kernels for 0% -> 5%
where the time goes in v2:
time: 103 us; the launch traced here: 102 us
  starting transfers between devices  53.9 us (52%)
  waiting for transfers between devices  34.4 us (33%)
  Pallas kernels  5.24 us (5%)
  matrix products  4.64 us (5%)
  other arithmetic  2.1 us (2%)
  local copies, waits for them, and re-layouts  1.14 us (1%)
    ppermute x25, starting transfers between devices, send(): return lax.ppermute(value, PLANE, perm)  44.1 us
    ppermute x25, waiting for transfers between devices, send(): return lax.ppermute(value, PLANE, perm)  29.8 us
    ppermute x6, starting transfers between devices, exchange_rows(): return [lax.ppermute(rounded, 'row', shift) for shift in ROW_SHIFTS]  9.74 us
    pallas_call x4, Pallas kernels, call(): pl.pallas_call(body, out_shape=[jax.ShapeDtypeStruct(shape, dtype) for sh...  5.24 us
    dot_general x2, matrix products, t_dot(): lax.dot_general(a, b, (((0,), (0,)), ((), ())), preferred_element_type=F32)  4.64 us
    ppermute x6, waiting for transfers between devices, exchange_rows(): return [lax.ppermute(rounded, 'row', shift) for shift in ROW_SHIFTS]  4.55 us
  transfers between devices with their start and end apart: 31, of which 15 were waited for; matrix products, arithmetic and copies ran while one was open for 5% of the time, Pallas kernels for 5%

profile of v2, /device:TPU:1, one launch (start us, length us, event | category | flops | bytes accessed | tf_op | source)
XLA Modules:
  0.0 102.4 jit_solution(7058324538865793751)
XLA Ops:
  1.4 3.3 %collective-permute-start = (bf16[2,4,3072]{2,1,0:T(4,128)(2,1)S(1)}, bf16[2,4,3072]{2,1,0:T(4,128)(2,1)S(1)}, u32[]{:S(2)}, u32[]{:S(2)}) collective-permute-start(bf16[2,4,3072]{2,1,0:T(4,128)(2,1)S(1)} %pad_maximum_fusion.4), channel_id=1, source_target_pairs={{16,0},{17,1},{18,2},{19,3},{0,16},{1,17},{2,18},{3,19},{48,32},{4... | collective-permute-start | bytes 147464 | tf_op jit(solution)/shard_map/ppermute | solution.py:46
  6.4 7.1 %collective-permute-start.1 = (bf16[2,8,3072]{2,1,0:T(8,128)(2,1)S(1)}, bf16[2,8,3072]{2,1,0:T(8,128)(2,1)S(1)}, u32[]{:S(2)}, u32[]{:S(2)}) collective-permute-start(bf16[2,8,3072]{2,1,0:T(8,128)(2,1)S(1)} %pad_maximum_fusion.3), channel_id=1, source_target_pairs={{0,0},{1,1},{2,2},{3,3},{18,16},{19,17},{16,18},{17,19},{32,32},{3... | collective-permute-start | bytes 294920 | tf_op jit(solution)/shard_map/ppermute | solution.py:46
  14.4 1.2 %collective-permute-start.3 = (bf16[2,8,3072]{2,1,0:T(8,128)(2,1)S(1)}, bf16[2,8,3072]{2,1,0:T(8,128)(2,1)S(1)}, u32[]{:S(2)}, u32[]{:S(2)}) collective-permute-start(bf16[2,8,3072]{2,1,0:T(8,128)(2,1)S(1)} %pad_maximum_fusion.3), channel_id=1, source_target_pairs={{1,0},{2,1},{3,2},{0,3},{19,16},{16,17},{17,18},{18,19},{33,32},{3... | collective-permute-start | bytes 294920 | tf_op jit(solution)/shard_map/ppermute | solution.py:46
  15.8 2.8 %collective-permute-done.2 = bf16[2,8,3072]{2,1,0:T(8,128)(2,1)S(1)} collective-permute-done((bf16[2,8,3072]{2,1,0:T(8,128)(2,1)S(1)}, bf16[2,8,3072]{2,1,0:T(8,128)(2,1)S(1)}, u32[]{:S(2)}, u32[]{:S(2)}) %collective-permute-start.2) | collective-permute-done | bytes 98336 | tf_op jit(solution)/shard_map/ppermute | solution.py:46
  18.6 4.5 %collective-permute-done.3 = bf16[2,8,3072]{2,1,0:T(8,128)(2,1)S(1)} collective-permute-done((bf16[2,8,3072]{2,1,0:T(8,128)(2,1)S(1)}, bf16[2,8,3072]{2,1,0:T(8,128)(2,1)S(1)}, u32[]{:S(2)}, u32[]{:S(2)}) %collective-permute-start.3) | collective-permute-done | bytes 98336 | tf_op jit(solution)/shard_map/ppermute | solution.py:46
  23.3 2.8 %collective-permute-start.7 = (bf16[32,3072]{1,0:T(8,128)(2,1)S(1)}, bf16[32,3072]{1,0:T(8,128)(2,1)S(1)}, u32[]{:S(2)}, u32[]{:S(2)}) collective-permute-start(bf16[32,3072]{1,0:T(8,128)(2,1)S(1)} %get-tuple-element.66.own), channel_id=1, source_target_pairs={{128,0},{129,1},{130,2},{131,3},{144,16},{145,17},{146,18},{147,19... | collective-permute-start | bytes 589832 | tf_op jit(solution)/shard_map/ppermute | solution.py:46
  26.3 1.1 %collective-permute-start.8 = (bf16[3072,384]{1,0:T(8,128)(2,1)}, bf16[3072,384]{1,0:T(8,128)(2,1)S(1)}, u32[]{:S(2)}, u32[]{:S(2)}) collective-permute-start(bf16[3072,384]{1,0:T(8,128)(2,1)} %w_a.7), channel_id=1, source_target_pairs={{16,0},{17,1},{18,2},{19,3},{0,16},{1,17},{2,18},{3,19},{48,32},{4... | collective-permute-start | bytes 7077896 | tf_op jit(solution)/shard_map/ppermute | solution.py:46
  27.5 1.3 %collective-permute-start.6 = (bf16[64,3072]{1,0:T(8,128)(2,1)S(1)}, bf16[64,3072]{1,0:T(8,128)(2,1)S(1)}, u32[]{:S(2)}, u32[]{:S(2)}) collective-permute-start(bf16[64,3072]{1,0:T(8,128)(2,1)S(1)} %get-tuple-element.59), channel_id=1, source_target_pairs={{64,0},{65,1},{66,2},{67,3},{208,16},{209,17},{210,18},{211,19},{9... | collective-permute-start | bytes 1179656 | tf_op jit(solution)/shard_map/ppermute | solution.py:46
  28.8 11.1 %collective-permute-done.6.near = bf16[64,3072]{1,0:T(8,128)(2,1)S(1)} collective-permute-done((bf16[64,3072]{1,0:T(8,128)(2,1)S(1)}, bf16[64,3072]{1,0:T(8,128)(2,1)S(1)}, u32[]{:S(2)}, u32[]{:S(2)}) %collective-permute-start.6) | collective-permute-done | bytes 393248 | tf_op jit(solution)/shard_map/ppermute | solution.py:46
  39.9 1.5 %collective-permute-start.10 = (bf16[64,3072]{1,0:T(8,128)(2,1)S(1)}, bf16[64,3072]{1,0:T(8,128)(2,1)S(1)}, u32[]{:S(2)}, u32[]{:S(2)}) collective-permute-start(bf16[64,3072]{1,0:T(8,128)(2,1)S(1)} %get-tuple-element.58), channel_id=1, source_target_pairs={{64,0},{65,1},{66,2},{67,3},{208,16},{209,17},{210,18},{211,19},{9... | collective-permute-start | bytes 1179656 | tf_op jit(solution)/shard_map/ppermute | solution.py:46
  42.6 1.4 %collective-permute-start.9 = (bf16[128,768]{1,0:T(8,128)(2,1)S(1)}, bf16[128,768]{1,0:T(8,128)(2,1)S(1)}, u32[]{:S(2)}, u32[]{:S(2)}) collective-permute-start(bf16[128,768]{1,0:T(8,128)(2,1)S(1)} %get-tuple-element.32), channel_id=1, source_target_pairs={{0,4},{4,8},{8,12},{12,0},{1,5},{5,9},{9,13},{13,1},{2,6},{6,10},{... | collective-permute-start | bytes 589832 | tf_op jit(solution)/shard_map/ppermute | solution.py:63
  43.9 2.6 %collective-permute-start.13 = (bf16[128,768]{1,0:T(8,128)(2,1)S(1)}, bf16[128,768]{1,0:T(8,128)(2,1)S(1)}, u32[]{:S(2)}, u32[]{:S(2)}) collective-permute-start(bf16[128,768]{1,0:T(8,128)(2,1)S(1)} %get-tuple-element.32), channel_id=1, source_target_pairs={{0,8},{4,12},{8,0},{12,4},{1,9},{5,13},{9,1},{13,5},{2,10},{6,14},... | collective-permute-start | bytes 589832 | tf_op jit(solution)/shard_map/ppermute | solution.py:63
  46.6 1.2 %collective-permute-done.10.near = bf16[64,3072]{1,0:T(8,128)(2,1)S(1)} collective-permute-done((bf16[64,3072]{1,0:T(8,128)(2,1)S(1)}, bf16[64,3072]{1,0:T(8,128)(2,1)S(1)}, u32[]{:S(2)}, u32[]{:S(2)}) %collective-permute-start.10) | collective-permute-done | bytes 393248 | tf_op jit(solution)/shard_map/ppermute | solution.py:46
  47.8 2.7 %collective-permute-start.14 = (bf16[128,768]{1,0:T(8,128)(2,1)S(1)}, bf16[128,768]{1,0:T(8,128)(2,1)S(1)}, u32[]{:S(2)}, u32[]{:S(2)}) collective-permute-start(bf16[128,768]{1,0:T(8,128)(2,1)S(1)} %get-tuple-element.32), channel_id=1, source_target_pairs={{0,12},{4,0},{8,4},{12,8},{1,13},{5,1},{9,5},{13,9},{2,14},{6,2},{... | collective-permute-start | bytes 589832 | tf_op jit(solution)/shard_map/ppermute | solution.py:63
  50.5 1.5 %shard_map.76 = (f32[128,768]{1,0:T(8,128)S(1)}, bf16[128,768]{1,0:T(8,128)(2,1)S(1)}) custom-call(bf16[32,3072]{1,0:T(8,128)(2,1)S(1)} %get-tuple-element.33.own, bf16[64,3072]{1,0:T(8,128)(2,1)S(1)} %collective-permute-done.10.near, bf16[32,3072]{1,0:T(8,128)(2,1)S(1)} %collective-permute-done.11.far, bf16[384,3072]{1,0:T(8,128)(2,1)S(1)} %copy-done, ...), custom_call_target="tpu_custom_call" | custom-call | tf_op jit(solution)/shard_map/pallas_call | solution.py:153
  52.2 1.6 %collective-permute-start.17 = (bf16[128,768]{1,0:T(8,128)(2,1)S(1)}, bf16[128,768]{1,0:T(8,128)(2,1)S(1)}, u32[]{:S(2)}, u32[]{:S(2)}) collective-permute-start(bf16[128,768]{1,0:T(8,128)(2,1)S(1)} %get-tuple-element.43), channel_id=1, source_target_pairs={{0,8},{4,12},{8,0},{12,4},{1,9},{5,13},{9,1},{13,5},{2,10},{6,14},... | collective-permute-start | bytes 589832 | tf_op jit(solution)/shard_map/ppermute | solution.py:63
  54.1 1.1 %collective-permute-start.18 = (bf16[128,768]{1,0:T(8,128)(2,1)S(1)}, bf16[128,768]{1,0:T(8,128)(2,1)S(1)}, u32[]{:S(2)}, u32[]{:S(2)}) collective-permute-start(bf16[128,768]{1,0:T(8,128)(2,1)S(1)} %get-tuple-element.43), channel_id=1, source_target_pairs={{0,12},{4,0},{8,4},{12,8},{1,13},{5,1},{9,5},{13,9},{2,14},{6,2},{... | collective-permute-start | bytes 589832 | tf_op jit(solution)/shard_map/ppermute | solution.py:63
  55.3 1.2 %shard_map.77 = (bf16[128,768]{1,0:T(8,128)(2,1)S(1)}, f32[128,768]{1,0:T(8,128)S(1)}, f32[32,3072]{1,0:T(8,128)S(1)}, bf16[64,3072]{1,0:T(8,128)(2,1)S(1)}, bf16[32,3072]{1,0:T(8,128)(2,1)S(1)}) custom-call(f32[128,768]{1,0:T(8,128)S(1)} %get-tuple-element.31.part, bf16[128,768]{1,0:T(8,128)(2,1)S(1)} %collective-permute-done.9.r0, ...), custom_call_target="tpu_custom_call" | custom-call | tf_op jit(solution)/shard_map/pallas_call | solution.py:153
  56.5 1.3 %collective-permute-start.15 = (bf16[64,3072]{1,0:T(8,128)(2,1)S(1)}, bf16[64,3072]{1,0:T(8,128)(2,1)S(1)}, u32[]{:S(2)}, u32[]{:S(2)}) collective-permute-start(bf16[64,3072]{1,0:T(8,128)(2,1)S(1)} %get-tuple-element.42), channel_id=1, source_target_pairs={{0,64},{1,65},{2,66},{3,67},{16,208},{17,209},{18,210},{19,211},{3... | collective-permute-start | bytes 1179656 | tf_op jit(solution)/shard_map/ppermute | solution.py:46
  57.7 1.9 %collective-permute-start.19 = (bf16[32,3072]{1,0:T(8,128)(2,1)S(1)}, bf16[32,3072]{1,0:T(8,128)(2,1)S(1)}, u32[]{:S(2)}, u32[]{:S(2)}) collective-permute-start(bf16[32,3072]{1,0:T(8,128)(2,1)S(1)} %get-tuple-element.47), channel_id=1, source_target_pairs={{0,128},{1,129},{2,130},{3,131},{16,144},{17,145},{18,146},{19,147... | collective-permute-start | bytes 589832 | tf_op jit(solution)/shard_map/ppermute | solution.py:46
  60.1 3.5 %collective-permute-done.17.r1 = bf16[128,768]{1,0:T(8,128)(2,1)S(1)} collective-permute-done((bf16[128,768]{1,0:T(8,128)(2,1)S(1)}, bf16[128,768]{1,0:T(8,128)(2,1)S(1)}, u32[]{:S(2)}, u32[]{:S(2)}) %collective-permute-start.17) | collective-permute-done | bytes 196640 | tf_op jit(solution)/shard_map/ppermute | solution.py:63
  64.2 1.6 %shard_map.78 = (bf16[128,768]{1,0:T(8,128)(2,1)S(1)}, f32[32,3072]{1,0:T(8,128)S(1)}, bf16[64,3072]{1,0:T(8,128)(2,1)S(1)}, bf16[32,3072]{1,0:T(8,128)(2,1)S(1)}) custom-call(f32[128,768]{1,0:T(8,128)S(1)} %get-tuple-element.37.part, bf16[128,768]{1,0:T(8,128)(2,1)S(1)} %collective-permute-done.16.r0, bf16[128,768]{1,0:T(8,128)(2,1)S(1)} %collective-permute-done.17.r1, ...), custom_call_target="tpu_custom_call" | custom-call | tf_op jit(solution)/shard_map/pallas_call | solution.py:153
  65.8 2.9 %collective-permute-start.22 = (bf16[2,96,3072]{2,1,0:T(8,128)(2,1)S(1)}, bf16[2,96,3072]{2,1,0:T(8,128)(2,1)S(1)}, u32[]{:S(2)}, u32[]{:S(2)}) collective-permute-start(bf16[2,96,3072]{2,1,0:T(8,128)(2,1)S(1)} %pad_maximum_fusion), channel_id=1, source_target_pairs={{16,0},{17,1},{18,2},{19,3},{0,16},{1,17},{2,18},{3,19},{48,32},{4... | collective-permute-start | bytes 3538952 | tf_op jit(solution)/shard_map/ppermute | solution.py:46
  70.0 6.1 %collective-permute-start.20 = (bf16[32,3072]{1,0:T(8,128)(2,1)S(1)}, bf16[32,3072]{1,0:T(8,128)(2,1)S(1)}, u32[]{:S(2)}, u32[]{:S(2)}) collective-permute-start(bf16[32,3072]{1,0:T(8,128)(2,1)S(1)} %slice.90), channel_id=1, source_target_pairs={{16,0},{17,1},{18,2},{19,3},{0,16},{1,17},{2,18},{3,19},{48,32},{4... | collective-permute-start | bytes 589832 | tf_op jit(solution)/shard_map/ppermute | solution.py:46
  76.1 1.0 %collective-permute-done.20 = bf16[32,3072]{1,0:T(8,128)(2,1)S(1)} collective-permute-done((bf16[32,3072]{1,0:T(8,128)(2,1)S(1)}, bf16[32,3072]{1,0:T(8,128)(2,1)S(1)}, u32[]{:S(2)}, u32[]{:S(2)}) %collective-permute-start.20) | collective-permute-done | bytes 196640 | tf_op jit(solution)/shard_map/ppermute | solution.py:46
  77.4 2.4 %convolution_convert_fusion.1 = bf16[3072,384]{1,0:T(8,128)(2,1)} fusion(bf16[256,3072]{1,0:T(8,128)(2,1)S(1)} %get-tuple-element.57, bf16[128,384]{1,0:T(8,128)(2,1)S(1)} %get-tuple-element.71, bf16[128,384]{1,0:T(8,128)(2,1)S(1)} %get-tuple-element.72), kind=kOutput, calls=%fused_computation.1 | convolution fusion | flops 605552640 | bytes 4128768 | tf_op jit(solution)/shard_map/dot_general | solution.py:92
  79.8 2.2 %convolution_convert_fusion = bf16[384,3072]{1,0:T(8,128)(2,1)} fusion(bf16[256,3072]{1,0:T(8,128)(2,1)S(1)} %get-tuple-element.56, bf16[128,384]{1,0:T(8,128)(2,1)S(1)} %get-tuple-element.70, bf16[128,384]{1,0:T(8,128)(2,1)S(1)} %get-tuple-element.68), kind=kOutput, calls=%fused_computation | convolution fusion | flops 605552640 | bytes 4128768 | tf_op jit(solution)/shard_map/dot_general | solution.py:92
  82.5 1.1 %collective-permute-done.25 = bf16[32,3072]{1,0:T(8,128)(2,1)S(1)} collective-permute-done((bf16[32,3072]{1,0:T(8,128)(2,1)S(1)}, bf16[32,3072]{1,0:T(8,128)(2,1)S(1)}, u32[]{:S(2)}, u32[]{:S(2)}) %collective-permute-start.25) | collective-permute-done | bytes 196640 | tf_op jit(solution)/shard_map/ppermute | solution.py:46
  83.7 4.5 %collective-permute-start.29 = (bf16[2,8,3072]{2,1,0:T(8,128)(2,1)S(1)}, bf16[2,8,3072]{2,1,0:T(8,128)(2,1)S(1)}, u32[]{:S(2)}, u32[]{:S(2)}) collective-permute-start(bf16[2,8,3072]{2,1,0:T(8,128)(2,1)S(1)} %get-tuple-element.62), channel_id=1, source_target_pairs={{0,33},{1,34},{2,35},{3,32},{16,50},{17,51},{18,48},{19,49},{32,2}... | collective-permute-start | bytes 294920 | tf_op jit(solution)/shard_map/ppermute | solution.py:46
  88.8 5.7 %collective-permute-start.26 = (bf16[2,8,3072]{2,1,0:T(8,128)(2,1)S(1)}, bf16[2,8,3072]{2,1,0:T(8,128)(2,1)S(1)}, u32[]{:S(2)}, u32[]{:S(2)}) collective-permute-start(bf16[2,8,3072]{2,1,0:T(8,128)(2,1)S(1)} %get-tuple-element.60), channel_id=1, source_target_pairs={{0,0},{1,1},{2,2},{3,3},{16,18},{17,19},{18,16},{19,17},{32,32},{3... | collective-permute-start | bytes 294920 | tf_op jit(solution)/shard_map/ppermute | solution.py:46
  95.7 4.6 %collective-permute-done.26 = bf16[2,8,3072]{2,1,0:T(8,128)(2,1)S(1)} collective-permute-done((bf16[2,8,3072]{2,1,0:T(8,128)(2,1)S(1)}, bf16[2,8,3072]{2,1,0:T(8,128)(2,1)S(1)}, u32[]{:S(2)}, u32[]{:S(2)}) %collective-permute-start.26) | collective-permute-done | bytes 98336 | tf_op jit(solution)/shard_map/ppermute | solution.py:46
  100.5 1.2 %collective-permute-done.30 = bf16[2,4,3072]{2,1,0:T(4,128)(2,1)S(1)} collective-permute-done((bf16[2,4,3072]{2,1,0:T(4,128)(2,1)S(1)}, bf16[2,4,3072]{2,1,0:T(4,128)(2,1)S(1)}, u32[]{:S(2)}, u32[]{:S(2)}) %collective-permute-start.30) | collective-permute-done | bytes 49184 | tf_op jit(solution)/shard_map/ppermute | solution.py:46
  (73 shorter events, 11.3 us)
Async XLA Ops:
  1.4 4.2 %collective-permute-start = (bf16[2,4,3072]{2,1,0:T(4,128)(2,1)S(1)}, bf16[2,4,3072]{2,1,0:T(4,128)(2,1)S(1)}, u32[]{:S(2)}, u32[]{:S(2)}) collective-permute-start(bf16[2,4,3072]{2,1,0:T(4,128)(2,1)S(1)} %pad_maximum_fusion.4), channel_id=1, source_target_pairs={{16,0},{17,1},{18,2},{19,3},{0,16},{1,17},{2,18},{3,19},{48,32},{4... | collective-permute-start | bytes 147464 | tf_op jit(solution)/shard_map/ppermute | solution.py:46
  6.4 9.4 %collective-permute-start.1 = (bf16[2,8,3072]{2,1,0:T(8,128)(2,1)S(1)}, bf16[2,8,3072]{2,1,0:T(8,128)(2,1)S(1)}, u32[]{:S(2)}, u32[]{:S(2)}) collective-permute-start(bf16[2,8,3072]{2,1,0:T(8,128)(2,1)S(1)} %pad_maximum_fusion.3), channel_id=1, source_target_pairs={{0,0},{1,1},{2,2},{3,3},{18,16},{19,17},{16,18},{17,19},{32,32},{3... | collective-permute-start | bytes 294920 | tf_op jit(solution)/shard_map/ppermute | solution.py:46
  13.5 5.1 %collective-permute-start.2 = (bf16[2,8,3072]{2,1,0:T(8,128)(2,1)S(1)}, bf16[2,8,3072]{2,1,0:T(8,128)(2,1)S(1)}, u32[]{:S(2)}, u32[]{:S(2)}) collective-permute-start(bf16[2,8,3072]{2,1,0:T(8,128)(2,1)S(1)} %pad_maximum_fusion.3), channel_id=1, source_target_pairs={{32,0},{33,1},{34,2},{35,3},{51,16},{48,17},{49,18},{50,19},{1,32}... | collective-permute-start | bytes 294920 | tf_op jit(solution)/shard_map/ppermute | solution.py:46
  14.4 8.7 %collective-permute-start.3 = (bf16[2,8,3072]{2,1,0:T(8,128)(2,1)S(1)}, bf16[2,8,3072]{2,1,0:T(8,128)(2,1)S(1)}, u32[]{:S(2)}, u32[]{:S(2)}) collective-permute-start(bf16[2,8,3072]{2,1,0:T(8,128)(2,1)S(1)} %pad_maximum_fusion.3), channel_id=1, source_target_pairs={{1,0},{2,1},{3,2},{0,3},{19,16},{16,17},{17,18},{18,19},{33,32},{3... | collective-permute-start | bytes 294920 | tf_op jit(solution)/shard_map/ppermute | solution.py:46
  15.5 7.6 %collective-permute-start.4 = (bf16[2,8,3072]{2,1,0:T(8,128)(2,1)S(1)}, bf16[2,8,3072]{2,1,0:T(8,128)(2,1)S(1)}, u32[]{:S(2)}, u32[]{:S(2)}) collective-permute-start(bf16[2,8,3072]{2,1,0:T(8,128)(2,1)S(1)} %pad_maximum_fusion.3), channel_id=1, source_target_pairs={{33,0},{34,1},{35,2},{32,3},{50,16},{51,17},{48,18},{49,19},{2,32}... | collective-permute-start | bytes 294920 | tf_op jit(solution)/shard_map/ppermute | solution.py:46
  23.1 3.2 %collective-permute-start.5 = (bf16[2,32,3072]{2,1,0:T(8,128)(2,1)S(1)}, bf16[2,32,3072]{2,1,0:T(8,128)(2,1)S(1)}, u32[]{:S(2)}, u32[]{:S(2)}) collective-permute-start(bf16[2,32,3072]{2,1,0:T(8,128)(2,1)S(1)} %get-tuple-element.75), channel_id=1, source_target_pairs={{16,0},{17,1},{18,2},{19,3},{0,16},{1,17},{2,18},{3,19},{48,32},{4... | collective-permute-start | bytes 1179656 | tf_op jit(solution)/shard_map/ppermute | solution.py:46
  23.3 18.2 %collective-permute-start.7 = (bf16[32,3072]{1,0:T(8,128)(2,1)S(1)}, bf16[32,3072]{1,0:T(8,128)(2,1)S(1)}, u32[]{:S(2)}, u32[]{:S(2)}) collective-permute-start(bf16[32,3072]{1,0:T(8,128)(2,1)S(1)} %get-tuple-element.66.own), channel_id=1, source_target_pairs={{128,0},{129,1},{130,2},{131,3},{144,16},{145,17},{146,18},{147,19... | collective-permute-start | bytes 589832 | tf_op jit(solution)/shard_map/ppermute | solution.py:46
  26.1 24.4 %collective-permute-start.11 = (bf16[32,3072]{1,0:T(8,128)(2,1)S(1)}, bf16[32,3072]{1,0:T(8,128)(2,1)S(1)}, u32[]{:S(2)}, u32[]{:S(2)}) collective-permute-start(bf16[32,3072]{1,0:T(8,128)(2,1)S(1)} %get-tuple-element.33.own), channel_id=1, source_target_pairs={{128,0},{129,1},{130,2},{131,3},{144,16},{145,17},{146,18},{147,19... | collective-permute-start | bytes 589832 | tf_op jit(solution)/shard_map/ppermute | solution.py:46
  26.3 15.2 %collective-permute-start.8 = (bf16[3072,384]{1,0:T(8,128)(2,1)}, bf16[3072,384]{1,0:T(8,128)(2,1)S(1)}, u32[]{:S(2)}, u32[]{:S(2)}) collective-permute-start(bf16[3072,384]{1,0:T(8,128)(2,1)} %w_a.7), channel_id=1, source_target_pairs={{16,0},{17,1},{18,2},{19,3},{0,16},{1,17},{2,18},{3,19},{48,32},{4... | collective-permute-start | bytes 7077896 | tf_op jit(solution)/shard_map/ppermute | solution.py:46
  27.4 23.1 %collective-permute-start.12 = (bf16[384,3072]{1,0:T(8,128)(2,1)}, bf16[384,3072]{1,0:T(8,128)(2,1)S(1)}, u32[]{:S(2)}, u32[]{:S(2)}) collective-permute-start(bf16[384,3072]{1,0:T(8,128)(2,1)} %w_a.6), channel_id=1, source_target_pairs={{16,0},{17,1},{18,2},{19,3},{0,16},{1,17},{2,18},{3,19},{48,32},{4... | collective-permute-start | bytes 7077896 | tf_op jit(solution)/shard_map/ppermute | solution.py:46
  27.5 14.1 %copy-start.1 = (bf16[3072,384]{1,0:T(8,128)(2,1)S(1)}, bf16[3072,384]{1,0:T(8,128)(2,1)}, u32[]{:S(2)}) copy-start(bf16[3072,384]{1,0:T(8,128)(2,1)} %w_a.7) | copy-start | bytes 7077892
  27.5 12.4 %collective-permute-start.6 = (bf16[64,3072]{1,0:T(8,128)(2,1)S(1)}, bf16[64,3072]{1,0:T(8,128)(2,1)S(1)}, u32[]{:S(2)}, u32[]{:S(2)}) collective-permute-start(bf16[64,3072]{1,0:T(8,128)(2,1)S(1)} %get-tuple-element.59), channel_id=1, source_target_pairs={{64,0},{65,1},{66,2},{67,3},{208,16},{209,17},{210,18},{211,19},{9... | collective-permute-start | bytes 1179656 | tf_op jit(solution)/shard_map/ppermute | solution.py:46
  39.9 7.8 %collective-permute-start.10 = (bf16[64,3072]{1,0:T(8,128)(2,1)S(1)}, bf16[64,3072]{1,0:T(8,128)(2,1)S(1)}, u32[]{:S(2)}, u32[]{:S(2)}) collective-permute-start(bf16[64,3072]{1,0:T(8,128)(2,1)S(1)} %get-tuple-element.58), channel_id=1, source_target_pairs={{64,0},{65,1},{66,2},{67,3},{208,16},{209,17},{210,18},{211,19},{9... | collective-permute-start | bytes 1179656 | tf_op jit(solution)/shard_map/ppermute | solution.py:46
  42.6 11.5 %collective-permute-start.9 = (bf16[128,768]{1,0:T(8,128)(2,1)S(1)}, bf16[128,768]{1,0:T(8,128)(2,1)S(1)}, u32[]{:S(2)}, u32[]{:S(2)}) collective-permute-start(bf16[128,768]{1,0:T(8,128)(2,1)S(1)} %get-tuple-element.32), channel_id=1, source_target_pairs={{0,4},{4,8},{8,12},{12,0},{1,5},{5,9},{9,13},{13,1},{2,6},{6,10},{... | collective-permute-start | bytes 589832 | tf_op jit(solution)/shard_map/ppermute | solution.py:63
  43.9 11.3 %collective-permute-start.13 = (bf16[128,768]{1,0:T(8,128)(2,1)S(1)}, bf16[128,768]{1,0:T(8,128)(2,1)S(1)}, u32[]{:S(2)}, u32[]{:S(2)}) collective-permute-start(bf16[128,768]{1,0:T(8,128)(2,1)S(1)} %get-tuple-element.32), channel_id=1, source_target_pairs={{0,8},{4,12},{8,0},{12,4},{1,9},{5,13},{9,1},{13,5},{2,10},{6,14},... | collective-permute-start | bytes 589832 | tf_op jit(solution)/shard_map/ppermute | solution.py:63
  47.8 7.5 %collective-permute-start.14 = (bf16[128,768]{1,0:T(8,128)(2,1)S(1)}, bf16[128,768]{1,0:T(8,128)(2,1)S(1)}, u32[]{:S(2)}, u32[]{:S(2)}) collective-permute-start(bf16[128,768]{1,0:T(8,128)(2,1)S(1)} %get-tuple-element.32), channel_id=1, source_target_pairs={{0,12},{4,0},{8,4},{12,8},{1,13},{5,1},{9,5},{13,9},{2,14},{6,2},{... | collective-permute-start | bytes 589832 | tf_op jit(solution)/shard_map/ppermute | solution.py:63
  52.0 8.2 %collective-permute-start.16 = (bf16[128,768]{1,0:T(8,128)(2,1)S(1)}, bf16[128,768]{1,0:T(8,128)(2,1)S(1)}, u32[]{:S(2)}, u32[]{:S(2)}) collective-permute-start(bf16[128,768]{1,0:T(8,128)(2,1)S(1)} %get-tuple-element.43), channel_id=1, source_target_pairs={{0,4},{4,8},{8,12},{12,0},{1,5},{5,9},{9,13},{13,1},{2,6},{6,10},{... | collective-permute-start | bytes 589832 | tf_op jit(solution)/shard_map/ppermute | solution.py:63
  52.2 11.4 %collective-permute-start.17 = (bf16[128,768]{1,0:T(8,128)(2,1)S(1)}, bf16[128,768]{1,0:T(8,128)(2,1)S(1)}, u32[]{:S(2)}, u32[]{:S(2)}) collective-permute-start(bf16[128,768]{1,0:T(8,128)(2,1)S(1)} %get-tuple-element.43), channel_id=1, source_target_pairs={{0,8},{4,12},{8,0},{12,4},{1,9},{5,13},{9,1},{13,5},{2,10},{6,14},... | collective-permute-start | bytes 589832 | tf_op jit(solution)/shard_map/ppermute | solution.py:63
  54.1 10.1 %collective-permute-start.18 = (bf16[128,768]{1,0:T(8,128)(2,1)S(1)}, bf16[128,768]{1,0:T(8,128)(2,1)S(1)}, u32[]{:S(2)}, u32[]{:S(2)}) collective-permute-start(bf16[128,768]{1,0:T(8,128)(2,1)S(1)} %get-tuple-element.43), channel_id=1, source_target_pairs={{0,12},{4,0},{8,4},{12,8},{1,13},{5,1},{9,5},{13,9},{2,14},{6,2},{... | collective-permute-start | bytes 589832 | tf_op jit(solution)/shard_map/ppermute | solution.py:63
  56.5 13.5 %collective-permute-start.15 = (bf16[64,3072]{1,0:T(8,128)(2,1)S(1)}, bf16[64,3072]{1,0:T(8,128)(2,1)S(1)}, u32[]{:S(2)}, u32[]{:S(2)}) collective-permute-start(bf16[64,3072]{1,0:T(8,128)(2,1)S(1)} %get-tuple-element.42), channel_id=1, source_target_pairs={{0,64},{1,65},{2,66},{3,67},{16,208},{17,209},{18,210},{19,211},{3... | collective-permute-start | bytes 1179656 | tf_op jit(solution)/shard_map/ppermute | solution.py:46
  57.7 11.3 %collective-permute-start.19 = (bf16[32,3072]{1,0:T(8,128)(2,1)S(1)}, bf16[32,3072]{1,0:T(8,128)(2,1)S(1)}, u32[]{:S(2)}, u32[]{:S(2)}) collective-permute-start(bf16[32,3072]{1,0:T(8,128)(2,1)S(1)} %get-tuple-element.47), channel_id=1, source_target_pairs={{0,128},{1,129},{2,130},{3,131},{16,144},{17,145},{18,146},{19,147... | collective-permute-start | bytes 589832 | tf_op jit(solution)/shard_map/ppermute | solution.py:46
  65.8 11.5 %collective-permute-start.22 = (bf16[2,96,3072]{2,1,0:T(8,128)(2,1)S(1)}, bf16[2,96,3072]{2,1,0:T(8,128)(2,1)S(1)}, u32[]{:S(2)}, u32[]{:S(2)}) collective-permute-start(bf16[2,96,3072]{2,1,0:T(8,128)(2,1)S(1)} %pad_maximum_fusion), channel_id=1, source_target_pairs={{16,0},{17,1},{18,2},{19,3},{0,16},{1,17},{2,18},{3,19},{48,32},{4... | collective-permute-start | bytes 3538952 | tf_op jit(solution)/shard_map/ppermute | solution.py:46
  68.8 7.4 %collective-permute-start.23 = (bf16[2,128,384]{2,1,0:T(8,128)(2,1)S(1)}, bf16[2,128,384]{2,1,0:T(8,128)(2,1)S(1)}, u32[]{:S(2)}, u32[]{:S(2)}) collective-permute-start(bf16[2,128,384]{2,1,0:T(8,128)(2,1)S(1)} %pad_maximum_fusion.1), channel_id=1, source_target_pairs={{16,0},{17,1},{18,2},{19,3},{0,16},{1,17},{2,18},{3,19},{48,32},{4... | collective-permute-start | bytes 589832 | tf_op jit(solution)/shard_map/ppermute | solution.py:46
  68.9 13.1 %collective-permute-start.21 = (bf16[64,3072]{1,0:T(8,128)(2,1)S(1)}, bf16[64,3072]{1,0:T(8,128)(2,1)S(1)}, u32[]{:S(2)}, u32[]{:S(2)}) collective-permute-start(bf16[64,3072]{1,0:T(8,128)(2,1)S(1)} %get-tuple-element.49), channel_id=1, source_target_pairs={{0,64},{1,65},{2,66},{3,67},{16,208},{17,209},{18,210},{19,211},{3... | collective-permute-start | bytes 1179656 | tf_op jit(solution)/shard_map/ppermute | solution.py:46
  69.0 13.5 %collective-permute-start.24 = (bf16[32,3072]{1,0:T(8,128)(2,1)S(1)}, bf16[32,3072]{1,0:T(8,128)(2,1)S(1)}, u32[]{:S(2)}, u32[]{:S(2)}) collective-permute-start(bf16[32,3072]{1,0:T(8,128)(2,1)S(1)} %get-tuple-element.54), channel_id=1, source_target_pairs={{0,128},{1,129},{2,130},{3,131},{16,144},{17,145},{18,146},{19,147... | collective-permute-start | bytes 589832 | tf_op jit(solution)/shard_map/ppermute | solution.py:46
  70.0 7.2 %collective-permute-start.20 = (bf16[32,3072]{1,0:T(8,128)(2,1)S(1)}, bf16[32,3072]{1,0:T(8,128)(2,1)S(1)}, u32[]{:S(2)}, u32[]{:S(2)}) collective-permute-start(bf16[32,3072]{1,0:T(8,128)(2,1)S(1)} %slice.90), channel_id=1, source_target_pairs={{16,0},{17,1},{18,2},{19,3},{0,16},{1,17},{2,18},{3,19},{48,32},{4... | collective-permute-start | bytes 589832 | tf_op jit(solution)/shard_map/ppermute | solution.py:46
  82.0 1.5 %collective-permute-start.25 = (bf16[32,3072]{1,0:T(8,128)(2,1)S(1)}, bf16[32,3072]{1,0:T(8,128)(2,1)S(1)}, u32[]{:S(2)}, u32[]{:S(2)}) collective-permute-start(bf16[32,3072]{1,0:T(8,128)(2,1)S(1)} %slice.102), channel_id=1, source_target_pairs={{16,0},{17,1},{18,2},{19,3},{0,16},{1,17},{2,18},{3,19},{48,32},{4... | collective-permute-start | bytes 589832 | tf_op jit(solution)/shard_map/ppermute | solution.py:46
  83.7 10.9 %collective-permute-start.29 = (bf16[2,8,3072]{2,1,0:T(8,128)(2,1)S(1)}, bf16[2,8,3072]{2,1,0:T(8,128)(2,1)S(1)}, u32[]{:S(2)}, u32[]{:S(2)}) collective-permute-start(bf16[2,8,3072]{2,1,0:T(8,128)(2,1)S(1)} %get-tuple-element.62), channel_id=1, source_target_pairs={{0,33},{1,34},{2,35},{3,32},{16,50},{17,51},{18,48},{19,49},{32,2}... | collective-permute-start | bytes 294920 | tf_op jit(solution)/shard_map/ppermute | solution.py:46
  88.2 6.5 %collective-permute-start.28 = (bf16[2,8,3072]{2,1,0:T(8,128)(2,1)S(1)}, bf16[2,8,3072]{2,1,0:T(8,128)(2,1)S(1)}, u32[]{:S(2)}, u32[]{:S(2)}) collective-permute-start(bf16[2,8,3072]{2,1,0:T(8,128)(2,1)S(1)} %get-tuple-element.63), channel_id=1, source_target_pairs={{0,1},{1,2},{2,3},{3,0},{16,19},{17,16},{18,17},{19,18},{32,33},{3... | collective-permute-start | bytes 294920 | tf_op jit(solution)/shard_map/ppermute | solution.py:46
  88.2 7.5 %collective-permute-start.27 = (bf16[2,8,3072]{2,1,0:T(8,128)(2,1)S(1)}, bf16[2,8,3072]{2,1,0:T(8,128)(2,1)S(1)}, u32[]{:S(2)}, u32[]{:S(2)}) collective-permute-start(bf16[2,8,3072]{2,1,0:T(8,128)(2,1)S(1)} %get-tuple-element.61), channel_id=1, source_target_pairs={{0,32},{1,33},{2,34},{3,35},{16,51},{17,48},{18,49},{19,50},{32,1}... | collective-permute-start | bytes 294920 | tf_op jit(solution)/shard_map/ppermute | solution.py:46
  88.8 11.5 %collective-permute-start.26 = (bf16[2,8,3072]{2,1,0:T(8,128)(2,1)S(1)}, bf16[2,8,3072]{2,1,0:T(8,128)(2,1)S(1)}, u32[]{:S(2)}, u32[]{:S(2)}) collective-permute-start(bf16[2,8,3072]{2,1,0:T(8,128)(2,1)S(1)} %get-tuple-element.60), channel_id=1, source_target_pairs={{0,0},{1,1},{2,2},{3,3},{16,18},{17,19},{18,16},{19,17},{32,32},{3... | collective-permute-start | bytes 294920 | tf_op jit(solution)/shard_map/ppermute | solution.py:46
  100.4 1.3 %collective-permute-start.30 = (bf16[2,4,3072]{2,1,0:T(4,128)(2,1)S(1)}, bf16[2,4,3072]{2,1,0:T(4,128)(2,1)S(1)}, u32[]{:S(2)}, u32[]{:S(2)}) collective-permute-start(bf16[2,4,3072]{2,1,0:T(4,128)(2,1)S(1)} %slice.179), channel_id=1, source_target_pairs={{16,0},{17,1},{18,2},{19,3},{0,16},{1,17},{2,18},{3,19},{48,32},{4... | collective-permute-start | bytes 147464 | tf_op jit(solution)/shard_map/ppermute | solution.py:46
  (1 other events, 8.9 us)

commit v3 on v2

--- a/solution.py
+++ b/solution.py
@@ -90,6 +90,15 @@
 
 def t_dot(a, b):
     return lax.dot_general(a, b, (((0,), (0,)), ((), ())), preferred_element_type=F32)
+
+
+def columns_of(pieces):
+    return jnp.concatenate(pieces, axis=1)
+
+
+def split_rows(value, count):
+    rows = value.shape[0] // count
+    return [value[i * rows : (i + 1) * rows] for i in range(count)]
 
 
 def rows_of(pieces):
@@ -164,23 +173,25 @@
     width, units = w_in.shape
     mine = jnp.stack([tokens, cotangent])
     block = jnp.concatenate([mine, send(mine, OTHER_CORE)], axis=1)
-    share = jnp.concatenate([send(block, p) for p in Z_SLOTS], axis=1)
+    slots = [send(block, p) for p in Z_SLOTS]
+    w_in_other = send(after(w_in, slots[1]), OTHER_CORE)
+    w_out_other = send(after(w_out, slots[2]), OTHER_CORE)
+    share = jnp.concatenate(slots, axis=1)
     across = send(share, OTHER_CORE)
     both = jnp.concatenate([share, across], axis=1)
 
     x_pieces = gather_x(share[0], both[0])
-    w_in_other = send(after(w_in, across), OTHER_CORE)
-    w_out_other = send(after(w_out, across), OTHER_CORE)
     rows, hidden_shape = 4 * share.shape[1], (4 * share.shape[1], 2 * units)
     outgoing = [((rows // 4, width), F32), ((rows // 2, width), BF16), ((rows // 4, width), BF16)]
-    g_pieces = gather_x(share[1], both[1])
+    g_near = send(both[1], X_NEXT)
     hidden_out = [(hidden_shape, F32), (hidden_shape, BF16)]
 
     inner_part, rounded = call(
         functools.partial(inward, False), x_pieces + [w_in, w_in_other], hidden_out, FLOPS
     )
     inner_rest = exchange_rows(rounded)
-    g_pieces = [after(piece, inner_part) for piece in g_pieces]
+    g_near = after(g_near, inner_part)
+    g_pieces = [share[1], g_near, send(g_near[: share.shape[1]], X_NEXT)]
     back_part, rounded = call(
         functools.partial(inward, True), g_pieces + [w_out, w_out_other], hidden_out
     )
@@ -199,22 +210,30 @@
     backward_rest = send(near, inverse(X_NEXT)), send(far, inverse(X_FAR))
     forward = finish_x(forward, [after(piece, backward) for piece in forward_rest])
 
-    x_own, g_own = rows_of(x_pieces), rows_of(g_pieces)
-    rest = after(jnp.stack([x_own[32:], g_own[32:]]), backward)
-    rest = send(rest, OTHER_CORE)
-    hidden = jnp.stack([activated[:, :units], grad_pre[:, :units]])
-    hidden_rest = send(jnp.stack([activated[:, units:], grad_pre[:, units:]]), OTHER_CORE)
-    x_whole = rows_of([x_own, across[0], rest[0]])
-    g_whole = rows_of([g_own, across[1], rest[1]])
-    w_out_grad = t_dot(rows_of([hidden[0], hidden_rest[0]]), g_whole).astype(BF16)
-    w_in_grad = t_dot(x_whole, rows_of([hidden[1], hidden_rest[1]])).astype(BF16)
+    x_rest, g_rest = (rows_of(pieces[1:]) for pieces in (x_pieces, g_pieces))
+    rest = [
+        rows_of([kept, columns_of(split_rows(hidden[:, units:], 8))])
+        for kept, hidden in ((x_rest, grad_pre), (g_rest, activated))
+    ]
+    rest = send(jnp.stack(rest), OTHER_CORE)
+    kept = x_rest.shape[0]
+
+    def with_other(share, mine, across, hidden, other):
+        hidden_other = rows_of([other[kept:, i * units : (i + 1) * units] for i in range(8)])
+        return rows_of([share, mine, across, other[:kept]]), rows_of([hidden[:, :units], hidden_other])
+
+    x_whole, pre_whole = with_other(share[0], x_rest, across[0], grad_pre, rest[0])
+    g_whole, act_whole = with_other(share[1], g_rest, across[1], activated, rest[1])
+    w_out_grad = t_dot(act_whole, g_whole).astype(BF16)
+    w_in_grad = t_dot(x_whole, pre_whole).astype(BF16)
 
     backward_rest = [after(piece, w_in_grad, w_out_grad, forward) for piece in backward_rest]
     backward = finish_x(backward, backward_rest)
     result = jnp.stack([forward, backward])
     summed = jnp.zeros((2, 8, width), F32)
-    for i, perm in enumerate(Z_SLOTS):
-        summed = summed + send(result[:, 8 * i : 8 * i + 8], inverse(perm)).astype(F32)
+    for i in (1, 2, 3, 0):
+        piece = send(result[:, 8 * i : 8 * i + 8], inverse(Z_SLOTS[i]))
+        summed = summed + piece.astype(F32)
     summed = summed[:, :4] + send(summed[:, 4:].astype(BF16), OTHER_CORE).astype(F32)
     layer_output, input_grad = summed[0].astype(BF16), summed[1].astype(BF16)
     return (layer_output, input_grad, w_in_grad, w_out_grad)

time: 103 us -> 96.9 us (0.941)
  starting transfers between devices: 53.9 us -> 44.8 us
  waiting for transfers between devices: 34.4 us -> 37.1 us
    ppermute x25 -> x24, starting transfers between devices: 44.1 us -> 37.5 us  [send(): return lax.ppermute(value, PLANE, perm)]
    ppermute x6, starting transfers between devices: 9.74 us -> 7.36 us  [exchange_rows(): return [lax.ppermute(rounded, 'row', shift) for shift in ROW_SHIFTS]]
    ppermute x25 -> x24, waiting for transfers between devices: 29.8 us -> 31.9 us  [send(): return lax.ppermute(value, PLANE, perm)]
  transfers between devices with their start and end apart: 31 -> 30, of which waited for: 15 -> 12; matrix products, arithmetic and copies ran while one was open for 5% -> 6% of each run, Pallas kernels for 5% -> 5%
where the time goes in v3:
time: 96.9 us; the launch traced here: 96.5 us
  starting transfers between devices  44.8 us (46%)
  waiting for transfers between devices  37.1 us (38%)
  Pallas kernels  5.23 us (5%)
  matrix products  4.63 us (5%)
  other arithmetic  2.1 us (2%)
  local copies, waits for them, and re-layouts  1.49 us (2%)
  between operations  1.09 us (1%)
    ppermute x24, starting transfers between devices, send(): return lax.ppermute(value, PLANE, perm)  37.5 us
    ppermute x24, waiting for transfers between devices, send(): return lax.ppermute(value, PLANE, perm)  31.9 us
    ppermute x6, starting transfers between devices, exchange_rows(): return [lax.ppermute(rounded, 'row', shift) for shift in ROW_SHIFTS]  7.36 us
    pallas_call x4, Pallas kernels, call(): pl.pallas_call(body, out_shape=[jax.ShapeDtypeStruct(shape, dtype) for sh...  5.23 us
    ppermute x6, waiting for transfers between devices, exchange_rows(): return [lax.ppermute(rounded, 'row', shift) for shift in ROW_SHIFTS]  5.21 us
    dot_general x2, matrix products, t_dot(): lax.dot_general(a, b, (((0,), (0,)), ((), ())), preferred_element_type=F32)  4.63 us
  transfers between devices with their start and end apart: 30, of which 12 were waited for; matrix products, arithmetic and copies ran while one was open for 6% of the time, Pallas kernels for 5%

profile of v3, /device:TPU:1, one launch (start us, length us, event | category | flops | bytes accessed | tf_op | source)
XLA Modules:
  0.0 96.5 jit_solution(13620981518278532382)
XLA Ops:
  1.4 3.3 %collective-permute-start = (bf16[2,4,3072]{2,1,0:T(4,128)(2,1)S(1)}, bf16[2,4,3072]{2,1,0:T(4,128)(2,1)S(1)}, u32[]{:S(2)}, u32[]{:S(2)}) collective-permute-start(bf16[2,4,3072]{2,1,0:T(4,128)(2,1)S(1)} %pad_maximum_fusion.3), channel_id=1, source_target_pairs={{16,0},{17,1},{18,2},{19,3},{0,16},{1,17},{2,18},{3,19},{48,32},{4... | collective-permute-start | bytes 147464 | tf_op jit(solution)/shard_map/ppermute | solution.py:46
  6.4 7.1 %collective-permute-start.1 = (bf16[2,8,3072]{2,1,0:T(8,128)(2,1)S(1)}, bf16[2,8,3072]{2,1,0:T(8,128)(2,1)S(1)}, u32[]{:S(2)}, u32[]{:S(2)}) collective-permute-start(bf16[2,8,3072]{2,1,0:T(8,128)(2,1)S(1)} %pad_maximum_fusion.2), channel_id=1, source_target_pairs={{0,0},{1,1},{2,2},{3,3},{18,16},{19,17},{16,18},{17,19},{32,32},{3... | collective-permute-start | bytes 294920 | tf_op jit(solution)/shard_map/ppermute | solution.py:46
  13.5 1.7 %collective-permute-start.4 = (bf16[2,8,3072]{2,1,0:T(8,128)(2,1)S(1)}, bf16[2,8,3072]{2,1,0:T(8,128)(2,1)S(1)}, u32[]{:S(2)}, u32[]{:S(2)}) collective-permute-start(bf16[2,8,3072]{2,1,0:T(8,128)(2,1)S(1)} %pad_maximum_fusion.2), channel_id=1, source_target_pairs={{33,0},{34,1},{35,2},{32,3},{50,16},{51,17},{48,18},{49,19},{2,32}... | collective-permute-start | bytes 294920 | tf_op jit(solution)/shard_map/ppermute | solution.py:46
  15.8 8.6 %collective-permute-done.2 = bf16[2,8,3072]{2,1,0:T(8,128)(2,1)S(1)} collective-permute-done((bf16[2,8,3072]{2,1,0:T(8,128)(2,1)S(1)}, bf16[2,8,3072]{2,1,0:T(8,128)(2,1)S(1)}, u32[]{:S(2)}, u32[]{:S(2)}) %collective-permute-start.2) | collective-permute-done | bytes 98336 | tf_op jit(solution)/shard_map/ppermute | solution.py:46
  24.7 2.8 %collective-permute-start.7 = (bf16[32,3072]{1,0:T(8,128)(2,1)S(1)}, bf16[32,3072]{1,0:T(8,128)(2,1)S(1)}, u32[]{:S(2)}, u32[]{:S(2)}) collective-permute-start(bf16[32,3072]{1,0:T(8,128)(2,1)S(1)} %get-tuple-element.64.own), channel_id=1, source_target_pairs={{128,0},{129,1},{130,2},{131,3},{144,16},{145,17},{146,18},{147,19... | collective-permute-start | bytes 589832 | tf_op jit(solution)/shard_map/ppermute | solution.py:46
  29.1 8.1 %collective-permute-done.6.near = bf16[64,3072]{1,0:T(8,128)(2,1)S(1)} collective-permute-done((bf16[64,3072]{1,0:T(8,128)(2,1)S(1)}, bf16[64,3072]{1,0:T(8,128)(2,1)S(1)}, u32[]{:S(2)}, u32[]{:S(2)}) %collective-permute-start.6) | collective-permute-done | bytes 393248 | tf_op jit(solution)/shard_map/ppermute | solution.py:46
  37.3 1.0 %shard_map.75 = (f32[128,768]{1,0:T(8,128)S(1)}, bf16[128,768]{1,0:T(8,128)(2,1)S(1)}) custom-call(bf16[32,3072]{1,0:T(8,128)(2,1)S(1)} %get-tuple-element.64.own, bf16[64,3072]{1,0:T(8,128)(2,1)S(1)} %collective-permute-done.6.near, bf16[32,3072]{1,0:T(8,128)(2,1)S(1)} %collective-permute-done.7.far, bf16[3072,384]{1,0:T(8,128)(2,1)S(1)} %copy-done.1, ...), custom_call_target="tpu_custom_call" | custom-call | flops 4000000000 | tf_op jit(solution)/shard_map/pallas_call | solution.py:162
  38.3 2.8 %collective-permute-start.14 = (bf16[128,768]{1,0:T(8,128)(2,1)S(1)}, bf16[128,768]{1,0:T(8,128)(2,1)S(1)}, u32[]{:S(2)}, u32[]{:S(2)}) collective-permute-start(bf16[128,768]{1,0:T(8,128)(2,1)S(1)} %get-tuple-element.29), channel_id=1, source_target_pairs={{0,12},{4,0},{8,4},{12,8},{1,13},{5,1},{9,5},{13,9},{2,14},{6,2},{... | collective-permute-start | bytes 589832 | tf_op jit(solution)/shard_map/ppermute | solution.py:63
  42.1 1.6 %collective-permute-start.11 = (bf16[32,3072]{1,0:T(8,128)(2,1)S(1)}, bf16[32,3072]{1,0:T(8,128)(2,1)S(1)}, u32[]{:S(2)}, u32[]{:S(2)}) collective-permute-start(bf16[32,3072]{1,0:T(8,128)(2,1)S(1)} %slice.206), channel_id=1, source_target_pairs={{64,0},{65,1},{66,2},{67,3},{208,16},{209,17},{210,18},{211,19},{9... | collective-permute-start | bytes 589832 | tf_op jit(solution)/shard_map/ppermute | solution.py:46
  43.8 4.5 %collective-permute-done.11.far = bf16[32,3072]{1,0:T(8,128)(2,1)S(1)} collective-permute-done((bf16[32,3072]{1,0:T(8,128)(2,1)S(1)}, bf16[32,3072]{1,0:T(8,128)(2,1)S(1)}, u32[]{:S(2)}, u32[]{:S(2)}) %collective-permute-start.11) | collective-permute-done | bytes 196640 | tf_op jit(solution)/shard_map/ppermute | solution.py:46
  48.3 1.4 %shard_map.76 = (f32[128,768]{1,0:T(8,128)S(1)}, bf16[128,768]{1,0:T(8,128)(2,1)S(1)}) custom-call(bf16[32,3072]{1,0:T(8,128)(2,1)S(1)} %get-tuple-element.65.own, bf16[64,3072]{1,0:T(8,128)(2,1)S(1)} %collective-permute-done.10.near, bf16[32,3072]{1,0:T(8,128)(2,1)S(1)} %collective-permute-done.11.far, bf16[384,3072]{1,0:T(8,128)(2,1)S(1)} %copy-done, ...), custom_call_target="tpu_custom_call" | custom-call | tf_op jit(solution)/shard_map/pallas_call | solution.py:162
  49.7 2.3 %collective-permute-start.18 = (bf16[128,768]{1,0:T(8,128)(2,1)S(1)}, bf16[128,768]{1,0:T(8,128)(2,1)S(1)}, u32[]{:S(2)}, u32[]{:S(2)}) collective-permute-start(bf16[128,768]{1,0:T(8,128)(2,1)S(1)} %get-tuple-element.38), channel_id=1, source_target_pairs={{0,12},{4,0},{8,4},{12,8},{1,13},{5,1},{9,5},{13,9},{2,14},{6,2},{... | collective-permute-start | bytes 589832 | tf_op jit(solution)/shard_map/ppermute | solution.py:63
  52.0 1.2 %collective-permute-start.17 = (bf16[128,768]{1,0:T(8,128)(2,1)S(1)}, bf16[128,768]{1,0:T(8,128)(2,1)S(1)}, u32[]{:S(2)}, u32[]{:S(2)}) collective-permute-start(bf16[128,768]{1,0:T(8,128)(2,1)S(1)} %get-tuple-element.38), channel_id=1, source_target_pairs={{0,8},{4,12},{8,0},{12,4},{1,9},{5,13},{9,1},{13,5},{2,10},{6,14},... | collective-permute-start | bytes 589832 | tf_op jit(solution)/shard_map/ppermute | solution.py:63
  53.6 1.2 %shard_map.77 = (bf16[128,768]{1,0:T(8,128)(2,1)S(1)}, f32[128,768]{1,0:T(8,128)S(1)}, f32[32,3072]{1,0:T(8,128)S(1)}, bf16[64,3072]{1,0:T(8,128)(2,1)S(1)}, bf16[32,3072]{1,0:T(8,128)(2,1)S(1)}) custom-call(f32[128,768]{1,0:T(8,128)S(1)} %get-tuple-element.28.part, bf16[128,768]{1,0:T(8,128)(2,1)S(1)} %collective-permute-done.9.r0, ...), custom_call_target="tpu_custom_call" | custom-call | tf_op jit(solution)/shard_map/pallas_call | solution.py:162
  54.9 3.1 %collective-permute-start.19 = (bf16[32,3072]{1,0:T(8,128)(2,1)S(1)}, bf16[32,3072]{1,0:T(8,128)(2,1)S(1)}, u32[]{:S(2)}, u32[]{:S(2)}) collective-permute-start(bf16[32,3072]{1,0:T(8,128)(2,1)S(1)} %get-tuple-element.42), channel_id=1, source_target_pairs={{0,128},{1,129},{2,130},{3,131},{16,144},{17,145},{18,146},{19,147... | collective-permute-start | bytes 589832 | tf_op jit(solution)/shard_map/ppermute | solution.py:46
  59.0 4.8 %collective-permute-done.16.r0 = bf16[128,768]{1,0:T(8,128)(2,1)S(1)} collective-permute-done((bf16[128,768]{1,0:T(8,128)(2,1)S(1)}, bf16[128,768]{1,0:T(8,128)(2,1)S(1)}, u32[]{:S(2)}, u32[]{:S(2)}) %collective-permute-start.16) | collective-permute-done | bytes 196640 | tf_op jit(solution)/shard_map/ppermute | solution.py:63
  63.8 1.6 %shard_map.78 = (bf16[128,768]{1,0:T(8,128)(2,1)S(1)}, f32[32,3072]{1,0:T(8,128)S(1)}, bf16[64,3072]{1,0:T(8,128)(2,1)S(1)}, bf16[32,3072]{1,0:T(8,128)(2,1)S(1)}) custom-call(f32[128,768]{1,0:T(8,128)S(1)} %get-tuple-element.32.part, bf16[128,768]{1,0:T(8,128)(2,1)S(1)} %collective-permute-done.16.r0, bf16[128,768]{1,0:T(8,128)(2,1)S(1)} %collective-permute-done.17.r1, ...), custom_call_target="tpu_custom_call" | custom-call | tf_op jit(solution)/shard_map/pallas_call | solution.py:162
  65.7 1.3 %collective-permute-start.22 = (bf16[2,112,3072]{2,1,0:T(8,128)(2,1)S(1)}, bf16[2,112,3072]{2,1,0:T(8,128)(2,1)S(1)}, u32[]{:S(2)}, u32[]{:S(2)}) collective-permute-start(bf16[2,112,3072]{2,1,0:T(8,128)(2,1)S(1)} %pad_maximum_fusion), channel_id=1, source_target_pairs={{16,0},{17,1},{18,2},{19,3},{0,16},{1,17},{2,18},{3,19},{48,32},{4... | collective-permute-start | bytes 4128776 | tf_op jit(solution)/shard_map/ppermute | solution.py:46
  67.0 1.8 %collective-permute-start.23 = (bf16[32,3072]{1,0:T(8,128)(2,1)S(1)}, bf16[32,3072]{1,0:T(8,128)(2,1)S(1)}, u32[]{:S(2)}, u32[]{:S(2)}) collective-permute-start(bf16[32,3072]{1,0:T(8,128)(2,1)S(1)} %get-tuple-element.48), channel_id=1, source_target_pairs={{0,128},{1,129},{2,130},{3,131},{16,144},{17,145},{18,146},{19,147... | collective-permute-start | bytes 589832 | tf_op jit(solution)/shard_map/ppermute | solution.py:46
  68.9 0.9 collective-permute-start.21
  69.8 0.9 collective-permute-start.20
  70.8 1.1 %collective-permute-done.20 = bf16[32,3072]{1,0:T(8,128)(2,1)S(1)} collective-permute-done((bf16[32,3072]{1,0:T(8,128)(2,1)S(1)}, bf16[32,3072]{1,0:T(8,128)(2,1)S(1)}, u32[]{:S(2)}, u32[]{:S(2)}) %collective-permute-start.20) | collective-permute-done | bytes 196640 | tf_op jit(solution)/shard_map/ppermute | solution.py:46
  72.3 2.2 %convolution_convert_fusion = bf16[384,3072]{1,0:T(8,128)(2,1)} fusion(bf16[256,384]{1,0:T(8,128)(2,1)S(1)} %get-tuple-element.77, bf16[256,3072]{1,0:T(8,128)(2,1)S(1)} %get-tuple-element.50), kind=kOutput, calls=%fused_computation | convolution fusion | flops 605159424 | bytes 4128768 | tf_op jit(solution)/shard_map/dot_general | solution.py:92
  74.5 2.4 %convolution_convert_fusion.1 = bf16[3072,384]{1,0:T(8,128)(2,1)} fusion(bf16[256,3072]{1,0:T(8,128)(2,1)S(1)} %get-tuple-element.51, bf16[256,384]{1,0:T(8,128)(2,1)S(1)} %get-tuple-element.76), kind=kOutput, calls=%fused_computation.1 | convolution fusion | flops 605159424 | bytes 4128768 | tf_op jit(solution)/shard_map/dot_general | solution.py:92
  76.9 1.7 %collective-permute-done.21 = bf16[64,3072]{1,0:T(8,128)(2,1)S(1)} collective-permute-done((bf16[64,3072]{1,0:T(8,128)(2,1)S(1)}, bf16[64,3072]{1,0:T(8,128)(2,1)S(1)}, u32[]{:S(2)}, u32[]{:S(2)}) %collective-permute-start.21) | collective-permute-done | bytes 393248 | tf_op jit(solution)/shard_map/ppermute | solution.py:46
  78.7 1.6 %collective-permute-start.24 = (bf16[32,3072]{1,0:T(8,128)(2,1)S(1)}, bf16[32,3072]{1,0:T(8,128)(2,1)S(1)}, u32[]{:S(2)}, u32[]{:S(2)}) collective-permute-start(bf16[32,3072]{1,0:T(8,128)(2,1)S(1)} %slice.252), channel_id=1, source_target_pairs={{16,0},{17,1},{18,2},{19,3},{0,16},{1,17},{2,18},{3,19},{48,32},{4... | collective-permute-start | bytes 589832 | tf_op jit(solution)/shard_map/ppermute | solution.py:46
  80.3 1.1 %collective-permute-done.24 = bf16[32,3072]{1,0:T(8,128)(2,1)S(1)} collective-permute-done((bf16[32,3072]{1,0:T(8,128)(2,1)S(1)}, bf16[32,3072]{1,0:T(8,128)(2,1)S(1)}, u32[]{:S(2)}, u32[]{:S(2)}) %collective-permute-start.24) | collective-permute-done | bytes 196640 | tf_op jit(solution)/shard_map/ppermute | solution.py:46
  81.5 1.0 %collective-permute-start.25 = (bf16[2,8,3072]{2,1,0:T(8,128)(2,1)S(1)}, bf16[2,8,3072]{2,1,0:T(8,128)(2,1)S(1)}, u32[]{:S(2)}, u32[]{:S(2)}) collective-permute-start(bf16[2,8,3072]{2,1,0:T(8,128)(2,1)S(1)} %get-tuple-element.56), channel_id=1, source_target_pairs={{0,32},{1,33},{2,34},{3,35},{16,51},{17,48},{18,49},{19,50},{32,1}... | collective-permute-start | bytes 294920 | tf_op jit(solution)/shard_map/ppermute | solution.py:46
  83.4 4.6 %collective-permute-start.28 = (bf16[2,8,3072]{2,1,0:T(8,128)(2,1)S(1)}, bf16[2,8,3072]{2,1,0:T(8,128)(2,1)S(1)}, u32[]{:S(2)}, u32[]{:S(2)}) collective-permute-start(bf16[2,8,3072]{2,1,0:T(8,128)(2,1)S(1)} %get-tuple-element.58), channel_id=1, source_target_pairs={{0,0},{1,1},{2,2},{3,3},{16,18},{17,19},{18,16},{19,17},{32,32},{3... | collective-permute-start | bytes 294920 | tf_op jit(solution)/shard_map/ppermute | solution.py:46
  88.0 1.9 %collective-permute-start.27 = (bf16[2,8,3072]{2,1,0:T(8,128)(2,1)S(1)}, bf16[2,8,3072]{2,1,0:T(8,128)(2,1)S(1)}, u32[]{:S(2)}, u32[]{:S(2)}) collective-permute-start(bf16[2,8,3072]{2,1,0:T(8,128)(2,1)S(1)} %get-tuple-element.59), channel_id=1, source_target_pairs={{0,33},{1,34},{2,35},{3,32},{16,50},{17,51},{18,48},{19,49},{32,2}... | collective-permute-start | bytes 294920 | tf_op jit(solution)/shard_map/ppermute | solution.py:46
  89.9 4.5 %collective-permute-done.28 = bf16[2,8,3072]{2,1,0:T(8,128)(2,1)S(1)} collective-permute-done((bf16[2,8,3072]{2,1,0:T(8,128)(2,1)S(1)}, bf16[2,8,3072]{2,1,0:T(8,128)(2,1)S(1)}, u32[]{:S(2)}, u32[]{:S(2)}) %collective-permute-start.28) | collective-permute-done | bytes 98336 | tf_op jit(solution)/shard_map/ppermute | solution.py:46
  94.6 1.2 %collective-permute-done.29 = bf16[2,4,3072]{2,1,0:T(4,128)(2,1)S(1)} collective-permute-done((bf16[2,4,3072]{2,1,0:T(4,128)(2,1)S(1)}, bf16[2,4,3072]{2,1,0:T(4,128)(2,1)S(1)}, u32[]{:S(2)}, u32[]{:S(2)}) %collective-permute-start.29) | collective-permute-done | bytes 49184 | tf_op jit(solution)/shard_map/ppermute | solution.py:46
  (101 shorter events, 9.9 us)
Async XLA Ops:
  1.4 4.2 %collective-permute-start = (bf16[2,4,3072]{2,1,0:T(4,128)(2,1)S(1)}, bf16[2,4,3072]{2,1,0:T(4,128)(2,1)S(1)}, u32[]{:S(2)}, u32[]{:S(2)}) collective-permute-start(bf16[2,4,3072]{2,1,0:T(4,128)(2,1)S(1)} %pad_maximum_fusion.3), channel_id=1, source_target_pairs={{16,0},{17,1},{18,2},{19,3},{0,16},{1,17},{2,18},{3,19},{48,32},{4... | collective-permute-start | bytes 147464 | tf_op jit(solution)/shard_map/ppermute | solution.py:46
  6.4 9.4 %collective-permute-start.1 = (bf16[2,8,3072]{2,1,0:T(8,128)(2,1)S(1)}, bf16[2,8,3072]{2,1,0:T(8,128)(2,1)S(1)}, u32[]{:S(2)}, u32[]{:S(2)}) collective-permute-start(bf16[2,8,3072]{2,1,0:T(8,128)(2,1)S(1)} %pad_maximum_fusion.2), channel_id=1, source_target_pairs={{0,0},{1,1},{2,2},{3,3},{18,16},{19,17},{16,18},{17,19},{32,32},{3... | collective-permute-start | bytes 294920 | tf_op jit(solution)/shard_map/ppermute | solution.py:46
  13.5 11.0 %collective-permute-start.4 = (bf16[2,8,3072]{2,1,0:T(8,128)(2,1)S(1)}, bf16[2,8,3072]{2,1,0:T(8,128)(2,1)S(1)}, u32[]{:S(2)}, u32[]{:S(2)}) collective-permute-start(bf16[2,8,3072]{2,1,0:T(8,128)(2,1)S(1)} %pad_maximum_fusion.2), channel_id=1, source_target_pairs={{33,0},{34,1},{35,2},{32,3},{50,16},{51,17},{48,18},{49,19},{2,32}... | collective-permute-start | bytes 294920 | tf_op jit(solution)/shard_map/ppermute | solution.py:46
  15.3 9.2 %collective-permute-start.3 = (bf16[2,8,3072]{2,1,0:T(8,128)(2,1)S(1)}, bf16[2,8,3072]{2,1,0:T(8,128)(2,1)S(1)}, u32[]{:S(2)}, u32[]{:S(2)}) collective-permute-start(bf16[2,8,3072]{2,1,0:T(8,128)(2,1)S(1)} %pad_maximum_fusion.2), channel_id=1, source_target_pairs={{1,0},{2,1},{3,2},{0,3},{19,16},{16,17},{17,18},{18,19},{33,32},{3... | collective-permute-start | bytes 294920 | tf_op jit(solution)/shard_map/ppermute | solution.py:46
  15.3 9.2 %collective-permute-start.2 = (bf16[2,8,3072]{2,1,0:T(8,128)(2,1)S(1)}, bf16[2,8,3072]{2,1,0:T(8,128)(2,1)S(1)}, u32[]{:S(2)}, u32[]{:S(2)}) collective-permute-start(bf16[2,8,3072]{2,1,0:T(8,128)(2,1)S(1)} %pad_maximum_fusion.2), channel_id=1, source_target_pairs={{32,0},{33,1},{34,2},{35,3},{51,16},{48,17},{49,18},{50,19},{1,32}... | collective-permute-start | bytes 294920 | tf_op jit(solution)/shard_map/ppermute | solution.py:46
  24.6 3.7 %collective-permute-start.5 = (bf16[2,32,3072]{2,1,0:T(8,128)(2,1)S(1)}, bf16[2,32,3072]{2,1,0:T(8,128)(2,1)S(1)}, u32[]{:S(2)}, u32[]{:S(2)}) collective-permute-start(bf16[2,32,3072]{2,1,0:T(8,128)(2,1)S(1)} %get-tuple-element.67), channel_id=1, source_target_pairs={{16,0},{17,1},{18,2},{19,3},{0,16},{1,17},{2,18},{3,19},{48,32},{4... | collective-permute-start | bytes 1179656 | tf_op jit(solution)/shard_map/ppermute | solution.py:46
  24.7 12.5 %collective-permute-start.7 = (bf16[32,3072]{1,0:T(8,128)(2,1)S(1)}, bf16[32,3072]{1,0:T(8,128)(2,1)S(1)}, u32[]{:S(2)}, u32[]{:S(2)}) collective-permute-start(bf16[32,3072]{1,0:T(8,128)(2,1)S(1)} %get-tuple-element.64.own), channel_id=1, source_target_pairs={{128,0},{129,1},{130,2},{131,3},{144,16},{145,17},{146,18},{147,19... | collective-permute-start | bytes 589832 | tf_op jit(solution)/shard_map/ppermute | solution.py:46
  27.5 9.7 %collective-permute-start.8 = (bf16[3072,384]{1,0:T(8,128)(2,1)}, bf16[3072,384]{1,0:T(8,128)(2,1)S(1)}, u32[]{:S(2)}, u32[]{:S(2)}) collective-permute-start(bf16[3072,384]{1,0:T(8,128)(2,1)} %w_a.7), channel_id=1, source_target_pairs={{16,0},{17,1},{18,2},{19,3},{0,16},{1,17},{2,18},{3,19},{48,32},{4... | collective-permute-start | bytes 7077896 | tf_op jit(solution)/shard_map/ppermute | solution.py:46
  28.3 15.5 %collective-permute-start.12 = (bf16[384,3072]{1,0:T(8,128)(2,1)}, bf16[384,3072]{1,0:T(8,128)(2,1)S(1)}, u32[]{:S(2)}, u32[]{:S(2)}) collective-permute-start(bf16[384,3072]{1,0:T(8,128)(2,1)} %w_a.6), channel_id=1, source_target_pairs={{16,0},{17,1},{18,2},{19,3},{0,16},{1,17},{2,18},{3,19},{48,32},{4... | collective-permute-start | bytes 7077896 | tf_op jit(solution)/shard_map/ppermute | solution.py:46
  28.3 8.9 %copy-start.1 = (bf16[3072,384]{1,0:T(8,128)(2,1)S(1)}, bf16[3072,384]{1,0:T(8,128)(2,1)}, u32[]{:S(2)}) copy-start(bf16[3072,384]{1,0:T(8,128)(2,1)} %w_a.7) | copy-start | bytes 7077892
  28.4 8.8 %collective-permute-start.6 = (bf16[64,3072]{1,0:T(8,128)(2,1)S(1)}, bf16[64,3072]{1,0:T(8,128)(2,1)S(1)}, u32[]{:S(2)}, u32[]{:S(2)}) collective-permute-start(bf16[64,3072]{1,0:T(8,128)(2,1)S(1)} %get-tuple-element.54), channel_id=1, source_target_pairs={{64,0},{65,1},{66,2},{67,3},{208,16},{209,17},{210,18},{211,19},{9... | collective-permute-start | bytes 1179656 | tf_op jit(solution)/shard_map/ppermute | solution.py:46
  28.8 13.3 %collective-permute-start.10 = (bf16[64,3072]{1,0:T(8,128)(2,1)S(1)}, bf16[64,3072]{1,0:T(8,128)(2,1)S(1)}, u32[]{:S(2)}, u32[]{:S(2)}) collective-permute-start(bf16[64,3072]{1,0:T(8,128)(2,1)S(1)} %get-tuple-element.55), channel_id=1, source_target_pairs={{64,0},{65,1},{66,2},{67,3},{208,16},{209,17},{210,18},{211,19},{9... | collective-permute-start | bytes 1179656 | tf_op jit(solution)/shard_map/ppermute | solution.py:46
  37.3 11.0 %copy-start = (bf16[384,3072]{1,0:T(8,128)(2,1)S(1)}, bf16[384,3072]{1,0:T(8,128)(2,1)}, u32[]{:S(2)}) copy-start(bf16[384,3072]{1,0:T(8,128)(2,1)} %w_a.6) | copy-start | bytes 7077892
  38.3 14.9 %collective-permute-start.14 = (bf16[128,768]{1,0:T(8,128)(2,1)S(1)}, bf16[128,768]{1,0:T(8,128)(2,1)S(1)}, u32[]{:S(2)}, u32[]{:S(2)}) collective-permute-start(bf16[128,768]{1,0:T(8,128)(2,1)S(1)} %get-tuple-element.29), channel_id=1, source_target_pairs={{0,12},{4,0},{8,4},{12,8},{1,13},{5,1},{9,5},{13,9},{2,14},{6,2},{... | collective-permute-start | bytes 589832 | tf_op jit(solution)/shard_map/ppermute | solution.py:63
  41.1 12.1 %collective-permute-start.13 = (bf16[128,768]{1,0:T(8,128)(2,1)S(1)}, bf16[128,768]{1,0:T(8,128)(2,1)S(1)}, u32[]{:S(2)}, u32[]{:S(2)}) collective-permute-start(bf16[128,768]{1,0:T(8,128)(2,1)S(1)} %get-tuple-element.29), channel_id=1, source_target_pairs={{0,8},{4,12},{8,0},{12,4},{1,9},{5,13},{9,1},{13,5},{2,10},{6,14},... | collective-permute-start | bytes 589832 | tf_op jit(solution)/shard_map/ppermute | solution.py:63
  41.4 12.2 %collective-permute-start.9 = (bf16[128,768]{1,0:T(8,128)(2,1)S(1)}, bf16[128,768]{1,0:T(8,128)(2,1)S(1)}, u32[]{:S(2)}, u32[]{:S(2)}) collective-permute-start(bf16[128,768]{1,0:T(8,128)(2,1)S(1)} %get-tuple-element.29), channel_id=1, source_target_pairs={{0,4},{4,8},{8,12},{12,0},{1,5},{5,9},{9,13},{13,1},{2,6},{6,10},{... | collective-permute-start | bytes 589832 | tf_op jit(solution)/shard_map/ppermute | solution.py:63
  42.1 6.1 %collective-permute-start.11 = (bf16[32,3072]{1,0:T(8,128)(2,1)S(1)}, bf16[32,3072]{1,0:T(8,128)(2,1)S(1)}, u32[]{:S(2)}, u32[]{:S(2)}) collective-permute-start(bf16[32,3072]{1,0:T(8,128)(2,1)S(1)} %slice.206), channel_id=1, source_target_pairs={{64,0},{65,1},{66,2},{67,3},{208,16},{209,17},{210,18},{211,19},{9... | collective-permute-start | bytes 589832 | tf_op jit(solution)/shard_map/ppermute | solution.py:46
  49.7 9.3 %collective-permute-start.18 = (bf16[128,768]{1,0:T(8,128)(2,1)S(1)}, bf16[128,768]{1,0:T(8,128)(2,1)S(1)}, u32[]{:S(2)}, u32[]{:S(2)}) collective-permute-start(bf16[128,768]{1,0:T(8,128)(2,1)S(1)} %get-tuple-element.38), channel_id=1, source_target_pairs={{0,12},{4,0},{8,4},{12,8},{1,13},{5,1},{9,5},{13,9},{2,14},{6,2},{... | collective-permute-start | bytes 589832 | tf_op jit(solution)/shard_map/ppermute | solution.py:63
  52.0 7.0 %collective-permute-start.17 = (bf16[128,768]{1,0:T(8,128)(2,1)S(1)}, bf16[128,768]{1,0:T(8,128)(2,1)S(1)}, u32[]{:S(2)}, u32[]{:S(2)}) collective-permute-start(bf16[128,768]{1,0:T(8,128)(2,1)S(1)} %get-tuple-element.38), channel_id=1, source_target_pairs={{0,8},{4,12},{8,0},{12,4},{1,9},{5,13},{9,1},{13,5},{2,10},{6,14},... | collective-permute-start | bytes 589832 | tf_op jit(solution)/shard_map/ppermute | solution.py:63
  53.2 10.6 %collective-permute-start.16 = (bf16[128,768]{1,0:T(8,128)(2,1)S(1)}, bf16[128,768]{1,0:T(8,128)(2,1)S(1)}, u32[]{:S(2)}, u32[]{:S(2)}) collective-permute-start(bf16[128,768]{1,0:T(8,128)(2,1)S(1)} %get-tuple-element.38), channel_id=1, source_target_pairs={{0,4},{4,8},{8,12},{12,0},{1,5},{5,9},{9,13},{13,1},{2,6},{6,10},{... | collective-permute-start | bytes 589832 | tf_op jit(solution)/shard_map/ppermute | solution.py:63
  54.9 12.1 %collective-permute-start.19 = (bf16[32,3072]{1,0:T(8,128)(2,1)S(1)}, bf16[32,3072]{1,0:T(8,128)(2,1)S(1)}, u32[]{:S(2)}, u32[]{:S(2)}) collective-permute-start(bf16[32,3072]{1,0:T(8,128)(2,1)S(1)} %get-tuple-element.42), channel_id=1, source_target_pairs={{0,128},{1,129},{2,130},{3,131},{16,144},{17,145},{18,146},{19,147... | collective-permute-start | bytes 589832 | tf_op jit(solution)/shard_map/ppermute | solution.py:46
  58.1 11.7 %collective-permute-start.15 = (bf16[64,3072]{1,0:T(8,128)(2,1)S(1)}, bf16[64,3072]{1,0:T(8,128)(2,1)S(1)}, u32[]{:S(2)}, u32[]{:S(2)}) collective-permute-start(bf16[64,3072]{1,0:T(8,128)(2,1)S(1)} %get-tuple-element.37), channel_id=1, source_target_pairs={{0,64},{1,65},{2,66},{3,67},{16,208},{17,209},{18,210},{19,211},{3... | collective-permute-start | bytes 1179656 | tf_op jit(solution)/shard_map/ppermute | solution.py:46
  65.7 6.2 %collective-permute-start.22 = (bf16[2,112,3072]{2,1,0:T(8,128)(2,1)S(1)}, bf16[2,112,3072]{2,1,0:T(8,128)(2,1)S(1)}, u32[]{:S(2)}, u32[]{:S(2)}) collective-permute-start(bf16[2,112,3072]{2,1,0:T(8,128)(2,1)S(1)} %pad_maximum_fusion), channel_id=1, source_target_pairs={{16,0},{17,1},{18,2},{19,3},{0,16},{1,17},{2,18},{3,19},{48,32},{4... | collective-permute-start | bytes 4128776 | tf_op jit(solution)/shard_map/ppermute | solution.py:46
  67.0 13.2 %collective-permute-start.23 = (bf16[32,3072]{1,0:T(8,128)(2,1)S(1)}, bf16[32,3072]{1,0:T(8,128)(2,1)S(1)}, u32[]{:S(2)}, u32[]{:S(2)}) collective-permute-start(bf16[32,3072]{1,0:T(8,128)(2,1)S(1)} %get-tuple-element.48), channel_id=1, source_target_pairs={{0,128},{1,129},{2,130},{3,131},{16,144},{17,145},{18,146},{19,147... | collective-permute-start | bytes 589832 | tf_op jit(solution)/shard_map/ppermute | solution.py:46
  68.9 9.8 %collective-permute-start.21 = (bf16[64,3072]{1,0:T(8,128)(2,1)S(1)}, bf16[64,3072]{1,0:T(8,128)(2,1)S(1)}, u32[]{:S(2)}, u32[]{:S(2)}) collective-permute-start(bf16[64,3072]{1,0:T(8,128)(2,1)S(1)} %get-tuple-element.44), channel_id=1, source_target_pairs={{0,64},{1,65},{2,66},{3,67},{16,208},{17,209},{18,210},{19,211},{3... | collective-permute-start | bytes 1179656 | tf_op jit(solution)/shard_map/ppermute | solution.py:46
  69.8 2.0 %collective-permute-start.20 = (bf16[32,3072]{1,0:T(8,128)(2,1)S(1)}, bf16[32,3072]{1,0:T(8,128)(2,1)S(1)}, u32[]{:S(2)}, u32[]{:S(2)}) collective-permute-start(bf16[32,3072]{1,0:T(8,128)(2,1)S(1)} %slice.208), channel_id=1, source_target_pairs={{16,0},{17,1},{18,2},{19,3},{0,16},{1,17},{2,18},{3,19},{48,32},{4... | collective-permute-start | bytes 589832 | tf_op jit(solution)/shard_map/ppermute | solution.py:46
  78.7 2.6 %collective-permute-start.24 = (bf16[32,3072]{1,0:T(8,128)(2,1)S(1)}, bf16[32,3072]{1,0:T(8,128)(2,1)S(1)}, u32[]{:S(2)}, u32[]{:S(2)}) collective-permute-start(bf16[32,3072]{1,0:T(8,128)(2,1)S(1)} %slice.252), channel_id=1, source_target_pairs={{16,0},{17,1},{18,2},{19,3},{0,16},{1,17},{2,18},{3,19},{48,32},{4... | collective-permute-start | bytes 589832 | tf_op jit(solution)/shard_map/ppermute | solution.py:46
  81.5 8.5 %collective-permute-start.25 = (bf16[2,8,3072]{2,1,0:T(8,128)(2,1)S(1)}, bf16[2,8,3072]{2,1,0:T(8,128)(2,1)S(1)}, u32[]{:S(2)}, u32[]{:S(2)}) collective-permute-start(bf16[2,8,3072]{2,1,0:T(8,128)(2,1)S(1)} %get-tuple-element.56), channel_id=1, source_target_pairs={{0,32},{1,33},{2,34},{3,35},{16,51},{17,48},{18,49},{19,50},{32,1}... | collective-permute-start | bytes 294920 | tf_op jit(solution)/shard_map/ppermute | solution.py:46
  82.5 7.5 %collective-permute-start.26 = (bf16[2,8,3072]{2,1,0:T(8,128)(2,1)S(1)}, bf16[2,8,3072]{2,1,0:T(8,128)(2,1)S(1)}, u32[]{:S(2)}, u32[]{:S(2)}) collective-permute-start(bf16[2,8,3072]{2,1,0:T(8,128)(2,1)S(1)} %get-tuple-element.57), channel_id=1, source_target_pairs={{0,1},{1,2},{2,3},{3,0},{16,19},{17,16},{18,17},{19,18},{32,33},{3... | collective-permute-start | bytes 294920 | tf_op jit(solution)/shard_map/ppermute | solution.py:46
  83.4 11.0 %collective-permute-start.28 = (bf16[2,8,3072]{2,1,0:T(8,128)(2,1)S(1)}, bf16[2,8,3072]{2,1,0:T(8,128)(2,1)S(1)}, u32[]{:S(2)}, u32[]{:S(2)}) collective-permute-start(bf16[2,8,3072]{2,1,0:T(8,128)(2,1)S(1)} %get-tuple-element.58), channel_id=1, source_target_pairs={{0,0},{1,1},{2,2},{3,3},{16,18},{17,19},{18,16},{19,17},{32,32},{3... | collective-permute-start | bytes 294920 | tf_op jit(solution)/shard_map/ppermute | solution.py:46
  88.0 6.4 %collective-permute-start.27 = (bf16[2,8,3072]{2,1,0:T(8,128)(2,1)S(1)}, bf16[2,8,3072]{2,1,0:T(8,128)(2,1)S(1)}, u32[]{:S(2)}, u32[]{:S(2)}) collective-permute-start(bf16[2,8,3072]{2,1,0:T(8,128)(2,1)S(1)} %get-tuple-element.59), channel_id=1, source_target_pairs={{0,33},{1,34},{2,35},{3,32},{16,50},{17,51},{18,48},{19,49},{32,2}... | collective-permute-start | bytes 294920 | tf_op jit(solution)/shard_map/ppermute | solution.py:46
  94.5 1.3 %collective-permute-start.29 = (bf16[2,4,3072]{2,1,0:T(4,128)(2,1)S(1)}, bf16[2,4,3072]{2,1,0:T(4,128)(2,1)S(1)}, u32[]{:S(2)}, u32[]{:S(2)}) collective-permute-start(bf16[2,4,3072]{2,1,0:T(4,128)(2,1)S(1)} %slice.379), channel_id=1, source_target_pairs={{16,0},{17,1},{18,2},{19,3},{0,16},{1,17},{2,18},{3,19},{48,32},{4... | collective-permute-start | bytes 147464 | tf_op jit(solution)/shard_map/ppermute | solution.py:46

commit v4 on v3

--- a/solution.py
+++ b/solution.py
@@ -39,7 +39,7 @@
 ]
 X_NEXT = pairs(lambda x, z, c: (x + 1 - 2 * c, z, c))
 X_FAR = pairs(lambda x, z, c: (x + 2, z, c))
-ROW_SHIFTS = [[(i, (i + d) % 4) for i in range(4)] for d in (1, 2, 3)]
+ROW_SHIFTS = [[(i, (i + d) % 4) for i in range(4)] for d in (2, 3, 1)]
 
 
 def send(value, perm):
@@ -173,7 +173,8 @@
     width, units = w_in.shape
     mine = jnp.stack([tokens, cotangent])
     block = jnp.concatenate([mine, send(mine, OTHER_CORE)], axis=1)
-    slots = [send(block, p) for p in Z_SLOTS]
+    slots = {i: send(block, Z_SLOTS[i]) for i in (3, 2, 1, 0)}
+    slots = [slots[i] for i in range(4)]
     w_in_other = send(after(w_in, slots[1]), OTHER_CORE)
     w_out_other = send(after(w_out, slots[2]), OTHER_CORE)
     share = jnp.concatenate(slots, axis=1)
@@ -231,7 +232,7 @@
     backward = finish_x(backward, backward_rest)
     result = jnp.stack([forward, backward])
     summed = jnp.zeros((2, 8, width), F32)
-    for i in (1, 2, 3, 0):
+    for i in (1, 2, 0, 3):
         piece = send(result[:, 8 * i : 8 * i + 8], inverse(Z_SLOTS[i]))
         summed = summed + piece.astype(F32)
     summed = summed[:, :4] + send(summed[:, 4:].astype(BF16), OTHER_CORE).astype(F32)

time: 96.9 us -> 94.9 us (0.979)
  waiting for transfers between devices: 37.1 us -> 35.5 us
    ppermute x6, waiting for transfers between devices: 5.21 us -> 3.77 us  [exchange_rows(): return [lax.ppermute(rounded, 'row', shift) for shift in ROW_SHIFTS]]
  transfers between devices with their start and end apart: 30 -> 30, of which waited for: 12 -> 11; matrix products, arithmetic and copies ran while one was open for 6% -> 6% of each run, Pallas kernels for 5% -> 6%
where the time goes in v4:
time: 94.9 us; the launch traced here: 94.6 us
  starting transfers between devices  44.6 us (47%)
  waiting for transfers between devices  35.5 us (37%)
  Pallas kernels  5.23 us (6%)
  matrix products  4.64 us (5%)
  other arithmetic  2.1 us (2%)
  local copies, waits for them, and re-layouts  1.49 us (2%)
  between operations  1.11 us (1%)
    ppermute x24, starting transfers between devices, send(): return lax.ppermute(value, PLANE, perm)  36.7 us
    ppermute x24, waiting for transfers between devices, send(): return lax.ppermute(value, PLANE, perm)  31.7 us
    ppermute x6, starting transfers between devices, exchange_rows(): return [lax.ppermute(rounded, 'row', shift) for shift in ROW_SHIFTS]  7.91 us
    pallas_call x4, Pallas kernels, call(): pl.pallas_call(body, out_shape=[jax.ShapeDtypeStruct(shape, dtype) for sh...  5.23 us
    dot_general x2, matrix products, t_dot(): lax.dot_general(a, b, (((0,), (0,)), ((), ())), preferred_element_type=F32)  4.64 us
    ppermute x6, waiting for transfers between devices, exchange_rows(): return [lax.ppermute(rounded, 'row', shift) for shift in ROW_SHIFTS]  3.77 us
  transfers between devices with their start and end apart: 30, of which 11 were waited for; matrix products, arithmetic and copies ran while one was open for 6% of the time, Pallas kernels for 6%

profile of v4, /device:TPU:1, one launch (start us, length us, event | category | flops | bytes accessed | tf_op | source)
XLA Modules:
  0.0 94.6 jit_solution(17757069978552316028)
XLA Ops:
  1.4 3.3 %collective-permute-start = (bf16[2,4,3072]{2,1,0:T(4,128)(2,1)S(1)}, bf16[2,4,3072]{2,1,0:T(4,128)(2,1)S(1)}, u32[]{:S(2)}, u32[]{:S(2)}) collective-permute-start(bf16[2,4,3072]{2,1,0:T(4,128)(2,1)S(1)} %pad_maximum_fusion.3), channel_id=1, source_target_pairs={{16,0},{17,1},{18,2},{19,3},{0,16},{1,17},{2,18},{3,19},{48,32},{4... | collective-permute-start | bytes 147464 | tf_op jit(solution)/shard_map/ppermute | solution.py:46
  6.4 7.1 %collective-permute-start.1 = (bf16[2,8,3072]{2,1,0:T(8,128)(2,1)S(1)}, bf16[2,8,3072]{2,1,0:T(8,128)(2,1)S(1)}, u32[]{:S(2)}, u32[]{:S(2)}) collective-permute-start(bf16[2,8,3072]{2,1,0:T(8,128)(2,1)S(1)} %pad_maximum_fusion.2), channel_id=1, source_target_pairs={{0,0},{1,1},{2,2},{3,3},{18,16},{19,17},{16,18},{17,19},{32,32},{3... | collective-permute-start | bytes 294920 | tf_op jit(solution)/shard_map/ppermute | solution.py:46
  13.5 1.7 %collective-permute-start.4 = (bf16[2,8,3072]{2,1,0:T(8,128)(2,1)S(1)}, bf16[2,8,3072]{2,1,0:T(8,128)(2,1)S(1)}, u32[]{:S(2)}, u32[]{:S(2)}) collective-permute-start(bf16[2,8,3072]{2,1,0:T(8,128)(2,1)S(1)} %pad_maximum_fusion.2), channel_id=1, source_target_pairs={{33,0},{34,1},{35,2},{32,3},{50,16},{51,17},{48,18},{49,19},{2,32}... | collective-permute-start | bytes 294920 | tf_op jit(solution)/shard_map/ppermute | solution.py:46
  15.8 8.6 %collective-permute-done.2 = bf16[2,8,3072]{2,1,0:T(8,128)(2,1)S(1)} collective-permute-done((bf16[2,8,3072]{2,1,0:T(8,128)(2,1)S(1)}, bf16[2,8,3072]{2,1,0:T(8,128)(2,1)S(1)}, u32[]{:S(2)}, u32[]{:S(2)}) %collective-permute-start.2) | collective-permute-done | bytes 98336 | tf_op jit(solution)/shard_map/ppermute | solution.py:46
  24.7 2.8 %collective-permute-start.7 = (bf16[32,3072]{1,0:T(8,128)(2,1)S(1)}, bf16[32,3072]{1,0:T(8,128)(2,1)S(1)}, u32[]{:S(2)}, u32[]{:S(2)}) collective-permute-start(bf16[32,3072]{1,0:T(8,128)(2,1)S(1)} %get-tuple-element.64.own), channel_id=1, source_target_pairs={{128,0},{129,1},{130,2},{131,3},{144,16},{145,17},{146,18},{147,19... | collective-permute-start | bytes 589832 | tf_op jit(solution)/shard_map/ppermute | solution.py:46
  29.1 8.1 %collective-permute-done.6.near = bf16[64,3072]{1,0:T(8,128)(2,1)S(1)} collective-permute-done((bf16[64,3072]{1,0:T(8,128)(2,1)S(1)}, bf16[64,3072]{1,0:T(8,128)(2,1)S(1)}, u32[]{:S(2)}, u32[]{:S(2)}) %collective-permute-start.6) | collective-permute-done | bytes 393248 | tf_op jit(solution)/shard_map/ppermute | solution.py:46
  37.3 1.0 %shard_map.75 = (f32[128,768]{1,0:T(8,128)S(1)}, bf16[128,768]{1,0:T(8,128)(2,1)S(1)}) custom-call(bf16[32,3072]{1,0:T(8,128)(2,1)S(1)} %get-tuple-element.64.own, bf16[64,3072]{1,0:T(8,128)(2,1)S(1)} %collective-permute-done.6.near, bf16[32,3072]{1,0:T(8,128)(2,1)S(1)} %collective-permute-done.7.far, bf16[3072,384]{1,0:T(8,128)(2,1)S(1)} %copy-done.1, ...), custom_call_target="tpu_custom_call" | custom-call | flops 4000000000 | tf_op jit(solution)/shard_map/pallas_call | solution.py:162
  38.3 1.4 %collective-permute-start.14 = (bf16[128,768]{1,0:T(8,128)(2,1)S(1)}, bf16[128,768]{1,0:T(8,128)(2,1)S(1)}, u32[]{:S(2)}, u32[]{:S(2)}) collective-permute-start(bf16[128,768]{1,0:T(8,128)(2,1)S(1)} %get-tuple-element.29), channel_id=1, source_target_pairs={{0,4},{4,8},{8,12},{12,0},{1,5},{5,9},{9,13},{13,1},{2,6},{6,10},{... | collective-permute-start | bytes 589832 | tf_op jit(solution)/shard_map/ppermute | solution.py:63
  39.6 1.5 %collective-permute-start.13 = (bf16[128,768]{1,0:T(8,128)(2,1)S(1)}, bf16[128,768]{1,0:T(8,128)(2,1)S(1)}, u32[]{:S(2)}, u32[]{:S(2)}) collective-permute-start(bf16[128,768]{1,0:T(8,128)(2,1)S(1)} %get-tuple-element.29), channel_id=1, source_target_pairs={{0,12},{4,0},{8,4},{12,8},{1,13},{5,1},{9,5},{13,9},{2,14},{6,2},{... | collective-permute-start | bytes 589832 | tf_op jit(solution)/shard_map/ppermute | solution.py:63
  41.2 1.6 %collective-permute-start.9 = (bf16[128,768]{1,0:T(8,128)(2,1)S(1)}, bf16[128,768]{1,0:T(8,128)(2,1)S(1)}, u32[]{:S(2)}, u32[]{:S(2)}) collective-permute-start(bf16[128,768]{1,0:T(8,128)(2,1)S(1)} %get-tuple-element.29), channel_id=1, source_target_pairs={{0,8},{4,12},{8,0},{12,4},{1,9},{5,13},{9,1},{13,5},{2,10},{6,14},... | collective-permute-start | bytes 589832 | tf_op jit(solution)/shard_map/ppermute | solution.py:63
  42.8 1.6 %collective-permute-start.11 = (bf16[32,3072]{1,0:T(8,128)(2,1)S(1)}, bf16[32,3072]{1,0:T(8,128)(2,1)S(1)}, u32[]{:S(2)}, u32[]{:S(2)}) collective-permute-start(bf16[32,3072]{1,0:T(8,128)(2,1)S(1)} %slice.206), channel_id=1, source_target_pairs={{64,0},{65,1},{66,2},{67,3},{208,16},{209,17},{210,18},{211,19},{9... | collective-permute-start | bytes 589832 | tf_op jit(solution)/shard_map/ppermute | solution.py:46
  44.4 4.2 %collective-permute-done.11.far = bf16[32,3072]{1,0:T(8,128)(2,1)S(1)} collective-permute-done((bf16[32,3072]{1,0:T(8,128)(2,1)S(1)}, bf16[32,3072]{1,0:T(8,128)(2,1)S(1)}, u32[]{:S(2)}, u32[]{:S(2)}) %collective-permute-start.11) | collective-permute-done | bytes 196640 | tf_op jit(solution)/shard_map/ppermute | solution.py:46
  48.6 1.4 %shard_map.76 = (f32[128,768]{1,0:T(8,128)S(1)}, bf16[128,768]{1,0:T(8,128)(2,1)S(1)}) custom-call(bf16[32,3072]{1,0:T(8,128)(2,1)S(1)} %get-tuple-element.65.own, bf16[64,3072]{1,0:T(8,128)(2,1)S(1)} %collective-permute-done.10.near, bf16[32,3072]{1,0:T(8,128)(2,1)S(1)} %collective-permute-done.11.far, bf16[384,3072]{1,0:T(8,128)(2,1)S(1)} %copy-done, ...), custom_call_target="tpu_custom_call" | custom-call | tf_op jit(solution)/shard_map/pallas_call | solution.py:162
  50.7 2.3 %collective-permute-start.17 = (bf16[128,768]{1,0:T(8,128)(2,1)S(1)}, bf16[128,768]{1,0:T(8,128)(2,1)S(1)}, u32[]{:S(2)}, u32[]{:S(2)}) collective-permute-start(bf16[128,768]{1,0:T(8,128)(2,1)S(1)} %get-tuple-element.38), channel_id=1, source_target_pairs={{0,12},{4,0},{8,4},{12,8},{1,13},{5,1},{9,5},{13,9},{2,14},{6,2},{... | collective-permute-start | bytes 589832 | tf_op jit(solution)/shard_map/ppermute | solution.py:63
  53.5 1.2 %shard_map.77 = (bf16[128,768]{1,0:T(8,128)(2,1)S(1)}, f32[128,768]{1,0:T(8,128)S(1)}, f32[32,3072]{1,0:T(8,128)S(1)}, bf16[64,3072]{1,0:T(8,128)(2,1)S(1)}, bf16[32,3072]{1,0:T(8,128)(2,1)S(1)}) custom-call(f32[128,768]{1,0:T(8,128)S(1)} %get-tuple-element.28.part, bf16[128,768]{1,0:T(8,128)(2,1)S(1)} %collective-permute-done.9.r0, ...), custom_call_target="tpu_custom_call" | custom-call | tf_op jit(solution)/shard_map/pallas_call | solution.py:162
  54.8 2.0 %collective-permute-start.19 = (bf16[32,3072]{1,0:T(8,128)(2,1)S(1)}, bf16[32,3072]{1,0:T(8,128)(2,1)S(1)}, u32[]{:S(2)}, u32[]{:S(2)}) collective-permute-start(bf16[32,3072]{1,0:T(8,128)(2,1)S(1)} %get-tuple-element.42), channel_id=1, source_target_pairs={{0,128},{1,129},{2,130},{3,131},{16,144},{17,145},{18,146},{19,147... | collective-permute-start | bytes 589832 | tf_op jit(solution)/shard_map/ppermute | solution.py:46
  57.8 3.8 %collective-permute-done.16.r0 = bf16[128,768]{1,0:T(8,128)(2,1)S(1)} collective-permute-done((bf16[128,768]{1,0:T(8,128)(2,1)S(1)}, bf16[128,768]{1,0:T(8,128)(2,1)S(1)}, u32[]{:S(2)}, u32[]{:S(2)}) %collective-permute-start.16) | collective-permute-done | bytes 196640 | tf_op jit(solution)/shard_map/ppermute | solution.py:63
  61.5 1.6 %shard_map.78 = (bf16[128,768]{1,0:T(8,128)(2,1)S(1)}, f32[32,3072]{1,0:T(8,128)S(1)}, bf16[64,3072]{1,0:T(8,128)(2,1)S(1)}, bf16[32,3072]{1,0:T(8,128)(2,1)S(1)}) custom-call(f32[128,768]{1,0:T(8,128)S(1)} %get-tuple-element.32.part, bf16[128,768]{1,0:T(8,128)(2,1)S(1)} %collective-permute-done.16.r0, bf16[128,768]{1,0:T(8,128)(2,1)S(1)} %collective-permute-done.17.r1, ...), custom_call_target="tpu_custom_call" | custom-call | tf_op jit(solution)/shard_map/pallas_call | solution.py:162
  63.4 1.8 %collective-permute-start.22 = (bf16[2,112,3072]{2,1,0:T(8,128)(2,1)S(1)}, bf16[2,112,3072]{2,1,0:T(8,128)(2,1)S(1)}, u32[]{:S(2)}, u32[]{:S(2)}) collective-permute-start(bf16[2,112,3072]{2,1,0:T(8,128)(2,1)S(1)} %pad_maximum_fusion), channel_id=1, source_target_pairs={{16,0},{17,1},{18,2},{19,3},{0,16},{1,17},{2,18},{3,19},{48,32},{4... | collective-permute-start | bytes 4128776 | tf_op jit(solution)/shard_map/ppermute | solution.py:46
  65.3 1.9 %collective-permute-start.23 = (bf16[32,3072]{1,0:T(8,128)(2,1)S(1)}, bf16[32,3072]{1,0:T(8,128)(2,1)S(1)}, u32[]{:S(2)}, u32[]{:S(2)}) collective-permute-start(bf16[32,3072]{1,0:T(8,128)(2,1)S(1)} %get-tuple-element.48), channel_id=1, source_target_pairs={{0,128},{1,129},{2,130},{3,131},{16,144},{17,145},{18,146},{19,147... | collective-permute-start | bytes 589832 | tf_op jit(solution)/shard_map/ppermute | solution.py:46
  67.2 1.3 %collective-permute-start.21 = (bf16[64,3072]{1,0:T(8,128)(2,1)S(1)}, bf16[64,3072]{1,0:T(8,128)(2,1)S(1)}, u32[]{:S(2)}, u32[]{:S(2)}) collective-permute-start(bf16[64,3072]{1,0:T(8,128)(2,1)S(1)} %get-tuple-element.44), channel_id=1, source_target_pairs={{0,64},{1,65},{2,66},{3,67},{16,208},{17,209},{18,210},{19,211},{3... | collective-permute-start | bytes 1179656 | tf_op jit(solution)/shard_map/ppermute | solution.py:46
  68.5 1.4 %collective-permute-start.20 = (bf16[32,3072]{1,0:T(8,128)(2,1)S(1)}, bf16[32,3072]{1,0:T(8,128)(2,1)S(1)}, u32[]{:S(2)}, u32[]{:S(2)}) collective-permute-start(bf16[32,3072]{1,0:T(8,128)(2,1)S(1)} %slice.208), channel_id=1, source_target_pairs={{16,0},{17,1},{18,2},{19,3},{0,16},{1,17},{2,18},{3,19},{48,32},{4... | collective-permute-start | bytes 589832 | tf_op jit(solution)/shard_map/ppermute | solution.py:46
  69.9 1.1 %collective-permute-done.20 = bf16[32,3072]{1,0:T(8,128)(2,1)S(1)} collective-permute-done((bf16[32,3072]{1,0:T(8,128)(2,1)S(1)}, bf16[32,3072]{1,0:T(8,128)(2,1)S(1)}, u32[]{:S(2)}, u32[]{:S(2)}) %collective-permute-start.20) | collective-permute-done | bytes 196640 | tf_op jit(solution)/shard_map/ppermute | solution.py:46
  71.5 2.2 %convolution_convert_fusion = bf16[384,3072]{1,0:T(8,128)(2,1)} fusion(bf16[256,384]{1,0:T(8,128)(2,1)S(1)} %get-tuple-element.77, bf16[256,3072]{1,0:T(8,128)(2,1)S(1)} %get-tuple-element.50), kind=kOutput, calls=%fused_computation | convolution fusion | flops 605159424 | bytes 4128768 | tf_op jit(solution)/shard_map/dot_general | solution.py:92
  73.7 2.4 %convolution_convert_fusion.1 = bf16[3072,384]{1,0:T(8,128)(2,1)} fusion(bf16[256,3072]{1,0:T(8,128)(2,1)S(1)} %get-tuple-element.51, bf16[256,384]{1,0:T(8,128)(2,1)S(1)} %get-tuple-element.76), kind=kOutput, calls=%fused_computation.1 | convolution fusion | flops 605159424 | bytes 4128768 | tf_op jit(solution)/shard_map/dot_general | solution.py:92
  76.1 1.9 %collective-permute-done.21 = bf16[64,3072]{1,0:T(8,128)(2,1)S(1)} collective-permute-done((bf16[64,3072]{1,0:T(8,128)(2,1)S(1)}, bf16[64,3072]{1,0:T(8,128)(2,1)S(1)}, u32[]{:S(2)}, u32[]{:S(2)}) %collective-permute-start.21) | collective-permute-done | bytes 393248 | tf_op jit(solution)/shard_map/ppermute | solution.py:46
  78.5 1.1 %collective-permute-done.24 = bf16[32,3072]{1,0:T(8,128)(2,1)S(1)} collective-permute-done((bf16[32,3072]{1,0:T(8,128)(2,1)S(1)}, bf16[32,3072]{1,0:T(8,128)(2,1)S(1)}, u32[]{:S(2)}, u32[]{:S(2)}) %collective-permute-start.24) | collective-permute-done | bytes 196640 | tf_op jit(solution)/shard_map/ppermute | solution.py:46
  79.7 1.0 %collective-permute-start.25 = (bf16[2,8,3072]{2,1,0:T(8,128)(2,1)S(1)}, bf16[2,8,3072]{2,1,0:T(8,128)(2,1)S(1)}, u32[]{:S(2)}, u32[]{:S(2)}) collective-permute-start(bf16[2,8,3072]{2,1,0:T(8,128)(2,1)S(1)} %get-tuple-element.56), channel_id=1, source_target_pairs={{0,32},{1,33},{2,34},{3,35},{16,51},{17,48},{18,49},{19,50},{32,1}... | collective-permute-start | bytes 294920 | tf_op jit(solution)/shard_map/ppermute | solution.py:46
  81.6 1.6 %collective-permute-start.28 = (bf16[2,8,3072]{2,1,0:T(8,128)(2,1)S(1)}, bf16[2,8,3072]{2,1,0:T(8,128)(2,1)S(1)}, u32[]{:S(2)}, u32[]{:S(2)}) collective-permute-start(bf16[2,8,3072]{2,1,0:T(8,128)(2,1)S(1)} %get-tuple-element.58), channel_id=1, source_target_pairs={{0,33},{1,34},{2,35},{3,32},{16,50},{17,51},{18,48},{19,49},{32,2}... | collective-permute-start | bytes 294920 | tf_op jit(solution)/shard_map/ppermute | solution.py:46
  83.2 4.8 %collective-permute-start.27 = (bf16[2,8,3072]{2,1,0:T(8,128)(2,1)S(1)}, bf16[2,8,3072]{2,1,0:T(8,128)(2,1)S(1)}, u32[]{:S(2)}, u32[]{:S(2)}) collective-permute-start(bf16[2,8,3072]{2,1,0:T(8,128)(2,1)S(1)} %get-tuple-element.59), channel_id=1, source_target_pairs={{0,0},{1,1},{2,2},{3,3},{16,18},{17,19},{18,16},{19,17},{32,32},{3... | collective-permute-start | bytes 294920 | tf_op jit(solution)/shard_map/ppermute | solution.py:46
  88.1 4.5 %collective-permute-done.27 = bf16[2,8,3072]{2,1,0:T(8,128)(2,1)S(1)} collective-permute-done((bf16[2,8,3072]{2,1,0:T(8,128)(2,1)S(1)}, bf16[2,8,3072]{2,1,0:T(8,128)(2,1)S(1)}, u32[]{:S(2)}, u32[]{:S(2)}) %collective-permute-start.27) | collective-permute-done | bytes 98336 | tf_op jit(solution)/shard_map/ppermute | solution.py:46
  92.7 1.2 %collective-permute-done.29 = bf16[2,4,3072]{2,1,0:T(4,128)(2,1)S(1)} collective-permute-done((bf16[2,4,3072]{2,1,0:T(4,128)(2,1)S(1)}, bf16[2,4,3072]{2,1,0:T(4,128)(2,1)S(1)}, u32[]{:S(2)}, u32[]{:S(2)}) %collective-permute-start.29) | collective-permute-done | bytes 49184 | tf_op jit(solution)/shard_map/ppermute | solution.py:46
  (101 shorter events, 10.1 us)
Async XLA Ops:
  1.4 4.2 %collective-permute-start = (bf16[2,4,3072]{2,1,0:T(4,128)(2,1)S(1)}, bf16[2,4,3072]{2,1,0:T(4,128)(2,1)S(1)}, u32[]{:S(2)}, u32[]{:S(2)}) collective-permute-start(bf16[2,4,3072]{2,1,0:T(4,128)(2,1)S(1)} %pad_maximum_fusion.3), channel_id=1, source_target_pairs={{16,0},{17,1},{18,2},{19,3},{0,16},{1,17},{2,18},{3,19},{48,32},{4... | collective-permute-start | bytes 147464 | tf_op jit(solution)/shard_map/ppermute | solution.py:46
  6.4 9.4 %collective-permute-start.1 = (bf16[2,8,3072]{2,1,0:T(8,128)(2,1)S(1)}, bf16[2,8,3072]{2,1,0:T(8,128)(2,1)S(1)}, u32[]{:S(2)}, u32[]{:S(2)}) collective-permute-start(bf16[2,8,3072]{2,1,0:T(8,128)(2,1)S(1)} %pad_maximum_fusion.2), channel_id=1, source_target_pairs={{0,0},{1,1},{2,2},{3,3},{18,16},{19,17},{16,18},{17,19},{32,32},{3... | collective-permute-start | bytes 294920 | tf_op jit(solution)/shard_map/ppermute | solution.py:46
  13.5 11.0 %collective-permute-start.4 = (bf16[2,8,3072]{2,1,0:T(8,128)(2,1)S(1)}, bf16[2,8,3072]{2,1,0:T(8,128)(2,1)S(1)}, u32[]{:S(2)}, u32[]{:S(2)}) collective-permute-start(bf16[2,8,3072]{2,1,0:T(8,128)(2,1)S(1)} %pad_maximum_fusion.2), channel_id=1, source_target_pairs={{33,0},{34,1},{35,2},{32,3},{50,16},{51,17},{48,18},{49,19},{2,32}... | collective-permute-start | bytes 294920 | tf_op jit(solution)/shard_map/ppermute | solution.py:46
  15.3 9.2 %collective-permute-start.3 = (bf16[2,8,3072]{2,1,0:T(8,128)(2,1)S(1)}, bf16[2,8,3072]{2,1,0:T(8,128)(2,1)S(1)}, u32[]{:S(2)}, u32[]{:S(2)}) collective-permute-start(bf16[2,8,3072]{2,1,0:T(8,128)(2,1)S(1)} %pad_maximum_fusion.2), channel_id=1, source_target_pairs={{1,0},{2,1},{3,2},{0,3},{19,16},{16,17},{17,18},{18,19},{33,32},{3... | collective-permute-start | bytes 294920 | tf_op jit(solution)/shard_map/ppermute | solution.py:46
  15.3 9.2 %collective-permute-start.2 = (bf16[2,8,3072]{2,1,0:T(8,128)(2,1)S(1)}, bf16[2,8,3072]{2,1,0:T(8,128)(2,1)S(1)}, u32[]{:S(2)}, u32[]{:S(2)}) collective-permute-start(bf16[2,8,3072]{2,1,0:T(8,128)(2,1)S(1)} %pad_maximum_fusion.2), channel_id=1, source_target_pairs={{32,0},{33,1},{34,2},{35,3},{51,16},{48,17},{49,18},{50,19},{1,32}... | collective-permute-start | bytes 294920 | tf_op jit(solution)/shard_map/ppermute | solution.py:46
  24.6 3.7 %collective-permute-start.5 = (bf16[2,32,3072]{2,1,0:T(8,128)(2,1)S(1)}, bf16[2,32,3072]{2,1,0:T(8,128)(2,1)S(1)}, u32[]{:S(2)}, u32[]{:S(2)}) collective-permute-start(bf16[2,32,3072]{2,1,0:T(8,128)(2,1)S(1)} %get-tuple-element.67), channel_id=1, source_target_pairs={{16,0},{17,1},{18,2},{19,3},{0,16},{1,17},{2,18},{3,19},{48,32},{4... | collective-permute-start | bytes 1179656 | tf_op jit(solution)/shard_map/ppermute | solution.py:46
  24.7 12.5 %collective-permute-start.7 = (bf16[32,3072]{1,0:T(8,128)(2,1)S(1)}, bf16[32,3072]{1,0:T(8,128)(2,1)S(1)}, u32[]{:S(2)}, u32[]{:S(2)}) collective-permute-start(bf16[32,3072]{1,0:T(8,128)(2,1)S(1)} %get-tuple-element.64.own), channel_id=1, source_target_pairs={{128,0},{129,1},{130,2},{131,3},{144,16},{145,17},{146,18},{147,19... | collective-permute-start | bytes 589832 | tf_op jit(solution)/shard_map/ppermute | solution.py:46
  27.5 9.7 %collective-permute-start.8 = (bf16[3072,384]{1,0:T(8,128)(2,1)}, bf16[3072,384]{1,0:T(8,128)(2,1)S(1)}, u32[]{:S(2)}, u32[]{:S(2)}) collective-permute-start(bf16[3072,384]{1,0:T(8,128)(2,1)} %w_a.7), channel_id=1, source_target_pairs={{16,0},{17,1},{18,2},{19,3},{0,16},{1,17},{2,18},{3,19},{48,32},{4... | collective-permute-start | bytes 7077896 | tf_op jit(solution)/shard_map/ppermute | solution.py:46
  28.3 16.1 %collective-permute-start.12 = (bf16[384,3072]{1,0:T(8,128)(2,1)}, bf16[384,3072]{1,0:T(8,128)(2,1)S(1)}, u32[]{:S(2)}, u32[]{:S(2)}) collective-permute-start(bf16[384,3072]{1,0:T(8,128)(2,1)} %w_a.6), channel_id=1, source_target_pairs={{16,0},{17,1},{18,2},{19,3},{0,16},{1,17},{2,18},{3,19},{48,32},{4... | collective-permute-start | bytes 7077896 | tf_op jit(solution)/shard_map/ppermute | solution.py:46
  28.3 8.9 %copy-start.1 = (bf16[3072,384]{1,0:T(8,128)(2,1)S(1)}, bf16[3072,384]{1,0:T(8,128)(2,1)}, u32[]{:S(2)}) copy-start(bf16[3072,384]{1,0:T(8,128)(2,1)} %w_a.7) | copy-start | bytes 7077892
  28.4 8.8 %collective-permute-start.6 = (bf16[64,3072]{1,0:T(8,128)(2,1)S(1)}, bf16[64,3072]{1,0:T(8,128)(2,1)S(1)}, u32[]{:S(2)}, u32[]{:S(2)}) collective-permute-start(bf16[64,3072]{1,0:T(8,128)(2,1)S(1)} %get-tuple-element.54), channel_id=1, source_target_pairs={{64,0},{65,1},{66,2},{67,3},{208,16},{209,17},{210,18},{211,19},{9... | collective-permute-start | bytes 1179656 | tf_op jit(solution)/shard_map/ppermute | solution.py:46
  28.8 13.9 %collective-permute-start.10 = (bf16[64,3072]{1,0:T(8,128)(2,1)S(1)}, bf16[64,3072]{1,0:T(8,128)(2,1)S(1)}, u32[]{:S(2)}, u32[]{:S(2)}) collective-permute-start(bf16[64,3072]{1,0:T(8,128)(2,1)S(1)} %get-tuple-element.55), channel_id=1, source_target_pairs={{64,0},{65,1},{66,2},{67,3},{208,16},{209,17},{210,18},{211,19},{9... | collective-permute-start | bytes 1179656 | tf_op jit(solution)/shard_map/ppermute | solution.py:46
  37.3 11.3 %copy-start = (bf16[384,3072]{1,0:T(8,128)(2,1)S(1)}, bf16[384,3072]{1,0:T(8,128)(2,1)}, u32[]{:S(2)}) copy-start(bf16[384,3072]{1,0:T(8,128)(2,1)} %w_a.6) | copy-start | bytes 7077892
  38.3 14.7 %collective-permute-start.14 = (bf16[128,768]{1,0:T(8,128)(2,1)S(1)}, bf16[128,768]{1,0:T(8,128)(2,1)S(1)}, u32[]{:S(2)}, u32[]{:S(2)}) collective-permute-start(bf16[128,768]{1,0:T(8,128)(2,1)S(1)} %get-tuple-element.29), channel_id=1, source_target_pairs={{0,4},{4,8},{8,12},{12,0},{1,5},{5,9},{9,13},{13,1},{2,6},{6,10},{... | collective-permute-start | bytes 589832 | tf_op jit(solution)/shard_map/ppermute | solution.py:63
  39.6 13.8 %collective-permute-start.13 = (bf16[128,768]{1,0:T(8,128)(2,1)S(1)}, bf16[128,768]{1,0:T(8,128)(2,1)S(1)}, u32[]{:S(2)}, u32[]{:S(2)}) collective-permute-start(bf16[128,768]{1,0:T(8,128)(2,1)S(1)} %get-tuple-element.29), channel_id=1, source_target_pairs={{0,12},{4,0},{8,4},{12,8},{1,13},{5,1},{9,5},{13,9},{2,14},{6,2},{... | collective-permute-start | bytes 589832 | tf_op jit(solution)/shard_map/ppermute | solution.py:63
  41.2 12.3 %collective-permute-start.9 = (bf16[128,768]{1,0:T(8,128)(2,1)S(1)}, bf16[128,768]{1,0:T(8,128)(2,1)S(1)}, u32[]{:S(2)}, u32[]{:S(2)}) collective-permute-start(bf16[128,768]{1,0:T(8,128)(2,1)S(1)} %get-tuple-element.29), channel_id=1, source_target_pairs={{0,8},{4,12},{8,0},{12,4},{1,9},{5,13},{9,1},{13,5},{2,10},{6,14},... | collective-permute-start | bytes 589832 | tf_op jit(solution)/shard_map/ppermute | solution.py:63
  42.8 5.8 %collective-permute-start.11 = (bf16[32,3072]{1,0:T(8,128)(2,1)S(1)}, bf16[32,3072]{1,0:T(8,128)(2,1)S(1)}, u32[]{:S(2)}, u32[]{:S(2)}) collective-permute-start(bf16[32,3072]{1,0:T(8,128)(2,1)S(1)} %slice.206), channel_id=1, source_target_pairs={{64,0},{65,1},{66,2},{67,3},{208,16},{209,17},{210,18},{211,19},{9... | collective-permute-start | bytes 589832 | tf_op jit(solution)/shard_map/ppermute | solution.py:46
  50.0 7.7 %collective-permute-start.18 = (bf16[128,768]{1,0:T(8,128)(2,1)S(1)}, bf16[128,768]{1,0:T(8,128)(2,1)S(1)}, u32[]{:S(2)}, u32[]{:S(2)}) collective-permute-start(bf16[128,768]{1,0:T(8,128)(2,1)S(1)} %get-tuple-element.38), channel_id=1, source_target_pairs={{0,4},{4,8},{8,12},{12,0},{1,5},{5,9},{9,13},{13,1},{2,6},{6,10},{... | collective-permute-start | bytes 589832 | tf_op jit(solution)/shard_map/ppermute | solution.py:63
  50.7 7.1 %collective-permute-start.17 = (bf16[128,768]{1,0:T(8,128)(2,1)S(1)}, bf16[128,768]{1,0:T(8,128)(2,1)S(1)}, u32[]{:S(2)}, u32[]{:S(2)}) collective-permute-start(bf16[128,768]{1,0:T(8,128)(2,1)S(1)} %get-tuple-element.38), channel_id=1, source_target_pairs={{0,12},{4,0},{8,4},{12,8},{1,13},{5,1},{9,5},{13,9},{2,14},{6,2},{... | collective-permute-start | bytes 589832 | tf_op jit(solution)/shard_map/ppermute | solution.py:63
  53.0 8.5 %collective-permute-start.16 = (bf16[128,768]{1,0:T(8,128)(2,1)S(1)}, bf16[128,768]{1,0:T(8,128)(2,1)S(1)}, u32[]{:S(2)}, u32[]{:S(2)}) collective-permute-start(bf16[128,768]{1,0:T(8,128)(2,1)S(1)} %get-tuple-element.38), channel_id=1, source_target_pairs={{0,8},{4,12},{8,0},{12,4},{1,9},{5,13},{9,1},{13,5},{2,10},{6,14},... | collective-permute-start | bytes 589832 | tf_op jit(solution)/shard_map/ppermute | solution.py:63
  54.8 10.4 %collective-permute-start.19 = (bf16[32,3072]{1,0:T(8,128)(2,1)S(1)}, bf16[32,3072]{1,0:T(8,128)(2,1)S(1)}, u32[]{:S(2)}, u32[]{:S(2)}) collective-permute-start(bf16[32,3072]{1,0:T(8,128)(2,1)S(1)} %get-tuple-element.42), channel_id=1, source_target_pairs={{0,128},{1,129},{2,130},{3,131},{16,144},{17,145},{18,146},{19,147... | collective-permute-start | bytes 589832 | tf_op jit(solution)/shard_map/ppermute | solution.py:46
  56.8 11.7 %collective-permute-start.15 = (bf16[64,3072]{1,0:T(8,128)(2,1)S(1)}, bf16[64,3072]{1,0:T(8,128)(2,1)S(1)}, u32[]{:S(2)}, u32[]{:S(2)}) collective-permute-start(bf16[64,3072]{1,0:T(8,128)(2,1)S(1)} %get-tuple-element.37), channel_id=1, source_target_pairs={{0,64},{1,65},{2,66},{3,67},{16,208},{17,209},{18,210},{19,211},{3... | collective-permute-start | bytes 1179656 | tf_op jit(solution)/shard_map/ppermute | solution.py:46
  63.4 7.7 %collective-permute-start.22 = (bf16[2,112,3072]{2,1,0:T(8,128)(2,1)S(1)}, bf16[2,112,3072]{2,1,0:T(8,128)(2,1)S(1)}, u32[]{:S(2)}, u32[]{:S(2)}) collective-permute-start(bf16[2,112,3072]{2,1,0:T(8,128)(2,1)S(1)} %pad_maximum_fusion), channel_id=1, source_target_pairs={{16,0},{17,1},{18,2},{19,3},{0,16},{1,17},{2,18},{3,19},{48,32},{4... | collective-permute-start | bytes 4128776 | tf_op jit(solution)/shard_map/ppermute | solution.py:46
  65.3 13.2 %collective-permute-start.23 = (bf16[32,3072]{1,0:T(8,128)(2,1)S(1)}, bf16[32,3072]{1,0:T(8,128)(2,1)S(1)}, u32[]{:S(2)}, u32[]{:S(2)}) collective-permute-start(bf16[32,3072]{1,0:T(8,128)(2,1)S(1)} %get-tuple-element.48), channel_id=1, source_target_pairs={{0,128},{1,129},{2,130},{3,131},{16,144},{17,145},{18,146},{19,147... | collective-permute-start | bytes 589832 | tf_op jit(solution)/shard_map/ppermute | solution.py:46
  67.2 10.8 %collective-permute-start.21 = (bf16[64,3072]{1,0:T(8,128)(2,1)S(1)}, bf16[64,3072]{1,0:T(8,128)(2,1)S(1)}, u32[]{:S(2)}, u32[]{:S(2)}) collective-permute-start(bf16[64,3072]{1,0:T(8,128)(2,1)S(1)} %get-tuple-element.44), channel_id=1, source_target_pairs={{0,64},{1,65},{2,66},{3,67},{16,208},{17,209},{18,210},{19,211},{3... | collective-permute-start | bytes 1179656 | tf_op jit(solution)/shard_map/ppermute | solution.py:46
  68.5 2.4 %collective-permute-start.20 = (bf16[32,3072]{1,0:T(8,128)(2,1)S(1)}, bf16[32,3072]{1,0:T(8,128)(2,1)S(1)}, u32[]{:S(2)}, u32[]{:S(2)}) collective-permute-start(bf16[32,3072]{1,0:T(8,128)(2,1)S(1)} %slice.208), channel_id=1, source_target_pairs={{16,0},{17,1},{18,2},{19,3},{0,16},{1,17},{2,18},{3,19},{48,32},{4... | collective-permute-start | bytes 589832 | tf_op jit(solution)/shard_map/ppermute | solution.py:46
  78.0 1.6 %collective-permute-start.24 = (bf16[32,3072]{1,0:T(8,128)(2,1)S(1)}, bf16[32,3072]{1,0:T(8,128)(2,1)S(1)}, u32[]{:S(2)}, u32[]{:S(2)}) collective-permute-start(bf16[32,3072]{1,0:T(8,128)(2,1)S(1)} %slice.252), channel_id=1, source_target_pairs={{16,0},{17,1},{18,2},{19,3},{0,16},{1,17},{2,18},{3,19},{48,32},{4... | collective-permute-start | bytes 589832 | tf_op jit(solution)/shard_map/ppermute | solution.py:46
  79.7 8.4 %collective-permute-start.25 = (bf16[2,8,3072]{2,1,0:T(8,128)(2,1)S(1)}, bf16[2,8,3072]{2,1,0:T(8,128)(2,1)S(1)}, u32[]{:S(2)}, u32[]{:S(2)}) collective-permute-start(bf16[2,8,3072]{2,1,0:T(8,128)(2,1)S(1)} %get-tuple-element.56), channel_id=1, source_target_pairs={{0,32},{1,33},{2,34},{3,35},{16,51},{17,48},{18,49},{19,50},{32,1}... | collective-permute-start | bytes 294920 | tf_op jit(solution)/shard_map/ppermute | solution.py:46
  80.7 7.4 %collective-permute-start.26 = (bf16[2,8,3072]{2,1,0:T(8,128)(2,1)S(1)}, bf16[2,8,3072]{2,1,0:T(8,128)(2,1)S(1)}, u32[]{:S(2)}, u32[]{:S(2)}) collective-permute-start(bf16[2,8,3072]{2,1,0:T(8,128)(2,1)S(1)} %get-tuple-element.57), channel_id=1, source_target_pairs={{0,1},{1,2},{2,3},{3,0},{16,19},{17,16},{18,17},{19,18},{32,33},{3... | collective-permute-start | bytes 294920 | tf_op jit(solution)/shard_map/ppermute | solution.py:46
  81.6 6.5 %collective-permute-start.28 = (bf16[2,8,3072]{2,1,0:T(8,128)(2,1)S(1)}, bf16[2,8,3072]{2,1,0:T(8,128)(2,1)S(1)}, u32[]{:S(2)}, u32[]{:S(2)}) collective-permute-start(bf16[2,8,3072]{2,1,0:T(8,128)(2,1)S(1)} %get-tuple-element.58), channel_id=1, source_target_pairs={{0,33},{1,34},{2,35},{3,32},{16,50},{17,51},{18,48},{19,49},{32,2}... | collective-permute-start | bytes 294920 | tf_op jit(solution)/shard_map/ppermute | solution.py:46
  83.2 9.3 %collective-permute-start.27 = (bf16[2,8,3072]{2,1,0:T(8,128)(2,1)S(1)}, bf16[2,8,3072]{2,1,0:T(8,128)(2,1)S(1)}, u32[]{:S(2)}, u32[]{:S(2)}) collective-permute-start(bf16[2,8,3072]{2,1,0:T(8,128)(2,1)S(1)} %get-tuple-element.59), channel_id=1, source_target_pairs={{0,0},{1,1},{2,2},{3,3},{16,18},{17,19},{18,16},{19,17},{32,32},{3... | collective-permute-start | bytes 294920 | tf_op jit(solution)/shard_map/ppermute | solution.py:46
  92.6 1.3 %collective-permute-start.29 = (bf16[2,4,3072]{2,1,0:T(4,128)(2,1)S(1)}, bf16[2,4,3072]{2,1,0:T(4,128)(2,1)S(1)}, u32[]{:S(2)}, u32[]{:S(2)}) collective-permute-start(bf16[2,4,3072]{2,1,0:T(4,128)(2,1)S(1)} %slice.379), channel_id=1, source_target_pairs={{16,0},{17,1},{18,2},{19,3},{0,16},{1,17},{2,18},{3,19},{48,32},{4... | collective-permute-start | bytes 147464 | tf_op jit(solution)/shard_map/ppermute | solution.py:46

commit v5 on v4

--- a/solution.py
+++ b/solution.py
@@ -105,7 +105,7 @@
     return jnp.concatenate(pieces, axis=0)
 
 
-CHUNK = 768
+CHUNK = 3072
 
 
 def cuts(size):

time: 94.9 us -> 94.9 us (level)
  no operation moved by 1% of the time
where the time goes in v5:
time: 94.9 us; the launch traced here: 94.7 us
  starting transfers between devices  44.5 us (47%)
  waiting for transfers between devices  35.6 us (38%)
  Pallas kernels  5.22 us (6%)
  matrix products  4.64 us (5%)
  other arithmetic  2.1 us (2%)
  local copies, waits for them, and re-layouts  1.49 us (2%)
  between operations  1.11 us (1%)
    ppermute x24, starting transfers between devices, send(): return lax.ppermute(value, PLANE, perm)  36.6 us
    ppermute x24, waiting for transfers between devices, send(): return lax.ppermute(value, PLANE, perm)  31.8 us
    ppermute x6, starting transfers between devices, exchange_rows(): return [lax.ppermute(rounded, 'row', shift) for shift in ROW_SHIFTS]  7.89 us
    pallas_call x4, Pallas kernels, call(): pl.pallas_call(body, out_shape=[jax.ShapeDtypeStruct(shape, dtype) for sh...  5.22 us
    dot_general x2, matrix products, t_dot(): lax.dot_general(a, b, (((0,), (0,)), ((), ())), preferred_element_type=F32)  4.64 us
    ppermute x6, waiting for transfers between devices, exchange_rows(): return [lax.ppermute(rounded, 'row', shift) for shift in ROW_SHIFTS]  3.81 us
  transfers between devices with their start and end apart: 30, of which 11 were waited for; matrix products, arithmetic and copies ran while one was open for 6% of the time, Pallas kernels for 6%

profile of v5, /device:TPU:1, one launch (start us, length us, event | category | flops | bytes accessed | tf_op | source)
XLA Modules:
  0.0 94.7 jit_solution(14510733472113871824)
XLA Ops:
  1.4 3.3 %collective-permute-start = (bf16[2,4,3072]{2,1,0:T(4,128)(2,1)S(1)}, bf16[2,4,3072]{2,1,0:T(4,128)(2,1)S(1)}, u32[]{:S(2)}, u32[]{:S(2)}) collective-permute-start(bf16[2,4,3072]{2,1,0:T(4,128)(2,1)S(1)} %pad_maximum_fusion.3), channel_id=1, source_target_pairs={{16,0},{17,1},{18,2},{19,3},{0,16},{1,17},{2,18},{3,19},{48,32},{4... | collective-permute-start | bytes 147464 | tf_op jit(solution)/shard_map/ppermute | solution.py:46
  6.4 7.1 %collective-permute-start.1 = (bf16[2,8,3072]{2,1,0:T(8,128)(2,1)S(1)}, bf16[2,8,3072]{2,1,0:T(8,128)(2,1)S(1)}, u32[]{:S(2)}, u32[]{:S(2)}) collective-permute-start(bf16[2,8,3072]{2,1,0:T(8,128)(2,1)S(1)} %pad_maximum_fusion.2), channel_id=1, source_target_pairs={{0,0},{1,1},{2,2},{3,3},{18,16},{19,17},{16,18},{17,19},{32,32},{3... | collective-permute-start | bytes 294920 | tf_op jit(solution)/shard_map/ppermute | solution.py:46
  13.5 1.7 %collective-permute-start.4 = (bf16[2,8,3072]{2,1,0:T(8,128)(2,1)S(1)}, bf16[2,8,3072]{2,1,0:T(8,128)(2,1)S(1)}, u32[]{:S(2)}, u32[]{:S(2)}) collective-permute-start(bf16[2,8,3072]{2,1,0:T(8,128)(2,1)S(1)} %pad_maximum_fusion.2), channel_id=1, source_target_pairs={{33,0},{34,1},{35,2},{32,3},{50,16},{51,17},{48,18},{49,19},{2,32}... | collective-permute-start | bytes 294920 | tf_op jit(solution)/shard_map/ppermute | solution.py:46
  15.8 8.6 %collective-permute-done.2 = bf16[2,8,3072]{2,1,0:T(8,128)(2,1)S(1)} collective-permute-done((bf16[2,8,3072]{2,1,0:T(8,128)(2,1)S(1)}, bf16[2,8,3072]{2,1,0:T(8,128)(2,1)S(1)}, u32[]{:S(2)}, u32[]{:S(2)}) %collective-permute-start.2) | collective-permute-done | bytes 98336 | tf_op jit(solution)/shard_map/ppermute | solution.py:46
  24.7 2.8 %collective-permute-start.7 = (bf16[32,3072]{1,0:T(8,128)(2,1)S(1)}, bf16[32,3072]{1,0:T(8,128)(2,1)S(1)}, u32[]{:S(2)}, u32[]{:S(2)}) collective-permute-start(bf16[32,3072]{1,0:T(8,128)(2,1)S(1)} %get-tuple-element.64.own), channel_id=1, source_target_pairs={{128,0},{129,1},{130,2},{131,3},{144,16},{145,17},{146,18},{147,19... | collective-permute-start | bytes 589832 | tf_op jit(solution)/shard_map/ppermute | solution.py:46
  29.1 8.1 %collective-permute-done.6.near = bf16[64,3072]{1,0:T(8,128)(2,1)S(1)} collective-permute-done((bf16[64,3072]{1,0:T(8,128)(2,1)S(1)}, bf16[64,3072]{1,0:T(8,128)(2,1)S(1)}, u32[]{:S(2)}, u32[]{:S(2)}) %collective-permute-start.6) | collective-permute-done | bytes 393248 | tf_op jit(solution)/shard_map/ppermute | solution.py:46
  37.3 1.0 %shard_map.75 = (f32[128,768]{1,0:T(8,128)S(1)}, bf16[128,768]{1,0:T(8,128)(2,1)S(1)}) custom-call(bf16[32,3072]{1,0:T(8,128)(2,1)S(1)} %get-tuple-element.64.own, bf16[64,3072]{1,0:T(8,128)(2,1)S(1)} %collective-permute-done.6.near, bf16[32,3072]{1,0:T(8,128)(2,1)S(1)} %collective-permute-done.7.far, bf16[3072,384]{1,0:T(8,128)(2,1)S(1)} %copy-done.1, ...), custom_call_target="tpu_custom_call" | custom-call | flops 4000000000 | tf_op jit(solution)/shard_map/pallas_call | solution.py:162
  38.3 1.4 %collective-permute-start.14 = (bf16[128,768]{1,0:T(8,128)(2,1)S(1)}, bf16[128,768]{1,0:T(8,128)(2,1)S(1)}, u32[]{:S(2)}, u32[]{:S(2)}) collective-permute-start(bf16[128,768]{1,0:T(8,128)(2,1)S(1)} %get-tuple-element.29), channel_id=1, source_target_pairs={{0,4},{4,8},{8,12},{12,0},{1,5},{5,9},{9,13},{13,1},{2,6},{6,10},{... | collective-permute-start | bytes 589832 | tf_op jit(solution)/shard_map/ppermute | solution.py:63
  39.6 1.5 %collective-permute-start.13 = (bf16[128,768]{1,0:T(8,128)(2,1)S(1)}, bf16[128,768]{1,0:T(8,128)(2,1)S(1)}, u32[]{:S(2)}, u32[]{:S(2)}) collective-permute-start(bf16[128,768]{1,0:T(8,128)(2,1)S(1)} %get-tuple-element.29), channel_id=1, source_target_pairs={{0,12},{4,0},{8,4},{12,8},{1,13},{5,1},{9,5},{13,9},{2,14},{6,2},{... | collective-permute-start | bytes 589832 | tf_op jit(solution)/shard_map/ppermute | solution.py:63
  41.2 1.6 %collective-permute-start.9 = (bf16[128,768]{1,0:T(8,128)(2,1)S(1)}, bf16[128,768]{1,0:T(8,128)(2,1)S(1)}, u32[]{:S(2)}, u32[]{:S(2)}) collective-permute-start(bf16[128,768]{1,0:T(8,128)(2,1)S(1)} %get-tuple-element.29), channel_id=1, source_target_pairs={{0,8},{4,12},{8,0},{12,4},{1,9},{5,13},{9,1},{13,5},{2,10},{6,14},... | collective-permute-start | bytes 589832 | tf_op jit(solution)/shard_map/ppermute | solution.py:63
  42.8 1.6 %collective-permute-start.11 = (bf16[32,3072]{1,0:T(8,128)(2,1)S(1)}, bf16[32,3072]{1,0:T(8,128)(2,1)S(1)}, u32[]{:S(2)}, u32[]{:S(2)}) collective-permute-start(bf16[32,3072]{1,0:T(8,128)(2,1)S(1)} %slice.206), channel_id=1, source_target_pairs={{64,0},{65,1},{66,2},{67,3},{208,16},{209,17},{210,18},{211,19},{9... | collective-permute-start | bytes 589832 | tf_op jit(solution)/shard_map/ppermute | solution.py:46
  44.4 4.2 %collective-permute-done.11.far = bf16[32,3072]{1,0:T(8,128)(2,1)S(1)} collective-permute-done((bf16[32,3072]{1,0:T(8,128)(2,1)S(1)}, bf16[32,3072]{1,0:T(8,128)(2,1)S(1)}, u32[]{:S(2)}, u32[]{:S(2)}) %collective-permute-start.11) | collective-permute-done | bytes 196640 | tf_op jit(solution)/shard_map/ppermute | solution.py:46
  48.6 1.5 %shard_map.76 = (f32[128,768]{1,0:T(8,128)S(1)}, bf16[128,768]{1,0:T(8,128)(2,1)S(1)}) custom-call(bf16[32,3072]{1,0:T(8,128)(2,1)S(1)} %get-tuple-element.65.own, bf16[64,3072]{1,0:T(8,128)(2,1)S(1)} %collective-permute-done.10.near, bf16[32,3072]{1,0:T(8,128)(2,1)S(1)} %collective-permute-done.11.far, bf16[384,3072]{1,0:T(8,128)(2,1)S(1)} %copy-done, ...), custom_call_target="tpu_custom_call" | custom-call | tf_op jit(solution)/shard_map/pallas_call | solution.py:162
  50.7 2.3 %collective-permute-start.17 = (bf16[128,768]{1,0:T(8,128)(2,1)S(1)}, bf16[128,768]{1,0:T(8,128)(2,1)S(1)}, u32[]{:S(2)}, u32[]{:S(2)}) collective-permute-start(bf16[128,768]{1,0:T(8,128)(2,1)S(1)} %get-tuple-element.38), channel_id=1, source_target_pairs={{0,12},{4,0},{8,4},{12,8},{1,13},{5,1},{9,5},{13,9},{2,14},{6,2},{... | collective-permute-start | bytes 589832 | tf_op jit(solution)/shard_map/ppermute | solution.py:63
  53.5 1.2 %shard_map.77 = (bf16[128,768]{1,0:T(8,128)(2,1)S(1)}, f32[128,768]{1,0:T(8,128)S(1)}, f32[32,3072]{1,0:T(8,128)S(1)}, bf16[64,3072]{1,0:T(8,128)(2,1)S(1)}, bf16[32,3072]{1,0:T(8,128)(2,1)S(1)}) custom-call(f32[128,768]{1,0:T(8,128)S(1)} %get-tuple-element.28.part, bf16[128,768]{1,0:T(8,128)(2,1)S(1)} %collective-permute-done.9.r0, ...), custom_call_target="tpu_custom_call" | custom-call | tf_op jit(solution)/shard_map/pallas_call | solution.py:162
  54.8 2.0 %collective-permute-start.19 = (bf16[32,3072]{1,0:T(8,128)(2,1)S(1)}, bf16[32,3072]{1,0:T(8,128)(2,1)S(1)}, u32[]{:S(2)}, u32[]{:S(2)}) collective-permute-start(bf16[32,3072]{1,0:T(8,128)(2,1)S(1)} %get-tuple-element.42), channel_id=1, source_target_pairs={{0,128},{1,129},{2,130},{3,131},{16,144},{17,145},{18,146},{19,147... | collective-permute-start | bytes 589832 | tf_op jit(solution)/shard_map/ppermute | solution.py:46
  57.8 3.8 %collective-permute-done.16.r0 = bf16[128,768]{1,0:T(8,128)(2,1)S(1)} collective-permute-done((bf16[128,768]{1,0:T(8,128)(2,1)S(1)}, bf16[128,768]{1,0:T(8,128)(2,1)S(1)}, u32[]{:S(2)}, u32[]{:S(2)}) %collective-permute-start.16) | collective-permute-done | bytes 196640 | tf_op jit(solution)/shard_map/ppermute | solution.py:63
  61.5 1.6 %shard_map.78 = (bf16[128,768]{1,0:T(8,128)(2,1)S(1)}, f32[32,3072]{1,0:T(8,128)S(1)}, bf16[64,3072]{1,0:T(8,128)(2,1)S(1)}, bf16[32,3072]{1,0:T(8,128)(2,1)S(1)}) custom-call(f32[128,768]{1,0:T(8,128)S(1)} %get-tuple-element.32.part, bf16[128,768]{1,0:T(8,128)(2,1)S(1)} %collective-permute-done.16.r0, bf16[128,768]{1,0:T(8,128)(2,1)S(1)} %collective-permute-done.17.r1, ...), custom_call_target="tpu_custom_call" | custom-call | tf_op jit(solution)/shard_map/pallas_call | solution.py:162
  63.4 1.8 %collective-permute-start.22 = (bf16[2,112,3072]{2,1,0:T(8,128)(2,1)S(1)}, bf16[2,112,3072]{2,1,0:T(8,128)(2,1)S(1)}, u32[]{:S(2)}, u32[]{:S(2)}) collective-permute-start(bf16[2,112,3072]{2,1,0:T(8,128)(2,1)S(1)} %pad_maximum_fusion), channel_id=1, source_target_pairs={{16,0},{17,1},{18,2},{19,3},{0,16},{1,17},{2,18},{3,19},{48,32},{4... | collective-permute-start | bytes 4128776 | tf_op jit(solution)/shard_map/ppermute | solution.py:46
  65.3 2.0 %collective-permute-start.23 = (bf16[32,3072]{1,0:T(8,128)(2,1)S(1)}, bf16[32,3072]{1,0:T(8,128)(2,1)S(1)}, u32[]{:S(2)}, u32[]{:S(2)}) collective-permute-start(bf16[32,3072]{1,0:T(8,128)(2,1)S(1)} %get-tuple-element.48), channel_id=1, source_target_pairs={{0,128},{1,129},{2,130},{3,131},{16,144},{17,145},{18,146},{19,147... | collective-permute-start | bytes 589832 | tf_op jit(solution)/shard_map/ppermute | solution.py:46
  67.2 1.3 %collective-permute-start.21 = (bf16[64,3072]{1,0:T(8,128)(2,1)S(1)}, bf16[64,3072]{1,0:T(8,128)(2,1)S(1)}, u32[]{:S(2)}, u32[]{:S(2)}) collective-permute-start(bf16[64,3072]{1,0:T(8,128)(2,1)S(1)} %get-tuple-element.44), channel_id=1, source_target_pairs={{0,64},{1,65},{2,66},{3,67},{16,208},{17,209},{18,210},{19,211},{3... | collective-permute-start | bytes 1179656 | tf_op jit(solution)/shard_map/ppermute | solution.py:46
  68.6 1.3 %collective-permute-start.20 = (bf16[32,3072]{1,0:T(8,128)(2,1)S(1)}, bf16[32,3072]{1,0:T(8,128)(2,1)S(1)}, u32[]{:S(2)}, u32[]{:S(2)}) collective-permute-start(bf16[32,3072]{1,0:T(8,128)(2,1)S(1)} %slice.208), channel_id=1, source_target_pairs={{16,0},{17,1},{18,2},{19,3},{0,16},{1,17},{2,18},{3,19},{48,32},{4... | collective-permute-start | bytes 589832 | tf_op jit(solution)/shard_map/ppermute | solution.py:46
  69.9 1.1 %collective-permute-done.20 = bf16[32,3072]{1,0:T(8,128)(2,1)S(1)} collective-permute-done((bf16[32,3072]{1,0:T(8,128)(2,1)S(1)}, bf16[32,3072]{1,0:T(8,128)(2,1)S(1)}, u32[]{:S(2)}, u32[]{:S(2)}) %collective-permute-start.20) | collective-permute-done | bytes 196640 | tf_op jit(solution)/shard_map/ppermute | solution.py:46
  71.5 2.2 %convolution_convert_fusion = bf16[384,3072]{1,0:T(8,128)(2,1)} fusion(bf16[256,384]{1,0:T(8,128)(2,1)S(1)} %get-tuple-element.77, bf16[256,3072]{1,0:T(8,128)(2,1)S(1)} %get-tuple-element.50), kind=kOutput, calls=%fused_computation | convolution fusion | flops 605159424 | bytes 4128768 | tf_op jit(solution)/shard_map/dot_general | solution.py:92
  73.7 2.4 %convolution_convert_fusion.1 = bf16[3072,384]{1,0:T(8,128)(2,1)} fusion(bf16[256,3072]{1,0:T(8,128)(2,1)S(1)} %get-tuple-element.51, bf16[256,384]{1,0:T(8,128)(2,1)S(1)} %get-tuple-element.76), kind=kOutput, calls=%fused_computation.1 | convolution fusion | flops 605159424 | bytes 4128768 | tf_op jit(solution)/shard_map/dot_general | solution.py:92
  76.1 1.9 %collective-permute-done.21 = bf16[64,3072]{1,0:T(8,128)(2,1)S(1)} collective-permute-done((bf16[64,3072]{1,0:T(8,128)(2,1)S(1)}, bf16[64,3072]{1,0:T(8,128)(2,1)S(1)}, u32[]{:S(2)}, u32[]{:S(2)}) %collective-permute-start.21) | collective-permute-done | bytes 393248 | tf_op jit(solution)/shard_map/ppermute | solution.py:46
  78.5 1.1 %collective-permute-done.24 = bf16[32,3072]{1,0:T(8,128)(2,1)S(1)} collective-permute-done((bf16[32,3072]{1,0:T(8,128)(2,1)S(1)}, bf16[32,3072]{1,0:T(8,128)(2,1)S(1)}, u32[]{:S(2)}, u32[]{:S(2)}) %collective-permute-start.24) | collective-permute-done | bytes 196640 | tf_op jit(solution)/shard_map/ppermute | solution.py:46
  79.7 1.0 %collective-permute-start.25 = (bf16[2,8,3072]{2,1,0:T(8,128)(2,1)S(1)}, bf16[2,8,3072]{2,1,0:T(8,128)(2,1)S(1)}, u32[]{:S(2)}, u32[]{:S(2)}) collective-permute-start(bf16[2,8,3072]{2,1,0:T(8,128)(2,1)S(1)} %get-tuple-element.56), channel_id=1, source_target_pairs={{0,32},{1,33},{2,34},{3,35},{16,51},{17,48},{18,49},{19,50},{32,1}... | collective-permute-start | bytes 294920 | tf_op jit(solution)/shard_map/ppermute | solution.py:46
  81.6 1.7 %collective-permute-start.28 = (bf16[2,8,3072]{2,1,0:T(8,128)(2,1)S(1)}, bf16[2,8,3072]{2,1,0:T(8,128)(2,1)S(1)}, u32[]{:S(2)}, u32[]{:S(2)}) collective-permute-start(bf16[2,8,3072]{2,1,0:T(8,128)(2,1)S(1)} %get-tuple-element.58), channel_id=1, source_target_pairs={{0,33},{1,34},{2,35},{3,32},{16,50},{17,51},{18,48},{19,49},{32,2}... | collective-permute-start | bytes 294920 | tf_op jit(solution)/shard_map/ppermute | solution.py:46
  83.3 4.8 %collective-permute-start.27 = (bf16[2,8,3072]{2,1,0:T(8,128)(2,1)S(1)}, bf16[2,8,3072]{2,1,0:T(8,128)(2,1)S(1)}, u32[]{:S(2)}, u32[]{:S(2)}) collective-permute-start(bf16[2,8,3072]{2,1,0:T(8,128)(2,1)S(1)} %get-tuple-element.59), channel_id=1, source_target_pairs={{0,0},{1,1},{2,2},{3,3},{16,18},{17,19},{18,16},{19,17},{32,32},{3... | collective-permute-start | bytes 294920 | tf_op jit(solution)/shard_map/ppermute | solution.py:46
  88.1 4.5 %collective-permute-done.27 = bf16[2,8,3072]{2,1,0:T(8,128)(2,1)S(1)} collective-permute-done((bf16[2,8,3072]{2,1,0:T(8,128)(2,1)S(1)}, bf16[2,8,3072]{2,1,0:T(8,128)(2,1)S(1)}, u32[]{:S(2)}, u32[]{:S(2)}) %collective-permute-start.27) | collective-permute-done | bytes 98336 | tf_op jit(solution)/shard_map/ppermute | solution.py:46
  92.8 1.2 %collective-permute-done.29 = bf16[2,4,3072]{2,1,0:T(4,128)(2,1)S(1)} collective-permute-done((bf16[2,4,3072]{2,1,0:T(4,128)(2,1)S(1)}, bf16[2,4,3072]{2,1,0:T(4,128)(2,1)S(1)}, u32[]{:S(2)}, u32[]{:S(2)}) %collective-permute-start.29) | collective-permute-done | bytes 49184 | tf_op jit(solution)/shard_map/ppermute | solution.py:46
  (101 shorter events, 10.1 us)
Async XLA Ops:
  1.4 4.2 %collective-permute-start = (bf16[2,4,3072]{2,1,0:T(4,128)(2,1)S(1)}, bf16[2,4,3072]{2,1,0:T(4,128)(2,1)S(1)}, u32[]{:S(2)}, u32[]{:S(2)}) collective-permute-start(bf16[2,4,3072]{2,1,0:T(4,128)(2,1)S(1)} %pad_maximum_fusion.3), channel_id=1, source_target_pairs={{16,0},{17,1},{18,2},{19,3},{0,16},{1,17},{2,18},{3,19},{48,32},{4... | collective-permute-start | bytes 147464 | tf_op jit(solution)/shard_map/ppermute | solution.py:46
  6.4 9.4 %collective-permute-start.1 = (bf16[2,8,3072]{2,1,0:T(8,128)(2,1)S(1)}, bf16[2,8,3072]{2,1,0:T(8,128)(2,1)S(1)}, u32[]{:S(2)}, u32[]{:S(2)}) collective-permute-start(bf16[2,8,3072]{2,1,0:T(8,128)(2,1)S(1)} %pad_maximum_fusion.2), channel_id=1, source_target_pairs={{0,0},{1,1},{2,2},{3,3},{18,16},{19,17},{16,18},{17,19},{32,32},{3... | collective-permute-start | bytes 294920 | tf_op jit(solution)/shard_map/ppermute | solution.py:46
  13.5 11.0 %collective-permute-start.4 = (bf16[2,8,3072]{2,1,0:T(8,128)(2,1)S(1)}, bf16[2,8,3072]{2,1,0:T(8,128)(2,1)S(1)}, u32[]{:S(2)}, u32[]{:S(2)}) collective-permute-start(bf16[2,8,3072]{2,1,0:T(8,128)(2,1)S(1)} %pad_maximum_fusion.2), channel_id=1, source_target_pairs={{33,0},{34,1},{35,2},{32,3},{50,16},{51,17},{48,18},{49,19},{2,32}... | collective-permute-start | bytes 294920 | tf_op jit(solution)/shard_map/ppermute | solution.py:46
  15.3 9.2 %collective-permute-start.3 = (bf16[2,8,3072]{2,1,0:T(8,128)(2,1)S(1)}, bf16[2,8,3072]{2,1,0:T(8,128)(2,1)S(1)}, u32[]{:S(2)}, u32[]{:S(2)}) collective-permute-start(bf16[2,8,3072]{2,1,0:T(8,128)(2,1)S(1)} %pad_maximum_fusion.2), channel_id=1, source_target_pairs={{1,0},{2,1},{3,2},{0,3},{19,16},{16,17},{17,18},{18,19},{33,32},{3... | collective-permute-start | bytes 294920 | tf_op jit(solution)/shard_map/ppermute | solution.py:46
  15.3 9.2 %collective-permute-start.2 = (bf16[2,8,3072]{2,1,0:T(8,128)(2,1)S(1)}, bf16[2,8,3072]{2,1,0:T(8,128)(2,1)S(1)}, u32[]{:S(2)}, u32[]{:S(2)}) collective-permute-start(bf16[2,8,3072]{2,1,0:T(8,128)(2,1)S(1)} %pad_maximum_fusion.2), channel_id=1, source_target_pairs={{32,0},{33,1},{34,2},{35,3},{51,16},{48,17},{49,18},{50,19},{1,32}... | collective-permute-start | bytes 294920 | tf_op jit(solution)/shard_map/ppermute | solution.py:46
  24.6 3.7 %collective-permute-start.5 = (bf16[2,32,3072]{2,1,0:T(8,128)(2,1)S(1)}, bf16[2,32,3072]{2,1,0:T(8,128)(2,1)S(1)}, u32[]{:S(2)}, u32[]{:S(2)}) collective-permute-start(bf16[2,32,3072]{2,1,0:T(8,128)(2,1)S(1)} %get-tuple-element.67), channel_id=1, source_target_pairs={{16,0},{17,1},{18,2},{19,3},{0,16},{1,17},{2,18},{3,19},{48,32},{4... | collective-permute-start | bytes 1179656 | tf_op jit(solution)/shard_map/ppermute | solution.py:46
  24.7 12.5 %collective-permute-start.7 = (bf16[32,3072]{1,0:T(8,128)(2,1)S(1)}, bf16[32,3072]{1,0:T(8,128)(2,1)S(1)}, u32[]{:S(2)}, u32[]{:S(2)}) collective-permute-start(bf16[32,3072]{1,0:T(8,128)(2,1)S(1)} %get-tuple-element.64.own), channel_id=1, source_target_pairs={{128,0},{129,1},{130,2},{131,3},{144,16},{145,17},{146,18},{147,19... | collective-permute-start | bytes 589832 | tf_op jit(solution)/shard_map/ppermute | solution.py:46
  27.5 9.7 %collective-permute-start.8 = (bf16[3072,384]{1,0:T(8,128)(2,1)}, bf16[3072,384]{1,0:T(8,128)(2,1)S(1)}, u32[]{:S(2)}, u32[]{:S(2)}) collective-permute-start(bf16[3072,384]{1,0:T(8,128)(2,1)} %w_a.7), channel_id=1, source_target_pairs={{16,0},{17,1},{18,2},{19,3},{0,16},{1,17},{2,18},{3,19},{48,32},{4... | collective-permute-start | bytes 7077896 | tf_op jit(solution)/shard_map/ppermute | solution.py:46
  28.3 16.1 %collective-permute-start.12 = (bf16[384,3072]{1,0:T(8,128)(2,1)}, bf16[384,3072]{1,0:T(8,128)(2,1)S(1)}, u32[]{:S(2)}, u32[]{:S(2)}) collective-permute-start(bf16[384,3072]{1,0:T(8,128)(2,1)} %w_a.6), channel_id=1, source_target_pairs={{16,0},{17,1},{18,2},{19,3},{0,16},{1,17},{2,18},{3,19},{48,32},{4... | collective-permute-start | bytes 7077896 | tf_op jit(solution)/shard_map/ppermute | solution.py:46
  28.3 8.9 %copy-start.1 = (bf16[3072,384]{1,0:T(8,128)(2,1)S(1)}, bf16[3072,384]{1,0:T(8,128)(2,1)}, u32[]{:S(2)}) copy-start(bf16[3072,384]{1,0:T(8,128)(2,1)} %w_a.7) | copy-start | bytes 7077892
  28.4 8.8 %collective-permute-start.6 = (bf16[64,3072]{1,0:T(8,128)(2,1)S(1)}, bf16[64,3072]{1,0:T(8,128)(2,1)S(1)}, u32[]{:S(2)}, u32[]{:S(2)}) collective-permute-start(bf16[64,3072]{1,0:T(8,128)(2,1)S(1)} %get-tuple-element.54), channel_id=1, source_target_pairs={{64,0},{65,1},{66,2},{67,3},{208,16},{209,17},{210,18},{211,19},{9... | collective-permute-start | bytes 1179656 | tf_op jit(solution)/shard_map/ppermute | solution.py:46
  28.8 13.9 %collective-permute-start.10 = (bf16[64,3072]{1,0:T(8,128)(2,1)S(1)}, bf16[64,3072]{1,0:T(8,128)(2,1)S(1)}, u32[]{:S(2)}, u32[]{:S(2)}) collective-permute-start(bf16[64,3072]{1,0:T(8,128)(2,1)S(1)} %get-tuple-element.55), channel_id=1, source_target_pairs={{64,0},{65,1},{66,2},{67,3},{208,16},{209,17},{210,18},{211,19},{9... | collective-permute-start | bytes 1179656 | tf_op jit(solution)/shard_map/ppermute | solution.py:46
  37.3 11.3 %copy-start = (bf16[384,3072]{1,0:T(8,128)(2,1)S(1)}, bf16[384,3072]{1,0:T(8,128)(2,1)}, u32[]{:S(2)}) copy-start(bf16[384,3072]{1,0:T(8,128)(2,1)} %w_a.6) | copy-start | bytes 7077892
  38.3 14.7 %collective-permute-start.14 = (bf16[128,768]{1,0:T(8,128)(2,1)S(1)}, bf16[128,768]{1,0:T(8,128)(2,1)S(1)}, u32[]{:S(2)}, u32[]{:S(2)}) collective-permute-start(bf16[128,768]{1,0:T(8,128)(2,1)S(1)} %get-tuple-element.29), channel_id=1, source_target_pairs={{0,4},{4,8},{8,12},{12,0},{1,5},{5,9},{9,13},{13,1},{2,6},{6,10},{... | collective-permute-start | bytes 589832 | tf_op jit(solution)/shard_map/ppermute | solution.py:63
  39.6 13.9 %collective-permute-start.13 = (bf16[128,768]{1,0:T(8,128)(2,1)S(1)}, bf16[128,768]{1,0:T(8,128)(2,1)S(1)}, u32[]{:S(2)}, u32[]{:S(2)}) collective-permute-start(bf16[128,768]{1,0:T(8,128)(2,1)S(1)} %get-tuple-element.29), channel_id=1, source_target_pairs={{0,12},{4,0},{8,4},{12,8},{1,13},{5,1},{9,5},{13,9},{2,14},{6,2},{... | collective-permute-start | bytes 589832 | tf_op jit(solution)/shard_map/ppermute | solution.py:63
  41.2 12.3 %collective-permute-start.9 = (bf16[128,768]{1,0:T(8,128)(2,1)S(1)}, bf16[128,768]{1,0:T(8,128)(2,1)S(1)}, u32[]{:S(2)}, u32[]{:S(2)}) collective-permute-start(bf16[128,768]{1,0:T(8,128)(2,1)S(1)} %get-tuple-element.29), channel_id=1, source_target_pairs={{0,8},{4,12},{8,0},{12,4},{1,9},{5,13},{9,1},{13,5},{2,10},{6,14},... | collective-permute-start | bytes 589832 | tf_op jit(solution)/shard_map/ppermute | solution.py:63
  42.8 5.8 %collective-permute-start.11 = (bf16[32,3072]{1,0:T(8,128)(2,1)S(1)}, bf16[32,3072]{1,0:T(8,128)(2,1)S(1)}, u32[]{:S(2)}, u32[]{:S(2)}) collective-permute-start(bf16[32,3072]{1,0:T(8,128)(2,1)S(1)} %slice.206), channel_id=1, source_target_pairs={{64,0},{65,1},{66,2},{67,3},{208,16},{209,17},{210,18},{211,19},{9... | collective-permute-start | bytes 589832 | tf_op jit(solution)/shard_map/ppermute | solution.py:46
  50.1 7.7 %collective-permute-start.18 = (bf16[128,768]{1,0:T(8,128)(2,1)S(1)}, bf16[128,768]{1,0:T(8,128)(2,1)S(1)}, u32[]{:S(2)}, u32[]{:S(2)}) collective-permute-start(bf16[128,768]{1,0:T(8,128)(2,1)S(1)} %get-tuple-element.38), channel_id=1, source_target_pairs={{0,4},{4,8},{8,12},{12,0},{1,5},{5,9},{9,13},{13,1},{2,6},{6,10},{... | collective-permute-start | bytes 589832 | tf_op jit(solution)/shard_map/ppermute | solution.py:63
  50.7 7.0 %collective-permute-start.17 = (bf16[128,768]{1,0:T(8,128)(2,1)S(1)}, bf16[128,768]{1,0:T(8,128)(2,1)S(1)}, u32[]{:S(2)}, u32[]{:S(2)}) collective-permute-start(bf16[128,768]{1,0:T(8,128)(2,1)S(1)} %get-tuple-element.38), channel_id=1, source_target_pairs={{0,12},{4,0},{8,4},{12,8},{1,13},{5,1},{9,5},{13,9},{2,14},{6,2},{... | collective-permute-start | bytes 589832 | tf_op jit(solution)/shard_map/ppermute | solution.py:63
  53.0 8.5 %collective-permute-start.16 = (bf16[128,768]{1,0:T(8,128)(2,1)S(1)}, bf16[128,768]{1,0:T(8,128)(2,1)S(1)}, u32[]{:S(2)}, u32[]{:S(2)}) collective-permute-start(bf16[128,768]{1,0:T(8,128)(2,1)S(1)} %get-tuple-element.38), channel_id=1, source_target_pairs={{0,8},{4,12},{8,0},{12,4},{1,9},{5,13},{9,1},{13,5},{2,10},{6,14},... | collective-permute-start | bytes 589832 | tf_op jit(solution)/shard_map/ppermute | solution.py:63
  54.8 10.5 %collective-permute-start.19 = (bf16[32,3072]{1,0:T(8,128)(2,1)S(1)}, bf16[32,3072]{1,0:T(8,128)(2,1)S(1)}, u32[]{:S(2)}, u32[]{:S(2)}) collective-permute-start(bf16[32,3072]{1,0:T(8,128)(2,1)S(1)} %get-tuple-element.42), channel_id=1, source_target_pairs={{0,128},{1,129},{2,130},{3,131},{16,144},{17,145},{18,146},{19,147... | collective-permute-start | bytes 589832 | tf_op jit(solution)/shard_map/ppermute | solution.py:46
  56.8 11.7 %collective-permute-start.15 = (bf16[64,3072]{1,0:T(8,128)(2,1)S(1)}, bf16[64,3072]{1,0:T(8,128)(2,1)S(1)}, u32[]{:S(2)}, u32[]{:S(2)}) collective-permute-start(bf16[64,3072]{1,0:T(8,128)(2,1)S(1)} %get-tuple-element.37), channel_id=1, source_target_pairs={{0,64},{1,65},{2,66},{3,67},{16,208},{17,209},{18,210},{19,211},{3... | collective-permute-start | bytes 1179656 | tf_op jit(solution)/shard_map/ppermute | solution.py:46
  63.4 7.7 %collective-permute-start.22 = (bf16[2,112,3072]{2,1,0:T(8,128)(2,1)S(1)}, bf16[2,112,3072]{2,1,0:T(8,128)(2,1)S(1)}, u32[]{:S(2)}, u32[]{:S(2)}) collective-permute-start(bf16[2,112,3072]{2,1,0:T(8,128)(2,1)S(1)} %pad_maximum_fusion), channel_id=1, source_target_pairs={{16,0},{17,1},{18,2},{19,3},{0,16},{1,17},{2,18},{3,19},{48,32},{4... | collective-permute-start | bytes 4128776 | tf_op jit(solution)/shard_map/ppermute | solution.py:46
  65.3 13.2 %collective-permute-start.23 = (bf16[32,3072]{1,0:T(8,128)(2,1)S(1)}, bf16[32,3072]{1,0:T(8,128)(2,1)S(1)}, u32[]{:S(2)}, u32[]{:S(2)}) collective-permute-start(bf16[32,3072]{1,0:T(8,128)(2,1)S(1)} %get-tuple-element.48), channel_id=1, source_target_pairs={{0,128},{1,129},{2,130},{3,131},{16,144},{17,145},{18,146},{19,147... | collective-permute-start | bytes 589832 | tf_op jit(solution)/shard_map/ppermute | solution.py:46
  67.2 10.8 %collective-permute-start.21 = (bf16[64,3072]{1,0:T(8,128)(2,1)S(1)}, bf16[64,3072]{1,0:T(8,128)(2,1)S(1)}, u32[]{:S(2)}, u32[]{:S(2)}) collective-permute-start(bf16[64,3072]{1,0:T(8,128)(2,1)S(1)} %get-tuple-element.44), channel_id=1, source_target_pairs={{0,64},{1,65},{2,66},{3,67},{16,208},{17,209},{18,210},{19,211},{3... | collective-permute-start | bytes 1179656 | tf_op jit(solution)/shard_map/ppermute | solution.py:46
  68.6 2.4 %collective-permute-start.20 = (bf16[32,3072]{1,0:T(8,128)(2,1)S(1)}, bf16[32,3072]{1,0:T(8,128)(2,1)S(1)}, u32[]{:S(2)}, u32[]{:S(2)}) collective-permute-start(bf16[32,3072]{1,0:T(8,128)(2,1)S(1)} %slice.208), channel_id=1, source_target_pairs={{16,0},{17,1},{18,2},{19,3},{0,16},{1,17},{2,18},{3,19},{48,32},{4... | collective-permute-start | bytes 589832 | tf_op jit(solution)/shard_map/ppermute | solution.py:46
  78.0 1.6 %collective-permute-start.24 = (bf16[32,3072]{1,0:T(8,128)(2,1)S(1)}, bf16[32,3072]{1,0:T(8,128)(2,1)S(1)}, u32[]{:S(2)}, u32[]{:S(2)}) collective-permute-start(bf16[32,3072]{1,0:T(8,128)(2,1)S(1)} %slice.252), channel_id=1, source_target_pairs={{16,0},{17,1},{18,2},{19,3},{0,16},{1,17},{2,18},{3,19},{48,32},{4... | collective-permute-start | bytes 589832 | tf_op jit(solution)/shard_map/ppermute | solution.py:46
  79.7 8.4 %collective-permute-start.25 = (bf16[2,8,3072]{2,1,0:T(8,128)(2,1)S(1)}, bf16[2,8,3072]{2,1,0:T(8,128)(2,1)S(1)}, u32[]{:S(2)}, u32[]{:S(2)}) collective-permute-start(bf16[2,8,3072]{2,1,0:T(8,128)(2,1)S(1)} %get-tuple-element.56), channel_id=1, source_target_pairs={{0,32},{1,33},{2,34},{3,35},{16,51},{17,48},{18,49},{19,50},{32,1}... | collective-permute-start | bytes 294920 | tf_op jit(solution)/shard_map/ppermute | solution.py:46
  80.7 7.4 %collective-permute-start.26 = (bf16[2,8,3072]{2,1,0:T(8,128)(2,1)S(1)}, bf16[2,8,3072]{2,1,0:T(8,128)(2,1)S(1)}, u32[]{:S(2)}, u32[]{:S(2)}) collective-permute-start(bf16[2,8,3072]{2,1,0:T(8,128)(2,1)S(1)} %get-tuple-element.57), channel_id=1, source_target_pairs={{0,1},{1,2},{2,3},{3,0},{16,19},{17,16},{18,17},{19,18},{32,33},{3... | collective-permute-start | bytes 294920 | tf_op jit(solution)/shard_map/ppermute | solution.py:46
  81.6 6.5 %collective-permute-start.28 = (bf16[2,8,3072]{2,1,0:T(8,128)(2,1)S(1)}, bf16[2,8,3072]{2,1,0:T(8,128)(2,1)S(1)}, u32[]{:S(2)}, u32[]{:S(2)}) collective-permute-start(bf16[2,8,3072]{2,1,0:T(8,128)(2,1)S(1)} %get-tuple-element.58), channel_id=1, source_target_pairs={{0,33},{1,34},{2,35},{3,32},{16,50},{17,51},{18,48},{19,49},{32,2}... | collective-permute-start | bytes 294920 | tf_op jit(solution)/shard_map/ppermute | solution.py:46
  83.3 9.3 %collective-permute-start.27 = (bf16[2,8,3072]{2,1,0:T(8,128)(2,1)S(1)}, bf16[2,8,3072]{2,1,0:T(8,128)(2,1)S(1)}, u32[]{:S(2)}, u32[]{:S(2)}) collective-permute-start(bf16[2,8,3072]{2,1,0:T(8,128)(2,1)S(1)} %get-tuple-element.59), channel_id=1, source_target_pairs={{0,0},{1,1},{2,2},{3,3},{16,18},{17,19},{18,16},{19,17},{32,32},{3... | collective-permute-start | bytes 294920 | tf_op jit(solution)/shard_map/ppermute | solution.py:46
  92.7 1.3 %collective-permute-start.29 = (bf16[2,4,3072]{2,1,0:T(4,128)(2,1)S(1)}, bf16[2,4,3072]{2,1,0:T(4,128)(2,1)S(1)}, u32[]{:S(2)}, u32[]{:S(2)}) collective-permute-start(bf16[2,4,3072]{2,1,0:T(4,128)(2,1)S(1)} %slice.379), channel_id=1, source_target_pairs={{16,0},{17,1},{18,2},{19,3},{0,16},{1,17},{2,18},{3,19},{48,32},{4... | collective-permute-start | bytes 147464 | tf_op jit(solution)/shard_map/ppermute | solution.py:46
